TPU v7x, 32 devices: a whole 2x2x4 slice. The times are simulated.
32 devices in a mesh: pair: 8 (over z, y), row: 4 (over x, core).
Axes of the slice: x: 2, y: 2, z: 4, core: 2. Of those that a mesh axis runs over, the one named last changes fastest.
Arguments:
- whitened: float32 [4096, 2048], P('row', 'pair'), may hold values from -50 to 50, as said below
- offsets: int32 [4, 4], replicated, may hold values from 0 to 127
Outputs:
- rotated: float32 [4096, 2048], P('row', 'pair')
- right_vectors: float32 [2048, 2048], P('row', 'pair')
Inputs may be any that keep to these rules, and one draw needn't show every extreme that they name: whitened has rows and columns of different scales.
All inputs are finite; a program needn't handle non-finite values.
Results may differ from a plain program's by a relative error of at most 0.0003.
Values sent between devices are 32-bit elements; how exact they have to be, the bound alone decides.
No kernel may reach another device: no remote copies, remote signals or barrier semaphores. Data moves between devices by JAX's collectives and lax.ppermute only.
A program may use at most 64 MiB of HBM per device.

v0:
```python
import functools

import jax
import jax.numpy as jnp
from jax import lax
from jax.experimental import pallas as pl
from jax.experimental.pallas import tpu as pltpu
from jax.sharding import PartitionSpec as P

B = 128
ROUNDS = 4
STEPS = 4
RECORD = 2 * ROUNDS
CHUNK = 64
AXES = ("pair", "row")
PARAMS = pltpu.CompilerParams(vmem_limit_bytes=40 * 1024 * 1024)
VMEM = pl.BlockSpec(memory_space=pltpu.VMEM)
SMEM = pl.BlockSpec(memory_space=pltpu.SMEM)


def given(slot, part):
    return slot, part


def crossed(slot, part):
    return (slot & ~1) | (part & 1), (part & ~1) | (slot & 1)


def route(source, target, change):
    pairs, rows = lax.axis_size("pair"), lax.axis_size("row")
    line = []
    for slot in range(pairs):
        for part in range(rows):
            a = source(slot, part)
            b = target(*change(slot, part, pairs))
            line.append((a[0] * rows + a[1], b[0] * rows + b[1]))
    return line


def inner(slot, part, pairs):
    return slot ^ 1, part


def outer(slot, part, pairs):
    if slot == 0 or slot == pairs - 1:
        return slot, part
    return (slot + 1 if slot & 1 else slot - 1), part


def send(x, source, target, change):
    return lax.ppermute(x, AXES, route(source, target, change))


def other_part(distance):
    return lambda slot, part, pairs: (slot, part ^ distance)


def back(shift_by):
    return (B - shift_by) & (B - 1)


def eye_mask():
    shape = (B, B)
    return lax.broadcasted_iota(jnp.int32, shape, 0) == lax.broadcasted_iota(jnp.int32, shape, 1)


def diagonal(mask, block):
    return jnp.sum(jnp.where(mask, block, 0.0), axis=0, keepdims=True)


def as_column(mask, row):
    return jnp.sum(jnp.where(mask, jnp.broadcast_to(row, (B, B)), 0.0), axis=1, keepdims=True)


def solve(first, across, second, offs):
    mask = eye_mask()
    angles = []
    held = 0
    for r in range(ROUNDS):
        turn = (held - offs[r]) & (B - 1)
        held = offs[r]
        across = pltpu.roll(across, turn, 1)
        second = pltpu.roll(pltpu.roll(second, turn, 1), turn, 0)
        a = diagonal(mask, first)
        d = diagonal(mask, second)
        c0 = diagonal(mask, across)
        h = 0.5 * (d - a)
        radius = jnp.sqrt(h * h + c0 * c0)
        sg = jnp.where(h >= 0, 1.0, -1.0)
        t = -sg * c0 / (jnp.abs(h) + radius + 1e-06 * (a + d))
        c = 1.0 / jnp.sqrt(1.0 + t * t)
        s = t * c
        angles.append((c, s))
        cc, sc = as_column(mask, c), as_column(mask, s)
        below = across.T
        first1 = first * c + across * s
        across1 = across * c - first * s
        below1 = below * c + second * s
        second1 = second * c - below * s
        first = cc * first1 + sc * below1
        across = cc * across1 + sc * second1
        second = cc * second1 - sc * across1
    second = pltpu.roll(pltpu.roll(second, held, 1), held, 0)
    return angles, first, second


def rotate(first, second, angles, offs):
    held = 0
    for r in range(ROUNDS):
        c, s = angles[r]
        second = pltpu.roll(second, (held - offs[r]) & (B - 1), 1)
        held = offs[r]
        first, second = c * first + s * second, c * second - s * first
    return first, pltpu.roll(second, held, 1)


def rotate_back(first, second, angles, offs):
    held = 0
    for r in reversed(range(ROUNDS)):
        c, s = angles[r]
        second = pltpu.roll(second, (held - offs[r]) & (B - 1), 1)
        held = offs[r]
        first, second = c * first - s * second, s * first + c * second
    return first, pltpu.roll(second, held, 1)


def read_record(rows):
    return [(rows[r : r + 1], rows[ROUNDS + r : ROUNDS + r + 1]) for r in range(ROUNDS)]


def write_record(ref, at, angles):
    for r, (c, s) in enumerate(angles):
        ref[at + r : at + r + 1, :] = c
        ref[at + ROUNDS + r : at + ROUNDS + r + 1, :] = s


def tree_sum(parts):
    parts = list(parts)
    while len(parts) > 1:
        parts = [parts[i] + parts[i + 1] for i in range(0, len(parts), 2)]
    return parts[0]


def rotate_rows(rows, angles, offs, take, put):
    @pl.loop(0, rows // CHUNK)
    def _(i):
        at = pl.ds(pl.multiple_of(i * CHUNK, CHUNK), CHUNK)
        put(at, *rotate(*take(at), angles, offs))


def step_offsets(offs_ref, step):
    return [offs_ref[step, r] for r in range(ROUNDS)]


def transposed_dot(left, right):
    return lax.dot_general(
        left,
        right,
        (((0,), (0,)), ((), ())),
        precision=lax.Precision.HIGHEST,
        preferred_element_type=jnp.float32,
    )


def whole_gram_kernel(x_ref, out_ref):
    gram = transposed_dot(x_ref[...], x_ref[...])
    out_ref[0:B, :] = gram[:B, :B]
    out_ref[B : 2 * B, :] = gram[:B, B:]
    out_ref[2 * B : 3 * B, :] = gram[B:, B:]


def whole_gram(x):
    return pl.pallas_call(
        whole_gram_kernel,
        out_shape=jax.ShapeDtypeStruct((3 * B, B), jnp.float32),
        in_specs=[VMEM],
        out_specs=VMEM,
        compiler_params=PARAMS,
    )(x)


def cross_gram_kernel(rows, u_ref, w_ref, out_ref):
    out_ref[...] = transposed_dot(u_ref[:rows, :], w_ref[:rows, :])


def cross_gram(rows, u, w):
    return pl.pallas_call(
        functools.partial(cross_gram_kernel, rows),
        out_shape=jax.ShapeDtypeStruct((B, B), jnp.float32),
        in_specs=[VMEM, VMEM],
        out_specs=VMEM,
        compiler_params=PARAMS,
    )(u, w)


def first_kernel(count, offs_ref, place_ref, *refs):
    parts, (x_ref, in_ref, out_ref) = refs[:count], refs[count:]
    rows = x_ref.shape[0]
    offs = step_offsets(offs_ref, 0)
    gram = tree_sum([p[...] for p in parts])
    angles, first, second = solve(gram[:B], gram[B : 2 * B], gram[2 * B :], offs)
    slot = place_ref[0]
    swap = jnp.logical_and((slot & 1) == 0, slot != 0)

    def finish(first_ref, second_ref):
        first_ref[rows : rows + B, :] = first
        second_ref[rows : rows + B, :] = second
        write_record(first_ref, rows + B, angles)
        write_record(second_ref, rows + B, angles)

        def put(at, t, b):
            first_ref[at, :] = t
            second_ref[at, :] = b

        rotate_rows(rows, angles, offs, lambda at: (x_ref[at, :B], x_ref[at, B:]), put)

    @pl.when(swap)
    def _():
        finish(in_ref, out_ref)

    @pl.when(jnp.logical_not(swap))
    def _():
        finish(out_ref, in_ref)


def first_step(offsets, place, parts, x):
    message = jax.ShapeDtypeStruct((x.shape[0] + B + RECORD, B), jnp.float32)
    return pl.pallas_call(
        functools.partial(first_kernel, len(parts)),
        out_shape=(message, message),
        in_specs=[SMEM, SMEM] + [VMEM] * (len(parts) + 1),
        out_specs=(VMEM, VMEM),
        compiler_params=PARAMS,
    )(offsets, place, *parts, x)


def cross_solve(rows, parts, odd, u_ref, w_ref, offs):
    gram = tree_sum([p[...] for p in parts])
    across = jnp.where(odd, gram, gram.T)
    gu, gw = u_ref[rows : rows + B, :], w_ref[rows : rows + B, :]
    return solve(jnp.where(odd, gu, gw), across, jnp.where(odd, gw, gu), offs)


def middle_kernel(step, rows, count, offs_ref, place_ref, *refs):
    parts, (u_ref, w_ref, in_ref, out_ref) = refs[:count], refs[count:]
    offs = step_offsets(offs_ref, step)
    slot = place_ref[0]
    odd = (slot & 1) == 1
    angles, first, second = cross_solve(rows, parts, odd, u_ref, w_ref, offs)
    past = u_ref.shape[0] - rows - B
    base = rows + B

    def finish(top_ref, low_ref, first_ref, second_ref):
        first_ref[rows : rows + B, :] = first
        second_ref[rows : rows + B, :] = second
        for ref in (first_ref, second_ref):
            write_record(ref, base, angles)
            ref[base + RECORD : base + RECORD + past, :] = top_ref[base : base + past, :]
            ref[base + RECORD + past : base + RECORD + 2 * past, :] = low_ref[base : base + past, :]

        def put(at, t, b):
            first_ref[at, :] = t
            second_ref[at, :] = b

        rotate_rows(rows, angles, offs, lambda at: (top_ref[at, :], low_ref[at, :]), put)

    @pl.when(odd)
    def _():
        finish(u_ref, w_ref, out_ref, in_ref)

    @pl.when(jnp.logical_and(jnp.logical_not(odd), slot != 0))
    def _():
        finish(w_ref, u_ref, in_ref, out_ref)

    @pl.when(slot == 0)
    def _():
        finish(w_ref, u_ref, out_ref, in_ref)


def middle_step(step, rows, offsets, place, parts, u, w):
    past = u.shape[0] - rows - B
    message = jax.ShapeDtypeStruct((rows + B + RECORD + 2 * past, B), jnp.float32)
    return pl.pallas_call(
        functools.partial(middle_kernel, step, rows, len(parts)),
        out_shape=(message, message),
        in_specs=[SMEM, SMEM] + [VMEM] * (len(parts) + 2),
        out_specs=(VMEM, VMEM),
        compiler_params=PARAMS,
    )(offsets, place, *parts, u, w)


def came_from(slot, is_first, pairs):
    if is_first:
        return jnp.where(slot == 0, 0, slot - 1), slot != 1
    last = slot == pairs - 1
    return jnp.where(last, slot, slot + 1), last


def vectors_kernel(rows, offs_ref, place_ref, u_ref, w_ref, out_ref):
    slot, pairs, part = place_ref[0], place_ref[1], place_ref[2]
    odd = (slot & 1) == 1
    held_slots = out_ref.shape[0] // (2 * B)
    base = rows + B
    past = u_ref.shape[0] - base
    out_ref[...] = jnp.zeros_like(out_ref)
    unit = jnp.where(eye_mask(), 1.0, 0.0)

    def descend(block, node, was_first, step, history, columns):
        zero = jnp.zeros_like(block)

        def turned():
            return rotate_back(
                jnp.where(was_first, block, zero),
                jnp.where(was_first, zero, block),
                read_record(history[:RECORD]),
                step_offsets(offs_ref, step),
            )

        if step == 0:

            @pl.when(node // held_slots == part)
            def _():
                at = pl.multiple_of((node - part * held_slots) * (2 * B), 2 * B)
                top, low = turned()
                out_ref[pl.ds(at, B), columns] += top.T
                out_ref[pl.ds(at + B, B), columns] += low.T

            return
        top, low = turned()
        half = (history.shape[0] - RECORD) // 2
        older = (history[RECORD : RECORD + half], history[RECORD + half :])
        descend(top, *came_from(node, True, pairs), step - 1, older[0], columns)
        descend(low, *came_from(node, False, pairs), step - 1, older[1], columns)

    hu, hw = u_ref[base : base + past, :], w_ref[base : base + past, :]
    top_history, low_history = jnp.where(odd, hu, hw), jnp.where(odd, hw, hu)
    descend(unit, *came_from(slot, True, pairs), STEPS - 2, top_history, slice(0, B))
    descend(unit, *came_from(slot, False, pairs), STEPS - 2, low_history, slice(B, 2 * B))


def vectors_before_last(rows, height, offsets, place, u, w):
    return pl.pallas_call(
        functools.partial(vectors_kernel, rows),
        out_shape=jax.ShapeDtypeStruct((height, 2 * B), jnp.float32),
        in_specs=[SMEM, SMEM, VMEM, VMEM],
        out_specs=VMEM,
        compiler_params=PARAMS,
    )(offsets, place, u, w)


def last_kernel(rows, count, offs_ref, place_ref, *refs):
    parts, (u_ref, w_ref, v_ref, x_out, v_out) = refs[:count], refs[count:]
    offs = step_offsets(offs_ref, STEPS - 1)
    odd = (place_ref[0] & 1) == 1
    angles, _, _ = cross_solve(rows, parts, odd, u_ref, w_ref, offs)

    def put(ref):
        def store(at, t, b):
            ref[at, :B] = t
            ref[at, B:] = b

        return store

    @pl.when(odd)
    def _():
        rotate_rows(rows, angles, offs, lambda at: (u_ref[at, :], w_ref[at, :]), put(x_out))

    @pl.when(jnp.logical_not(odd))
    def _():
        rotate_rows(rows, angles, offs, lambda at: (w_ref[at, :], u_ref[at, :]), put(x_out))

    rotate_rows(
        v_ref.shape[0], angles, offs, lambda at: (v_ref[at, :B], v_ref[at, B:]), put(v_out)
    )


def last_step(rows, offsets, place, parts, u, w, v):
    return pl.pallas_call(
        functools.partial(last_kernel, rows, len(parts)),
        out_shape=(
            jax.ShapeDtypeStruct((rows, 2 * B), jnp.float32),
            jax.ShapeDtypeStruct(v.shape, jnp.float32),
        ),
        in_specs=[SMEM, SMEM] + [VMEM] * (len(parts) + 3),
        out_specs=(VMEM, VMEM),
        compiler_params=PARAMS,
    )(offsets, place, *parts, u, w, v)


def in_stages(partial, layout):
    distance, count = 1, lax.axis_size("row")
    while 2 * distance < count:
        partial = partial + send(partial, layout, layout, other_part(distance))
        distance *= 2
    if distance < count:
        return [partial, send(partial, layout, layout, other_part(distance))]
    return [partial]


def at_once(partial, layout):
    others = range(1, lax.axis_size("row"))
    return [partial] + [send(partial, layout, layout, other_part(d)) for d in others]


def body(whitened, offsets):
    rows, width = whitened.shape
    pairs, parts = lax.axis_size("pair"), lax.axis_size("row")
    pair, row = lax.axis_index("pair"), lax.axis_index("row")
    place = {
        layout: jnp.stack([layout(pair, row)[0], jnp.int32(pairs), layout(pair, row)[1]])
        for layout in (given, crossed)
    }
    height = pairs * width // parts

    terms = in_stages(whole_gram(whitened), given)
    near, far = first_step(offsets, place[given], terms, whitened)
    before = given
    for step in range(1, STEPS):
        layout = given if step == STEPS - 1 else crossed
        u = send(near, before, layout, inner)
        w = send(far, before, layout, outer)
        cross = cross_gram(rows, u, w)
        if step < STEPS - 1:
            terms = at_once(cross, layout)
            near, far = middle_step(step, rows, offsets, place[layout], terms, u, w)
        before = layout
    terms = in_stages(cross, given)
    vectors = vectors_before_last(rows, height, offsets, place[given], u, w)
    return last_step(rows, offsets, place[given], terms, u, w, vectors)


def solution(mesh):
    in_specs = (P("row", "pair"), P())
    out_specs = (P("row", "pair"), P("row", "pair"))
    return jax.shard_map(body, mesh=mesh, in_specs=in_specs, out_specs=out_specs, check_vma=False)
```

profile of v0, /device:TPU:0, one launch (start us, length us, event | category | flops | bytes accessed | tf_op | source)
XLA Modules:
  0.0 117.3 jit_solution(509812206504136884)
XLA Ops:
  0.6 0.0 copy-start
  0.6 1.2 %copy-done = f32[1024,256]{1,0:T(8,128)S(1)} copy-done((f32[1024,256]{1,0:T(8,128)S(1)}, f32[1024,256]{1,0:T(8,128)}, u32[]{:S(2)}) %copy-start) | copy-done | bytes 1048600
  1.9 0.0 copy-start.1
  1.9 1.2 %shard_map.41 = f32[384,128]{1,0:T(8,128)S(1)} custom-call(f32[1024,256]{1,0:T(8,128)S(1)} %copy-done), custom_call_target="tpu_custom_call" | custom-call | tf_op jit(solution)/shard_map/pallas_call | solution.py:173
  3.0 0.5 collective-permute-start
  3.6 1.1 collective-permute-done
  4.7 2.9 %collective-permute-start.1 = (f32[384,128]{1,0:T(8,128)S(1)}, f32[384,128]{1,0:T(8,128)S(1)}, u32[]{:S(2)}, u32[]{:S(2)}) collective-permute-start(f32[384,128]{1,0:T(8,128)S(1)} %add.6.refs_0_), channel_id=1, source_target_pairs={{0,2},{1,3},{2,0},{3,1},{4,6},{5,7},{6,4},{7,5},{8,10},{9,11},{10,... | collective-permute-start | bytes 589832 | tf_op jit(solution)/shard_map/ppermute | solution.py:51
  7.6 0.1 fusion.place_ref
  7.7 5.1 %collective-permute-done.1.refs_1_ = f32[384,128]{1,0:T(8,128)S(1)} collective-permute-done((f32[384,128]{1,0:T(8,128)S(1)}, f32[384,128]{1,0:T(8,128)S(1)}, u32[]{:S(2)}, u32[]{:S(2)}) %collective-permute-start.1) | collective-permute-done | bytes 196640 | tf_op jit(solution)/shard_map/ppermute | solution.py:51
  12.8 0.0 copy-done.1
  12.8 0.0 copy-done.2
  12.8 7.6 %shard_map.42 = (f32[1160,128]{1,0:T(8,128)S(1)}, f32[1160,128]{1,0:T(8,128)S(1)}) custom-call(s32[4,4]{1,0:T(4,128)S(1)} %copy-done.2, s32[3]{0:T(128)S(1)} %fusion.place_ref, f32[384,128]{1,0:T(8,128)S(1)} %add.6.refs_0_, f32[384,128]{1,0:T(8,128)S(1)} %collective-permute-done.1.refs_1_, f32[1024,256]{1,0:T(8,128)S(1)} %copy-done.1), custom_call_target="tpu_custom_call" | custom-call | tf_op jit(solution)/shard_map/pallas_call | solution.py:228
  20.4 0.0 collective-permute-start.2
  20.4 0.7 collective-permute-start.3
  21.1 9.2 %collective-permute-done.2.u_ref.refs_4_ = f32[1160,128]{1,0:T(8,128)S(1)} collective-permute-done((f32[1160,128]{1,0:T(8,128)S(1)}, f32[1160,128]{1,0:T(8,128)S(1)}, u32[]{:S(2)}, u32[]{:S(2)}) %collective-permute-start.2) | collective-permute-done | bytes 593952 | tf_op jit(solution)/shard_map/ppermute | solution.py:51
  30.3 0.0 collective-permute-done.3.w_ref.refs_5_
  30.3 0.6 shard_map.43.refs_0_
  30.9 13.8 %collective-permute-start.6 = (f32[128,128]{1,0:T(8,128)S(1)}, f32[128,128]{1,0:T(8,128)S(1)}, u32[]{:S(2)}, u32[]{:S(2)}) collective-permute-start(f32[128,128]{1,0:T(8,128)S(1)} %shard_map.43.refs_0_), channel_id=1, source_target_pairs={{0,6},{4,2},{2,4},{6,0},{1,7},{5,3},{3,5},{7,1},{8,14},{12,10},{10... | collective-permute-start | bytes 196616 | tf_op jit(solution)/shard_map/ppermute | solution.py:51
  44.8 0.5 collective-permute-start.5
  45.3 0.1 collective-permute-start.4
  45.4 0.1 fusion.1.place_ref
  45.5 2.1 %collective-permute-done.6.refs_3_ = f32[128,128]{1,0:T(8,128)S(1)} collective-permute-done((f32[128,128]{1,0:T(8,128)S(1)}, f32[128,128]{1,0:T(8,128)S(1)}, u32[]{:S(2)}, u32[]{:S(2)}) %collective-permute-start.6) | collective-permute-done | bytes 65568 | tf_op jit(solution)/shard_map/ppermute | solution.py:51
  47.6 1.4 %collective-permute-done.5.refs_2_ = f32[128,128]{1,0:T(8,128)S(1)} collective-permute-done((f32[128,128]{1,0:T(8,128)S(1)}, f32[128,128]{1,0:T(8,128)S(1)}, u32[]{:S(2)}, u32[]{:S(2)}) %collective-permute-start.5) | collective-permute-done | bytes 65568 | tf_op jit(solution)/shard_map/ppermute | solution.py:51
  49.0 0.5 collective-permute-done.4.refs_1_
  49.6 7.6 %shard_map.44 = (f32[1176,128]{1,0:T(8,128)S(1)}, f32[1176,128]{1,0:T(8,128)S(1)}) custom-call(s32[4,4]{1,0:T(4,128)S(1)} %copy-done.2, s32[3]{0:T(128)S(1)} %fusion.1.place_ref, f32[128,128]{1,0:T(8,128)S(1)} %shard_map.43.refs_0_, f32[128,128]{1,0:T(8,128)S(1)} %collective-permute-done.4.refs_1_, f32[128,128]{1,0:T(8,128)S(1)} %collective-permute-done.5.refs_2_, ...), custom_call_target="tpu_custom_call" | custom-call | tf_op jit(solution)/shard_map/pallas_call | solution.py:283
  57.2 0.0 collective-permute-start.7
  57.2 0.7 collective-permute-start.8
  58.0 1.3 %collective-permute-done.7.u_ref.refs_4_ = f32[1176,128]{1,0:T(8,128)S(1)} collective-permute-done((f32[1176,128]{1,0:T(8,128)S(1)}, f32[1176,128]{1,0:T(8,128)S(1)}, u32[]{:S(2)}, u32[]{:S(2)}) %collective-permute-start.7) | collective-permute-done | bytes 602144 | tf_op jit(solution)/shard_map/ppermute | solution.py:51
  59.3 0.0 collective-permute-done.8.w_ref.refs_5_
  59.3 0.6 shard_map.45.refs_0_
  59.9 1.1 collective-permute-start.11
  61.0 0.5 collective-permute-start.10
  61.6 1.9 %collective-permute-start.9 = (f32[128,128]{1,0:T(8,128)S(1)}, f32[128,128]{1,0:T(8,128)S(1)}, u32[]{:S(2)}, u32[]{:S(2)}) collective-permute-start(f32[128,128]{1,0:T(8,128)S(1)} %shard_map.45.refs_0_), channel_id=1, source_target_pairs={{0,4},{4,0},{2,6},{6,2},{1,5},{5,1},{3,7},{7,3},{8,12},{12,8},{10,... | collective-permute-start | bytes 196616 | tf_op jit(solution)/shard_map/ppermute | solution.py:51
  63.5 1.7 %collective-permute-done.11.refs_3_ = f32[128,128]{1,0:T(8,128)S(1)} collective-permute-done((f32[128,128]{1,0:T(8,128)S(1)}, f32[128,128]{1,0:T(8,128)S(1)}, u32[]{:S(2)}, u32[]{:S(2)}) %collective-permute-start.11) | collective-permute-done | bytes 65568 | tf_op jit(solution)/shard_map/ppermute | solution.py:51
  65.1 0.2 collective-permute-done.10.refs_2_
  65.3 0.5 collective-permute-done.9.refs_1_
  65.8 7.6 %shard_map.46 = (f32[1208,128]{1,0:T(8,128)S(1)}, f32[1208,128]{1,0:T(8,128)S(1)}) custom-call(s32[4,4]{1,0:T(4,128)S(1)} %copy-done.2, s32[3]{0:T(128)S(1)} %fusion.1.place_ref, f32[128,128]{1,0:T(8,128)S(1)} %shard_map.45.refs_0_, f32[128,128]{1,0:T(8,128)S(1)} %collective-permute-done.9.refs_1_, f32[128,128]{1,0:T(8,128)S(1)} %collective-permute-done.10.refs_2_, ...), custom_call_target="tpu_custom_call" | custom-call | tf_op jit(solution)/shard_map/pallas_call | solution.py:283
  73.5 1.9 %collective-permute-start.12 = (f32[1208,128]{1,0:T(8,128)S(1)}, f32[1208,128]{1,0:T(8,128)S(1)}, u32[]{:S(2)}, u32[]{:S(2)}) collective-permute-start(f32[1208,128]{1,0:T(8,128)S(1)} %get-tuple-element.12), channel_id=1, source_target_pairs={{0,4},{4,5},{2,6},{6,7},{1,0},{5,1},{3,2},{7,3},{8,12},{12,13},{10... | collective-permute-start | bytes 1855496 | tf_op jit(solution)/shard_map/ppermute | solution.py:51
  75.4 0.7 collective-permute-start.13
  76.1 7.6 %collective-permute-done.12.u_ref.refs_2_ = f32[1208,128]{1,0:T(8,128)S(1)} collective-permute-done((f32[1208,128]{1,0:T(8,128)S(1)}, f32[1208,128]{1,0:T(8,128)S(1)}, u32[]{:S(2)}, u32[]{:S(2)}) %collective-permute-start.12) | collective-permute-done | bytes 618528 | tf_op jit(solution)/shard_map/ppermute | solution.py:51
  83.7 0.0 collective-permute-done.13.w_ref.refs_3_
  83.7 0.6 shard_map.47
  84.3 14.2 %collective-permute-start.14 = (f32[128,128]{1,0:T(8,128)S(1)}, f32[128,128]{1,0:T(8,128)S(1)}, u32[]{:S(2)}, u32[]{:S(2)}) collective-permute-start(f32[128,128]{1,0:T(8,128)S(1)} %shard_map.47), channel_id=1, source_target_pairs={{0,1},{1,0},{2,3},{3,2},{4,5},{5,4},{6,7},{7,6},{8,9},{9,8},{10,11... | collective-permute-start | bytes 196616 | tf_op jit(solution)/shard_map/ppermute | solution.py:51
  98.5 0.9 collective-permute-done.14
  99.4 1.6 %collective-permute-start.15 = (f32[128,128]{1,0:T(8,128)S(1)}, f32[128,128]{1,0:T(8,128)S(1)}, u32[]{:S(2)}, u32[]{:S(2)}) collective-permute-start(f32[128,128]{1,0:T(8,128)S(1)} %add.7.refs_0_), channel_id=1, source_target_pairs={{0,2},{1,3},{2,0},{3,1},{4,6},{5,7},{6,4},{7,5},{8,10},{9,11},{10,... | collective-permute-start | bytes 196616 | tf_op jit(solution)/shard_map/ppermute | solution.py:51
  101.0 5.3 %shard_map.48.refs_4_ = f32[512,256]{1,0:T(8,128)S(1)} custom-call(s32[4,4]{1,0:T(4,128)S(1)} %copy-done.2, s32[3]{0:T(128)S(1)} %fusion.place_ref, f32[1208,128]{1,0:T(8,128)S(1)} %collective-permute-done.12.u_ref.refs_2_, f32[1208,128]{1,0:T(8,128)S(1)} %collective-permute-done.13.w_ref.refs_3_), custom_call_target="tpu_custom_call" | custom-call | tf_op jit(solution)/shard_map/pallas_call | solution.py:342
  106.3 0.0 collective-permute-done.15.refs_1_
  106.3 11.0 %shard_map.49 = (f32[1024,256]{1,0:T(8,128)}, f32[512,256]{1,0:T(8,128)}) custom-call(s32[4,4]{1,0:T(4,128)S(1)} %copy-done.2, s32[3]{0:T(128)S(1)} %fusion.place_ref, f32[128,128]{1,0:T(8,128)S(1)} %add.7.refs_0_, f32[128,128]{1,0:T(8,128)S(1)} %collective-permute-done.15.refs_1_, f32[1208,128]{1,0:T(8,128)S(1)} %collective-permute-done.12.u_ref.refs_2_, ...), custom_call_target="tpu_custom_call" | custom-call | tf_op jit(solution)/shard_map/pallas_call | solution.py:378
  (3 shorter events, 0.0 us)
Async XLA Ops:
  0.6 1.2 %copy-start = (f32[1024,256]{1,0:T(8,128)S(1)}, f32[1024,256]{1,0:T(8,128)}, u32[]{:S(2)}) copy-start(f32[1024,256]{1,0:T(8,128)} %refs_2_.1) | copy-start | bytes 3145732
  1.9 10.9 %copy-start.1 = (f32[1024,256]{1,0:T(8,128)S(1)}, f32[1024,256]{1,0:T(8,128)}, u32[]{:S(2)}) copy-start(f32[1024,256]{1,0:T(8,128)} %refs_2_.1) | copy-start | bytes 3145732
  3.0 1.6 %collective-permute-start = (f32[384,128]{1,0:T(8,128)S(1)}, f32[384,128]{1,0:T(8,128)S(1)}, u32[]{:S(2)}, u32[]{:S(2)}) collective-permute-start(f32[384,128]{1,0:T(8,128)S(1)} %shard_map.41), channel_id=1, source_target_pairs={{0,1},{1,0},{2,3},{3,2},{4,5},{5,4},{6,7},{7,6},{8,9},{9,8},{10,11... | collective-permute-start | bytes 589832 | tf_op jit(solution)/shard_map/ppermute | solution.py:51
  4.7 8.1 %collective-permute-start.1 = (f32[384,128]{1,0:T(8,128)S(1)}, f32[384,128]{1,0:T(8,128)S(1)}, u32[]{:S(2)}, u32[]{:S(2)}) collective-permute-start(f32[384,128]{1,0:T(8,128)S(1)} %add.6.refs_0_), channel_id=1, source_target_pairs={{0,2},{1,3},{2,0},{3,1},{4,6},{5,7},{6,4},{7,5},{8,10},{9,11},{10,... | collective-permute-start | bytes 589832 | tf_op jit(solution)/shard_map/ppermute | solution.py:51
  7.6 5.2 %copy-start.2 = (s32[4,4]{1,0:T(4,128)S(1)}, s32[4,4]{1,0:T(4,128)}, u32[]{:S(2)}) copy-start(s32[4,4]{1,0:T(4,128)} %offs_ref.9) | copy-start | bytes 196
  20.4 9.9 %collective-permute-start.2 = (f32[1160,128]{1,0:T(8,128)S(1)}, f32[1160,128]{1,0:T(8,128)S(1)}, u32[]{:S(2)}, u32[]{:S(2)}) collective-permute-start(f32[1160,128]{1,0:T(8,128)S(1)} %get-tuple-element.8), channel_id=1, source_target_pairs={{0,1},{1,5},{2,3},{3,7},{4,0},{5,4},{6,2},{7,6},{8,9},{9,13},{10,1... | collective-permute-start | bytes 1781768 | tf_op jit(solution)/shard_map/ppermute | solution.py:51
  20.4 9.9 %collective-permute-start.3 = (f32[1160,128]{1,0:T(8,128)S(1)}, f32[1160,128]{1,0:T(8,128)S(1)}, u32[]{:S(2)}, u32[]{:S(2)}) collective-permute-start(f32[1160,128]{1,0:T(8,128)S(1)} %get-tuple-element.9), channel_id=1, source_target_pairs={{0,0},{1,4},{2,2},{3,6},{4,8},{5,12},{6,10},{7,14},{8,1},{9,5},{10... | collective-permute-start | bytes 1781768 | tf_op jit(solution)/shard_map/ppermute | solution.py:51
  30.9 16.6 %collective-permute-start.6 = (f32[128,128]{1,0:T(8,128)S(1)}, f32[128,128]{1,0:T(8,128)S(1)}, u32[]{:S(2)}, u32[]{:S(2)}) collective-permute-start(f32[128,128]{1,0:T(8,128)S(1)} %shard_map.43.refs_0_), channel_id=1, source_target_pairs={{0,6},{4,2},{2,4},{6,0},{1,7},{5,3},{3,5},{7,1},{8,14},{12,10},{10... | collective-permute-start | bytes 196616 | tf_op jit(solution)/shard_map/ppermute | solution.py:51
  44.8 4.3 %collective-permute-start.5 = (f32[128,128]{1,0:T(8,128)S(1)}, f32[128,128]{1,0:T(8,128)S(1)}, u32[]{:S(2)}, u32[]{:S(2)}) collective-permute-start(f32[128,128]{1,0:T(8,128)S(1)} %shard_map.43.refs_0_), channel_id=1, source_target_pairs={{0,2},{4,6},{2,0},{6,4},{1,3},{5,7},{3,1},{7,5},{8,10},{12,14},{10... | collective-permute-start | bytes 196616 | tf_op jit(solution)/shard_map/ppermute | solution.py:51
  45.3 4.3 %collective-permute-start.4 = (f32[128,128]{1,0:T(8,128)S(1)}, f32[128,128]{1,0:T(8,128)S(1)}, u32[]{:S(2)}, u32[]{:S(2)}) collective-permute-start(f32[128,128]{1,0:T(8,128)S(1)} %shard_map.43.refs_0_), channel_id=1, source_target_pairs={{0,4},{4,0},{2,6},{6,2},{1,5},{5,1},{3,7},{7,3},{8,12},{12,8},{10,... | collective-permute-start | bytes 196616 | tf_op jit(solution)/shard_map/ppermute | solution.py:51
  57.2 2.0 %collective-permute-start.7 = (f32[1176,128]{1,0:T(8,128)S(1)}, f32[1176,128]{1,0:T(8,128)S(1)}, u32[]{:S(2)}, u32[]{:S(2)}) collective-permute-start(f32[1176,128]{1,0:T(8,128)S(1)} %get-tuple-element.10), channel_id=1, source_target_pairs={{0,1},{4,5},{2,3},{6,7},{1,0},{5,4},{3,2},{7,6},{8,9},{12,13},{10,... | collective-permute-start | bytes 1806344 | tf_op jit(solution)/shard_map/ppermute | solution.py:51
  57.2 2.0 %collective-permute-start.8 = (f32[1176,128]{1,0:T(8,128)S(1)}, f32[1176,128]{1,0:T(8,128)S(1)}, u32[]{:S(2)}, u32[]{:S(2)}) collective-permute-start(f32[1176,128]{1,0:T(8,128)S(1)} %get-tuple-element.11), channel_id=1, source_target_pairs={{0,0},{4,4},{2,2},{6,6},{1,8},{5,12},{3,10},{7,14},{8,1},{12,5},{1... | collective-permute-start | bytes 1806344 | tf_op jit(solution)/shard_map/ppermute | solution.py:51
  59.9 5.2 %collective-permute-start.11 = (f32[128,128]{1,0:T(8,128)S(1)}, f32[128,128]{1,0:T(8,128)S(1)}, u32[]{:S(2)}, u32[]{:S(2)}) collective-permute-start(f32[128,128]{1,0:T(8,128)S(1)} %shard_map.45.refs_0_), channel_id=1, source_target_pairs={{0,6},{4,2},{2,4},{6,0},{1,7},{5,3},{3,5},{7,1},{8,14},{12,10},{10... | collective-permute-start | bytes 196616 | tf_op jit(solution)/shard_map/ppermute | solution.py:51
  61.0 4.3 %collective-permute-start.10 = (f32[128,128]{1,0:T(8,128)S(1)}, f32[128,128]{1,0:T(8,128)S(1)}, u32[]{:S(2)}, u32[]{:S(2)}) collective-permute-start(f32[128,128]{1,0:T(8,128)S(1)} %shard_map.45.refs_0_), channel_id=1, source_target_pairs={{0,2},{4,6},{2,0},{6,4},{1,3},{5,7},{3,1},{7,5},{8,10},{12,14},{10... | collective-permute-start | bytes 196616 | tf_op jit(solution)/shard_map/ppermute | solution.py:51
  61.6 4.3 %collective-permute-start.9 = (f32[128,128]{1,0:T(8,128)S(1)}, f32[128,128]{1,0:T(8,128)S(1)}, u32[]{:S(2)}, u32[]{:S(2)}) collective-permute-start(f32[128,128]{1,0:T(8,128)S(1)} %shard_map.45.refs_0_), channel_id=1, source_target_pairs={{0,4},{4,0},{2,6},{6,2},{1,5},{5,1},{3,7},{7,3},{8,12},{12,8},{10,... | collective-permute-start | bytes 196616 | tf_op jit(solution)/shard_map/ppermute | solution.py:51
  73.5 10.2 %collective-permute-start.12 = (f32[1208,128]{1,0:T(8,128)S(1)}, f32[1208,128]{1,0:T(8,128)S(1)}, u32[]{:S(2)}, u32[]{:S(2)}) collective-permute-start(f32[1208,128]{1,0:T(8,128)S(1)} %get-tuple-element.12), channel_id=1, source_target_pairs={{0,4},{4,5},{2,6},{6,7},{1,0},{5,1},{3,2},{7,3},{8,12},{12,13},{10... | collective-permute-start | bytes 1855496 | tf_op jit(solution)/shard_map/ppermute | solution.py:51
  75.4 8.3 %collective-permute-start.13 = (f32[1208,128]{1,0:T(8,128)S(1)}, f32[1208,128]{1,0:T(8,128)S(1)}, u32[]{:S(2)}, u32[]{:S(2)}) collective-permute-start(f32[1208,128]{1,0:T(8,128)S(1)} %get-tuple-element.13), channel_id=1, source_target_pairs={{0,0},{4,1},{2,2},{6,3},{1,8},{5,9},{3,10},{7,11},{8,4},{12,5},{10... | collective-permute-start | bytes 1855496 | tf_op jit(solution)/shard_map/ppermute | solution.py:51
  84.3 15.1 %collective-permute-start.14 = (f32[128,128]{1,0:T(8,128)S(1)}, f32[128,128]{1,0:T(8,128)S(1)}, u32[]{:S(2)}, u32[]{:S(2)}) collective-permute-start(f32[128,128]{1,0:T(8,128)S(1)} %shard_map.47), channel_id=1, source_target_pairs={{0,1},{1,0},{2,3},{3,2},{4,5},{5,4},{6,7},{7,6},{8,9},{9,8},{10,11... | collective-permute-start | bytes 196616 | tf_op jit(solution)/shard_map/ppermute | solution.py:51
  99.4 6.9 %collective-permute-start.15 = (f32[128,128]{1,0:T(8,128)S(1)}, f32[128,128]{1,0:T(8,128)S(1)}, u32[]{:S(2)}, u32[]{:S(2)}) collective-permute-start(f32[128,128]{1,0:T(8,128)S(1)} %add.7.refs_0_), channel_id=1, source_target_pairs={{0,2},{1,3},{2,0},{3,1},{4,6},{5,7},{6,4},{7,5},{8,10},{9,11},{10,... | collective-permute-start | bytes 196616 | tf_op jit(solution)/shard_map/ppermute | solution.py:51
where the time goes:
time: 118 us; the launch traced here: 117 us
  Pallas kernels  42.3 us (36%)
  starting transfers between devices  41.2 us (35%)
  waiting for transfers between devices  31.7 us (27%)
  local copies, waits for them, and re-layouts  1.23 us (1%)
    ppermute x16, starting transfers between devices, send(): return lax.ppermute(x, AXES, route(source, target, change))  41.2 us
    ppermute x16, waiting for transfers between devices, send(): return lax.ppermute(x, AXES, route(source, target, change))  31.7 us
    pallas_call x2, Pallas kernels, middle_step(): pl.pallas_call(functools.partial(middle_kernel, step, rows, len(parts)),...  15.3 us
    pallas_call x1, Pallas kernels, last_step(): pl.pallas_call(functools.partial(last_kernel, rows, len(parts)), out_shap...  11 us
    pallas_call x1, Pallas kernels, first_step(): pl.pallas_call(functools.partial(first_kernel, len(parts)), out_shape=(me...  7.57 us
    pallas_call x1, Pallas kernels, vectors_before_last(): pl.pallas_call(functools.partial(vectors_kernel, rows), out_shape=jax.Sha...  5.31 us
  transfers between devices with their start and end apart: 16, of which 12 were waited for; matrix products, arithmetic and copies ran while one was open for 0% of the time, Pallas kernels for 5%

commit v1 on v0

--- a/solution.py
+++ b/solution.py
@@ -11,7 +11,6 @@
 ROUNDS = 4
 STEPS = 4
 RECORD = 2 * ROUNDS
-CHUNK = 64
 AXES = ("pair", "row")
 PARAMS = pltpu.CompilerParams(vmem_limit_bytes=40 * 1024 * 1024)
 VMEM = pl.BlockSpec(memory_space=pltpu.VMEM)
@@ -55,15 +54,16 @@
     return lambda slot, part, pairs: (slot, part ^ distance)
 
 
-def back(shift_by):
-    return (B - shift_by) & (B - 1)
-
-
 def eye_mask():
     shape = (B, B)
     return lax.broadcasted_iota(jnp.int32, shape, 0) == lax.broadcasted_iota(jnp.int32, shape, 1)
 
 
+def identity_halves():
+    unit = jnp.where(eye_mask(), 1.0, 0.0)
+    return [(unit, jnp.zeros_like(unit)), (jnp.zeros_like(unit), unit)]
+
+
 def diagonal(mask, block):
     return jnp.sum(jnp.where(mask, block, 0.0), axis=0, keepdims=True)
 
@@ -75,12 +75,14 @@
 def solve(first, across, second, offs):
     mask = eye_mask()
     angles = []
+    turns = identity_halves()
     held = 0
     for r in range(ROUNDS):
         turn = (held - offs[r]) & (B - 1)
         held = offs[r]
         across = pltpu.roll(across, turn, 1)
         second = pltpu.roll(pltpu.roll(second, turn, 1), turn, 0)
+        turns = [(top, pltpu.roll(low, turn, 1)) for top, low in turns]
         a = diagonal(mask, first)
         d = diagonal(mask, second)
         c0 = diagonal(mask, across)
@@ -100,18 +102,11 @@
         first = cc * first1 + sc * below1
         across = cc * across1 + sc * second1
         second = cc * second1 - sc * across1
+        turns = [(c * top + s * low, c * low - s * top) for top, low in turns]
     second = pltpu.roll(pltpu.roll(second, held, 1), held, 0)
-    return angles, first, second
-
-
-def rotate(first, second, angles, offs):
-    held = 0
-    for r in range(ROUNDS):
-        c, s = angles[r]
-        second = pltpu.roll(second, (held - offs[r]) & (B - 1), 1)
-        held = offs[r]
-        first, second = c * first + s * second, c * second - s * first
-    return first, pltpu.roll(second, held, 1)
+    turns = [(top, pltpu.roll(low, held, 1)) for top, low in turns]
+    rotation = jnp.concatenate([jnp.concatenate(t, axis=1) for t in turns], axis=0)
+    return angles, rotation, first, second
 
 
 def rotate_back(first, second, angles, offs):
@@ -141,11 +136,19 @@
     return parts[0]
 
 
-def rotate_rows(rows, angles, offs, take, put):
-    @pl.loop(0, rows // CHUNK)
-    def _(i):
-        at = pl.ds(pl.multiple_of(i * CHUNK, CHUNK), CHUNK)
-        put(at, *rotate(*take(at), angles, offs))
+def split(x):
+    high = x.astype(jnp.bfloat16)
+    return high, (x - high.astype(jnp.float32)).astype(jnp.bfloat16)
+
+
+def product(x, rotation):
+    xh, xl = split(x)
+    rh, rl = split(rotation)
+
+    def dot(a, b):
+        return jnp.dot(a, b, preferred_element_type=jnp.float32)
+
+    return (dot(xl, rh) + dot(xh, rl)) + dot(xh, rh)
 
 
 def step_offsets(offs_ref, step):
@@ -198,7 +201,7 @@
     rows = x_ref.shape[0]
     offs = step_offsets(offs_ref, 0)
     gram = tree_sum([p[...] for p in parts])
-    angles, first, second = solve(gram[:B], gram[B : 2 * B], gram[2 * B :], offs)
+    angles, rotation, first, second = solve(gram[:B], gram[B : 2 * B], gram[2 * B :], offs)
     slot = place_ref[0]
     swap = jnp.logical_and((slot & 1) == 0, slot != 0)
 
@@ -208,11 +211,9 @@
         write_record(first_ref, rows + B, angles)
         write_record(second_ref, rows + B, angles)
 
-        def put(at, t, b):
-            first_ref[at, :] = t
-            second_ref[at, :] = b
-
-        rotate_rows(rows, angles, offs, lambda at: (x_ref[at, :B], x_ref[at, B:]), put)
+        x = product(x_ref[...], rotation)
+        first_ref[:rows, :] = x[:, :B]
+        second_ref[:rows, :] = x[:, B:]
 
     @pl.when(swap)
     def _():
@@ -246,7 +247,7 @@
     offs = step_offsets(offs_ref, step)
     slot = place_ref[0]
     odd = (slot & 1) == 1
-    angles, first, second = cross_solve(rows, parts, odd, u_ref, w_ref, offs)
+    angles, rotation, first, second = cross_solve(rows, parts, odd, u_ref, w_ref, offs)
     past = u_ref.shape[0] - rows - B
     base = rows + B
 
@@ -258,11 +259,9 @@
             ref[base + RECORD : base + RECORD + past, :] = top_ref[base : base + past, :]
             ref[base + RECORD + past : base + RECORD + 2 * past, :] = low_ref[base : base + past, :]
 
-        def put(at, t, b):
-            first_ref[at, :] = t
-            second_ref[at, :] = b
-
-        rotate_rows(rows, angles, offs, lambda at: (top_ref[at, :], low_ref[at, :]), put)
+        x = product(jnp.concatenate([top_ref[:rows, :], low_ref[:rows, :]], axis=1), rotation)
+        first_ref[:rows, :] = x[:, :B]
+        second_ref[:rows, :] = x[:, B:]
 
     @pl.when(odd)
     def _():
@@ -352,26 +351,17 @@
     parts, (u_ref, w_ref, v_ref, x_out, v_out) = refs[:count], refs[count:]
     offs = step_offsets(offs_ref, STEPS - 1)
     odd = (place_ref[0] & 1) == 1
-    angles, _, _ = cross_solve(rows, parts, odd, u_ref, w_ref, offs)
-
-    def put(ref):
-        def store(at, t, b):
-            ref[at, :B] = t
-            ref[at, B:] = b
-
-        return store
+    _, rotation, _, _ = cross_solve(rows, parts, odd, u_ref, w_ref, offs)
 
     @pl.when(odd)
     def _():
-        rotate_rows(rows, angles, offs, lambda at: (u_ref[at, :], w_ref[at, :]), put(x_out))
+        x_out[...] = product(jnp.concatenate([u_ref[:rows, :], w_ref[:rows, :]], axis=1), rotation)
 
     @pl.when(jnp.logical_not(odd))
     def _():
-        rotate_rows(rows, angles, offs, lambda at: (w_ref[at, :], u_ref[at, :]), put(x_out))
-
-    rotate_rows(
-        v_ref.shape[0], angles, offs, lambda at: (v_ref[at, :B], v_ref[at, B:]), put(v_out)
-    )
+        x_out[...] = product(jnp.concatenate([w_ref[:rows, :], u_ref[:rows, :]], axis=1), rotation)
+
+    v_out[...] = product(v_ref[...], rotation)
 
 
 def last_step(rows, offsets, place, parts, u, w, v):

time: 118 us -> 95.8 us (0.81)
  Pallas kernels: 42.3 us -> 19.8 us
    pallas_call x2, Pallas kernels: 15.3 us -> 5.14 us  [middle_step(): pl.pallas_call(functools.partial(middle_kernel, step, rows, len(parts)),...]
    pallas_call x1, Pallas kernels: 11 us -> 3.75 us  [last_step(): pl.pallas_call(functools.partial(last_kernel, rows, len(parts)), out_shap...]
    pallas_call x1, Pallas kernels: 7.57 us -> 2.51 us  [first_step(): pl.pallas_call(functools.partial(first_kernel, len(parts)), out_shape=(me...]
  transfers between devices with their start and end apart: 16 -> 16, of which waited for: 12 -> 12; matrix products, arithmetic and copies ran while one was open for 0% -> 0% of each run, Pallas kernels for 5% -> 6%
where the time goes in v1:
time: 95.8 us; the launch traced here: 95.6 us
  starting transfers between devices  41.6 us (43%)
  waiting for transfers between devices  32 us (33%)
  Pallas kernels  19.8 us (21%)
  local copies, waits for them, and re-layouts  1.23 us (1%)
    ppermute x16, starting transfers between devices, send(): return lax.ppermute(x, AXES, route(source, target, change))  41.6 us
    ppermute x16, waiting for transfers between devices, send(): return lax.ppermute(x, AXES, route(source, target, change))  32 us
    pallas_call x1, Pallas kernels, vectors_before_last(): pl.pallas_call(functools.partial(vectors_kernel, rows), out_shape=jax.Sha...  5.31 us
    pallas_call x2, Pallas kernels, middle_step(): pl.pallas_call(functools.partial(middle_kernel, step, rows, len(parts)),...  5.14 us
    pallas_call x1, Pallas kernels, last_step(): pl.pallas_call(functools.partial(last_kernel, rows, len(parts)), out_shap...  3.75 us
    pallas_call x1, Pallas kernels, first_step(): pl.pallas_call(functools.partial(first_kernel, len(parts)), out_shape=(me...  2.51 us
    pallas_call x3, Pallas kernels, cross_gram(): pl.pallas_call(functools.partial(cross_gram_kernel, rows), out_shape=jax....  1.92 us
  transfers between devices with their start and end apart: 16, of which 12 were waited for; matrix products, arithmetic and copies ran while one was open for 0% of the time, Pallas kernels for 6%

profile of v1, /device:TPU:0, one launch (start us, length us, event | category | flops | bytes accessed | tf_op | source)
XLA Modules:
  0.0 95.6 jit_solution(18378827469104403928)
XLA Ops:
  0.6 0.0 copy-start
  0.6 1.2 %copy-done = f32[1024,256]{1,0:T(8,128)S(1)} copy-done((f32[1024,256]{1,0:T(8,128)S(1)}, f32[1024,256]{1,0:T(8,128)}, u32[]{:S(2)}) %copy-start) | copy-done | bytes 1048600
  1.9 0.0 copy-start.1
  1.9 1.2 %shard_map.41 = f32[384,128]{1,0:T(8,128)S(1)} custom-call(f32[1024,256]{1,0:T(8,128)S(1)} %copy-done), custom_call_target="tpu_custom_call" | custom-call | tf_op jit(solution)/shard_map/pallas_call | solution.py:176
  3.0 0.5 collective-permute-start
  3.6 1.1 %collective-permute-done = f32[384,128]{1,0:T(8,128)S(1)} collective-permute-done((f32[384,128]{1,0:T(8,128)S(1)}, f32[384,128]{1,0:T(8,128)S(1)}, u32[]{:S(2)}, u32[]{:S(2)}) %collective-permute-start) | collective-permute-done | bytes 196640 | tf_op jit(solution)/shard_map/ppermute | solution.py:50
  4.7 2.9 %collective-permute-start.1 = (f32[384,128]{1,0:T(8,128)S(1)}, f32[384,128]{1,0:T(8,128)S(1)}, u32[]{:S(2)}, u32[]{:S(2)}) collective-permute-start(f32[384,128]{1,0:T(8,128)S(1)} %add.6.refs_0_), channel_id=1, source_target_pairs={{0,2},{1,3},{2,0},{3,1},{4,6},{5,7},{6,4},{7,5},{8,10},{9,11},{10,... | collective-permute-start | bytes 589832 | tf_op jit(solution)/shard_map/ppermute | solution.py:50
  7.6 0.1 fusion.place_ref
  7.7 5.1 %collective-permute-done.1.refs_1_ = f32[384,128]{1,0:T(8,128)S(1)} collective-permute-done((f32[384,128]{1,0:T(8,128)S(1)}, f32[384,128]{1,0:T(8,128)S(1)}, u32[]{:S(2)}, u32[]{:S(2)}) %collective-permute-start.1) | collective-permute-done | bytes 196640 | tf_op jit(solution)/shard_map/ppermute | solution.py:50
  12.8 0.0 copy-done.1
  12.8 0.0 copy-done.2
  12.8 2.5 %shard_map.42 = (f32[1160,128]{1,0:T(8,128)S(1)}, f32[1160,128]{1,0:T(8,128)S(1)}) custom-call(s32[4,4]{1,0:T(4,128)S(1)} %copy-done.2, s32[3]{0:T(128)S(1)} %fusion.place_ref, f32[384,128]{1,0:T(8,128)S(1)} %add.6.refs_0_, f32[384,128]{1,0:T(8,128)S(1)} %collective-permute-done.1.refs_1_, f32[1024,256]{1,0:T(8,128)S(1)} %copy-done.1), custom_call_target="tpu_custom_call" | custom-call | tf_op jit(solution)/shard_map/pallas_call | solution.py:229
  15.3 0.0 collective-permute-start.2
  15.3 0.7 collective-permute-start.3
  16.1 9.2 %collective-permute-done.2.u_ref.refs_4_ = f32[1160,128]{1,0:T(8,128)S(1)} collective-permute-done((f32[1160,128]{1,0:T(8,128)S(1)}, f32[1160,128]{1,0:T(8,128)S(1)}, u32[]{:S(2)}, u32[]{:S(2)}) %collective-permute-start.2) | collective-permute-done | bytes 593952 | tf_op jit(solution)/shard_map/ppermute | solution.py:50
  25.3 0.0 collective-permute-done.3.w_ref.refs_5_
  25.3 0.6 shard_map.43.refs_0_
  25.9 13.8 %collective-permute-start.6 = (f32[128,128]{1,0:T(8,128)S(1)}, f32[128,128]{1,0:T(8,128)S(1)}, u32[]{:S(2)}, u32[]{:S(2)}) collective-permute-start(f32[128,128]{1,0:T(8,128)S(1)} %shard_map.43.refs_0_), channel_id=1, source_target_pairs={{0,6},{4,2},{2,4},{6,0},{1,7},{5,3},{3,5},{7,1},{8,14},{12,10},{10... | collective-permute-start | bytes 196616 | tf_op jit(solution)/shard_map/ppermute | solution.py:50
  39.7 0.5 collective-permute-start.5
  40.3 0.1 collective-permute-start.4
  40.4 0.1 fusion.1.place_ref
  40.5 2.1 %collective-permute-done.6.refs_3_ = f32[128,128]{1,0:T(8,128)S(1)} collective-permute-done((f32[128,128]{1,0:T(8,128)S(1)}, f32[128,128]{1,0:T(8,128)S(1)}, u32[]{:S(2)}, u32[]{:S(2)}) %collective-permute-start.6) | collective-permute-done | bytes 65568 | tf_op jit(solution)/shard_map/ppermute | solution.py:50
  42.5 1.5 %collective-permute-done.5.refs_2_ = f32[128,128]{1,0:T(8,128)S(1)} collective-permute-done((f32[128,128]{1,0:T(8,128)S(1)}, f32[128,128]{1,0:T(8,128)S(1)}, u32[]{:S(2)}, u32[]{:S(2)}) %collective-permute-start.5) | collective-permute-done | bytes 65568 | tf_op jit(solution)/shard_map/ppermute | solution.py:50
  44.0 0.5 collective-permute-done.4.refs_1_
  44.5 2.6 %shard_map.44 = (f32[1176,128]{1,0:T(8,128)S(1)}, f32[1176,128]{1,0:T(8,128)S(1)}) custom-call(s32[4,4]{1,0:T(4,128)S(1)} %copy-done.2, s32[3]{0:T(128)S(1)} %fusion.1.place_ref, f32[128,128]{1,0:T(8,128)S(1)} %shard_map.43.refs_0_, f32[128,128]{1,0:T(8,128)S(1)} %collective-permute-done.4.refs_1_, f32[128,128]{1,0:T(8,128)S(1)} %collective-permute-done.5.refs_2_, ...), custom_call_target="tpu_custom_call" | custom-call | tf_op jit(solution)/shard_map/pallas_call | solution.py:282
  47.1 0.1 collective-permute-start.7
  47.2 0.7 collective-permute-start.8
  47.9 1.3 %collective-permute-done.7.u_ref.refs_4_ = f32[1176,128]{1,0:T(8,128)S(1)} collective-permute-done((f32[1176,128]{1,0:T(8,128)S(1)}, f32[1176,128]{1,0:T(8,128)S(1)}, u32[]{:S(2)}, u32[]{:S(2)}) %collective-permute-start.7) | collective-permute-done | bytes 602144 | tf_op jit(solution)/shard_map/ppermute | solution.py:50
  49.2 0.0 collective-permute-done.8.w_ref.refs_5_
  49.2 0.6 shard_map.45.refs_0_
  49.8 1.1 %collective-permute-start.11 = (f32[128,128]{1,0:T(8,128)S(1)}, f32[128,128]{1,0:T(8,128)S(1)}, u32[]{:S(2)}, u32[]{:S(2)}) collective-permute-start(f32[128,128]{1,0:T(8,128)S(1)} %shard_map.45.refs_0_), channel_id=1, source_target_pairs={{0,6},{4,2},{2,4},{6,0},{1,7},{5,3},{3,5},{7,1},{8,14},{12,10},{10... | collective-permute-start | bytes 196616 | tf_op jit(solution)/shard_map/ppermute | solution.py:50
  51.0 0.5 collective-permute-start.10
  51.5 1.9 %collective-permute-start.9 = (f32[128,128]{1,0:T(8,128)S(1)}, f32[128,128]{1,0:T(8,128)S(1)}, u32[]{:S(2)}, u32[]{:S(2)}) collective-permute-start(f32[128,128]{1,0:T(8,128)S(1)} %shard_map.45.refs_0_), channel_id=1, source_target_pairs={{0,4},{4,0},{2,6},{6,2},{1,5},{5,1},{3,7},{7,3},{8,12},{12,8},{10,... | collective-permute-start | bytes 196616 | tf_op jit(solution)/shard_map/ppermute | solution.py:50
  53.4 1.7 %collective-permute-done.11.refs_3_ = f32[128,128]{1,0:T(8,128)S(1)} collective-permute-done((f32[128,128]{1,0:T(8,128)S(1)}, f32[128,128]{1,0:T(8,128)S(1)}, u32[]{:S(2)}, u32[]{:S(2)}) %collective-permute-start.11) | collective-permute-done | bytes 65568 | tf_op jit(solution)/shard_map/ppermute | solution.py:50
  55.1 0.2 collective-permute-done.10.refs_2_
  55.2 0.5 collective-permute-done.9.refs_1_
  55.8 2.6 %shard_map.46 = (f32[1208,128]{1,0:T(8,128)S(1)}, f32[1208,128]{1,0:T(8,128)S(1)}) custom-call(s32[4,4]{1,0:T(4,128)S(1)} %copy-done.2, s32[3]{0:T(128)S(1)} %fusion.1.place_ref, f32[128,128]{1,0:T(8,128)S(1)} %shard_map.45.refs_0_, f32[128,128]{1,0:T(8,128)S(1)} %collective-permute-done.9.refs_1_, f32[128,128]{1,0:T(8,128)S(1)} %collective-permute-done.10.refs_2_, ...), custom_call_target="tpu_custom_call" | custom-call | tf_op jit(solution)/shard_map/pallas_call | solution.py:282
  58.3 1.9 %collective-permute-start.12 = (f32[1208,128]{1,0:T(8,128)S(1)}, f32[1208,128]{1,0:T(8,128)S(1)}, u32[]{:S(2)}, u32[]{:S(2)}) collective-permute-start(f32[1208,128]{1,0:T(8,128)S(1)} %get-tuple-element.12), channel_id=1, source_target_pairs={{0,4},{4,5},{2,6},{6,7},{1,0},{5,1},{3,2},{7,3},{8,12},{12,13},{10... | collective-permute-start | bytes 1855496 | tf_op jit(solution)/shard_map/ppermute | solution.py:50
  60.3 0.9 collective-permute-start.13
  61.1 7.9 %collective-permute-done.12.u_ref.refs_2_ = f32[1208,128]{1,0:T(8,128)S(1)} collective-permute-done((f32[1208,128]{1,0:T(8,128)S(1)}, f32[1208,128]{1,0:T(8,128)S(1)}, u32[]{:S(2)}, u32[]{:S(2)}) %collective-permute-start.12) | collective-permute-done | bytes 618528 | tf_op jit(solution)/shard_map/ppermute | solution.py:50
  69.1 0.0 collective-permute-done.13.w_ref.refs_3_
  69.1 0.6 shard_map.47
  69.7 14.3 %collective-permute-start.14 = (f32[128,128]{1,0:T(8,128)S(1)}, f32[128,128]{1,0:T(8,128)S(1)}, u32[]{:S(2)}, u32[]{:S(2)}) collective-permute-start(f32[128,128]{1,0:T(8,128)S(1)} %shard_map.47), channel_id=1, source_target_pairs={{0,1},{1,0},{2,3},{3,2},{4,5},{5,4},{6,7},{7,6},{8,9},{9,8},{10,11... | collective-permute-start | bytes 196616 | tf_op jit(solution)/shard_map/ppermute | solution.py:50
  84.0 0.9 collective-permute-done.14
  85.0 1.6 %collective-permute-start.15 = (f32[128,128]{1,0:T(8,128)S(1)}, f32[128,128]{1,0:T(8,128)S(1)}, u32[]{:S(2)}, u32[]{:S(2)}) collective-permute-start(f32[128,128]{1,0:T(8,128)S(1)} %add.7.refs_0_), channel_id=1, source_target_pairs={{0,2},{1,3},{2,0},{3,1},{4,6},{5,7},{6,4},{7,5},{8,10},{9,11},{10,... | collective-permute-start | bytes 196616 | tf_op jit(solution)/shard_map/ppermute | solution.py:50
  86.5 5.3 %shard_map.48.refs_4_ = f32[512,256]{1,0:T(8,128)S(1)} custom-call(s32[4,4]{1,0:T(4,128)S(1)} %copy-done.2, s32[3]{0:T(128)S(1)} %fusion.place_ref, f32[1208,128]{1,0:T(8,128)S(1)} %collective-permute-done.12.u_ref.refs_2_, f32[1208,128]{1,0:T(8,128)S(1)} %collective-permute-done.13.w_ref.refs_3_), custom_call_target="tpu_custom_call" | custom-call | tf_op jit(solution)/shard_map/pallas_call | solution.py:341
  91.8 0.0 collective-permute-done.15.refs_1_
  91.9 3.8 %shard_map.49 = (f32[1024,256]{1,0:T(8,128)}, f32[512,256]{1,0:T(8,128)}) custom-call(s32[4,4]{1,0:T(4,128)S(1)} %copy-done.2, s32[3]{0:T(128)S(1)} %fusion.place_ref, f32[128,128]{1,0:T(8,128)S(1)} %add.7.refs_0_, f32[128,128]{1,0:T(8,128)S(1)} %collective-permute-done.15.refs_1_, f32[1208,128]{1,0:T(8,128)S(1)} %collective-permute-done.12.u_ref.refs_2_, ...), custom_call_target="tpu_custom_call" | custom-call | tf_op jit(solution)/shard_map/pallas_call | solution.py:368
  (3 shorter events, 0.0 us)
Async XLA Ops:
  0.6 1.2 %copy-start = (f32[1024,256]{1,0:T(8,128)S(1)}, f32[1024,256]{1,0:T(8,128)}, u32[]{:S(2)}) copy-start(f32[1024,256]{1,0:T(8,128)} %refs_2_.1) | copy-start | bytes 3145732
  1.9 10.9 %copy-start.1 = (f32[1024,256]{1,0:T(8,128)S(1)}, f32[1024,256]{1,0:T(8,128)}, u32[]{:S(2)}) copy-start(f32[1024,256]{1,0:T(8,128)} %refs_2_.1) | copy-start | bytes 3145732
  3.0 1.6 %collective-permute-start = (f32[384,128]{1,0:T(8,128)S(1)}, f32[384,128]{1,0:T(8,128)S(1)}, u32[]{:S(2)}, u32[]{:S(2)}) collective-permute-start(f32[384,128]{1,0:T(8,128)S(1)} %shard_map.41), channel_id=1, source_target_pairs={{0,1},{1,0},{2,3},{3,2},{4,5},{5,4},{6,7},{7,6},{8,9},{9,8},{10,11... | collective-permute-start | bytes 589832 | tf_op jit(solution)/shard_map/ppermute | solution.py:50
  4.7 8.1 %collective-permute-start.1 = (f32[384,128]{1,0:T(8,128)S(1)}, f32[384,128]{1,0:T(8,128)S(1)}, u32[]{:S(2)}, u32[]{:S(2)}) collective-permute-start(f32[384,128]{1,0:T(8,128)S(1)} %add.6.refs_0_), channel_id=1, source_target_pairs={{0,2},{1,3},{2,0},{3,1},{4,6},{5,7},{6,4},{7,5},{8,10},{9,11},{10,... | collective-permute-start | bytes 589832 | tf_op jit(solution)/shard_map/ppermute | solution.py:50
  7.6 5.2 %copy-start.2 = (s32[4,4]{1,0:T(4,128)S(1)}, s32[4,4]{1,0:T(4,128)}, u32[]{:S(2)}) copy-start(s32[4,4]{1,0:T(4,128)} %offs_ref.9) | copy-start | bytes 196
  15.3 9.9 %collective-permute-start.2 = (f32[1160,128]{1,0:T(8,128)S(1)}, f32[1160,128]{1,0:T(8,128)S(1)}, u32[]{:S(2)}, u32[]{:S(2)}) collective-permute-start(f32[1160,128]{1,0:T(8,128)S(1)} %get-tuple-element.8), channel_id=1, source_target_pairs={{0,1},{1,5},{2,3},{3,7},{4,0},{5,4},{6,2},{7,6},{8,9},{9,13},{10,1... | collective-permute-start | bytes 1781768 | tf_op jit(solution)/shard_map/ppermute | solution.py:50
  15.3 9.9 %collective-permute-start.3 = (f32[1160,128]{1,0:T(8,128)S(1)}, f32[1160,128]{1,0:T(8,128)S(1)}, u32[]{:S(2)}, u32[]{:S(2)}) collective-permute-start(f32[1160,128]{1,0:T(8,128)S(1)} %get-tuple-element.9), channel_id=1, source_target_pairs={{0,0},{1,4},{2,2},{3,6},{4,8},{5,12},{6,10},{7,14},{8,1},{9,5},{10... | collective-permute-start | bytes 1781768 | tf_op jit(solution)/shard_map/ppermute | solution.py:50
  25.9 16.6 %collective-permute-start.6 = (f32[128,128]{1,0:T(8,128)S(1)}, f32[128,128]{1,0:T(8,128)S(1)}, u32[]{:S(2)}, u32[]{:S(2)}) collective-permute-start(f32[128,128]{1,0:T(8,128)S(1)} %shard_map.43.refs_0_), channel_id=1, source_target_pairs={{0,6},{4,2},{2,4},{6,0},{1,7},{5,3},{3,5},{7,1},{8,14},{12,10},{10... | collective-permute-start | bytes 196616 | tf_op jit(solution)/shard_map/ppermute | solution.py:50
  39.7 4.3 %collective-permute-start.5 = (f32[128,128]{1,0:T(8,128)S(1)}, f32[128,128]{1,0:T(8,128)S(1)}, u32[]{:S(2)}, u32[]{:S(2)}) collective-permute-start(f32[128,128]{1,0:T(8,128)S(1)} %shard_map.43.refs_0_), channel_id=1, source_target_pairs={{0,2},{4,6},{2,0},{6,4},{1,3},{5,7},{3,1},{7,5},{8,10},{12,14},{10... | collective-permute-start | bytes 196616 | tf_op jit(solution)/shard_map/ppermute | solution.py:50
  40.3 4.3 %collective-permute-start.4 = (f32[128,128]{1,0:T(8,128)S(1)}, f32[128,128]{1,0:T(8,128)S(1)}, u32[]{:S(2)}, u32[]{:S(2)}) collective-permute-start(f32[128,128]{1,0:T(8,128)S(1)} %shard_map.43.refs_0_), channel_id=1, source_target_pairs={{0,4},{4,0},{2,6},{6,2},{1,5},{5,1},{3,7},{7,3},{8,12},{12,8},{10,... | collective-permute-start | bytes 196616 | tf_op jit(solution)/shard_map/ppermute | solution.py:50
  47.1 2.1 %collective-permute-start.7 = (f32[1176,128]{1,0:T(8,128)S(1)}, f32[1176,128]{1,0:T(8,128)S(1)}, u32[]{:S(2)}, u32[]{:S(2)}) collective-permute-start(f32[1176,128]{1,0:T(8,128)S(1)} %get-tuple-element.10), channel_id=1, source_target_pairs={{0,1},{4,5},{2,3},{6,7},{1,0},{5,4},{3,2},{7,6},{8,9},{12,13},{10,... | collective-permute-start | bytes 1806344 | tf_op jit(solution)/shard_map/ppermute | solution.py:50
  47.2 2.0 %collective-permute-start.8 = (f32[1176,128]{1,0:T(8,128)S(1)}, f32[1176,128]{1,0:T(8,128)S(1)}, u32[]{:S(2)}, u32[]{:S(2)}) collective-permute-start(f32[1176,128]{1,0:T(8,128)S(1)} %get-tuple-element.11), channel_id=1, source_target_pairs={{0,0},{4,4},{2,2},{6,6},{1,8},{5,12},{3,10},{7,14},{8,1},{12,5},{1... | collective-permute-start | bytes 1806344 | tf_op jit(solution)/shard_map/ppermute | solution.py:50
  49.8 5.2 %collective-permute-start.11 = (f32[128,128]{1,0:T(8,128)S(1)}, f32[128,128]{1,0:T(8,128)S(1)}, u32[]{:S(2)}, u32[]{:S(2)}) collective-permute-start(f32[128,128]{1,0:T(8,128)S(1)} %shard_map.45.refs_0_), channel_id=1, source_target_pairs={{0,6},{4,2},{2,4},{6,0},{1,7},{5,3},{3,5},{7,1},{8,14},{12,10},{10... | collective-permute-start | bytes 196616 | tf_op jit(solution)/shard_map/ppermute | solution.py:50
  51.0 4.3 %collective-permute-start.10 = (f32[128,128]{1,0:T(8,128)S(1)}, f32[128,128]{1,0:T(8,128)S(1)}, u32[]{:S(2)}, u32[]{:S(2)}) collective-permute-start(f32[128,128]{1,0:T(8,128)S(1)} %shard_map.45.refs_0_), channel_id=1, source_target_pairs={{0,2},{4,6},{2,0},{6,4},{1,3},{5,7},{3,1},{7,5},{8,10},{12,14},{10... | collective-permute-start | bytes 196616 | tf_op jit(solution)/shard_map/ppermute | solution.py:50
  51.5 4.3 %collective-permute-start.9 = (f32[128,128]{1,0:T(8,128)S(1)}, f32[128,128]{1,0:T(8,128)S(1)}, u32[]{:S(2)}, u32[]{:S(2)}) collective-permute-start(f32[128,128]{1,0:T(8,128)S(1)} %shard_map.45.refs_0_), channel_id=1, source_target_pairs={{0,4},{4,0},{2,6},{6,2},{1,5},{5,1},{3,7},{7,3},{8,12},{12,8},{10,... | collective-permute-start | bytes 196616 | tf_op jit(solution)/shard_map/ppermute | solution.py:50
  58.3 10.7 %collective-permute-start.12 = (f32[1208,128]{1,0:T(8,128)S(1)}, f32[1208,128]{1,0:T(8,128)S(1)}, u32[]{:S(2)}, u32[]{:S(2)}) collective-permute-start(f32[1208,128]{1,0:T(8,128)S(1)} %get-tuple-element.12), channel_id=1, source_target_pairs={{0,4},{4,5},{2,6},{6,7},{1,0},{5,1},{3,2},{7,3},{8,12},{12,13},{10... | collective-permute-start | bytes 1855496 | tf_op jit(solution)/shard_map/ppermute | solution.py:50
  60.3 8.8 %collective-permute-start.13 = (f32[1208,128]{1,0:T(8,128)S(1)}, f32[1208,128]{1,0:T(8,128)S(1)}, u32[]{:S(2)}, u32[]{:S(2)}) collective-permute-start(f32[1208,128]{1,0:T(8,128)S(1)} %get-tuple-element.13), channel_id=1, source_target_pairs={{0,0},{4,1},{2,2},{6,3},{1,8},{5,9},{3,10},{7,11},{8,4},{12,5},{10... | collective-permute-start | bytes 1855496 | tf_op jit(solution)/shard_map/ppermute | solution.py:50
  69.7 15.2 %collective-permute-start.14 = (f32[128,128]{1,0:T(8,128)S(1)}, f32[128,128]{1,0:T(8,128)S(1)}, u32[]{:S(2)}, u32[]{:S(2)}) collective-permute-start(f32[128,128]{1,0:T(8,128)S(1)} %shard_map.47), channel_id=1, source_target_pairs={{0,1},{1,0},{2,3},{3,2},{4,5},{5,4},{6,7},{7,6},{8,9},{9,8},{10,11... | collective-permute-start | bytes 196616 | tf_op jit(solution)/shard_map/ppermute | solution.py:50
  85.0 6.9 %collective-permute-start.15 = (f32[128,128]{1,0:T(8,128)S(1)}, f32[128,128]{1,0:T(8,128)S(1)}, u32[]{:S(2)}, u32[]{:S(2)}) collective-permute-start(f32[128,128]{1,0:T(8,128)S(1)} %add.7.refs_0_), channel_id=1, source_target_pairs={{0,2},{1,3},{2,0},{3,1},{4,6},{5,7},{6,4},{7,5},{8,10},{9,11},{10,... | collective-permute-start | bytes 196616 | tf_op jit(solution)/shard_map/ppermute | solution.py:50

commit v2 on v1

--- a/solution.py
+++ b/solution.py
@@ -109,6 +109,16 @@
     return angles, rotation, first, second
 
 
+def rotate(first, second, angles, offs):
+    held = 0
+    for r in range(ROUNDS):
+        c, s = angles[r]
+        second = pltpu.roll(second, (held - offs[r]) & (B - 1), 1)
+        held = offs[r]
+        first, second = c * first + s * second, c * second - s * first
+    return first, pltpu.roll(second, held, 1)
+
+
 def rotate_back(first, second, angles, offs):
     held = 0
     for r in reversed(range(ROUNDS)):
@@ -196,32 +206,72 @@
     )(u, w)
 
 
+def joined_gram_kernel(place_ref, u_ref, w_ref, x_ref, gram_ref):
+    rows = x_ref.shape[0]
+    u, w = u_ref[:rows, :], w_ref[:rows, :]
+    odd = (place_ref[0] & 1) == 1
+
+    @pl.when(odd)
+    def _():
+        x_ref[:, :B] = u
+        x_ref[:, B:] = w
+
+    @pl.when(jnp.logical_not(odd))
+    def _():
+        x_ref[:, :B] = w
+        x_ref[:, B:] = u
+
+    gram_ref[...] = transposed_dot(u, w)
+
+
+def joined_gram(rows, place, u, w):
+    return pl.pallas_call(
+        joined_gram_kernel,
+        out_shape=(
+            jax.ShapeDtypeStruct((rows, 2 * B), jnp.float32),
+            jax.ShapeDtypeStruct((B, B), jnp.float32),
+        ),
+        in_specs=[SMEM, VMEM, VMEM],
+        out_specs=(VMEM, VMEM),
+        compiler_params=PARAMS,
+    )(place, u, w)
+
+
+def write_messages(near_ref, far_ref, near_base, far_base, slot, first, second, angles, past):
+    swap = jnp.logical_and((slot & 1) == 0, slot != 0)
+    near_ref[near_base : near_base + B, :] = jnp.where(swap, first, second)
+    far_ref[far_base : far_base + B, :] = jnp.where(swap, second, first)
+    for ref, at in ((near_ref, near_base + B), (far_ref, far_base + B)):
+        write_record(ref, at, angles)
+        at += RECORD
+        for history in past:
+            ref[at : at + history.shape[0], :] = history
+            at += history.shape[0]
+
+
+def write_blocks(near_ref, far_ref, rows, slot, x):
+    swap = jnp.logical_and((slot & 1) == 0, slot != 0)
+
+    @pl.when(swap)
+    def _():
+        near_ref[:rows, :] = x[:, :B]
+        far_ref[:rows, :] = x[:, B:]
+
+    @pl.when(jnp.logical_not(swap))
+    def _():
+        far_ref[:rows, :] = x[:, :B]
+        near_ref[:rows, :] = x[:, B:]
+
+
 def first_kernel(count, offs_ref, place_ref, *refs):
-    parts, (x_ref, in_ref, out_ref) = refs[:count], refs[count:]
+    parts, (x_ref, near_ref, far_ref) = refs[:count], refs[count:]
     rows = x_ref.shape[0]
+    gram = tree_sum([p[...] for p in parts])
     offs = step_offsets(offs_ref, 0)
-    gram = tree_sum([p[...] for p in parts])
     angles, rotation, first, second = solve(gram[:B], gram[B : 2 * B], gram[2 * B :], offs)
     slot = place_ref[0]
-    swap = jnp.logical_and((slot & 1) == 0, slot != 0)
-
-    def finish(first_ref, second_ref):
-        first_ref[rows : rows + B, :] = first
-        second_ref[rows : rows + B, :] = second
-        write_record(first_ref, rows + B, angles)
-        write_record(second_ref, rows + B, angles)
-
-        x = product(x_ref[...], rotation)
-        first_ref[:rows, :] = x[:, :B]
-        second_ref[:rows, :] = x[:, B:]
-
-    @pl.when(swap)
-    def _():
-        finish(in_ref, out_ref)
-
-    @pl.when(jnp.logical_not(swap))
-    def _():
-        finish(out_ref, in_ref)
+    write_messages(near_ref, far_ref, rows, rows, slot, first, second, angles, ())
+    write_blocks(near_ref, far_ref, rows, slot, product(x_ref[...], rotation))
 
 
 def first_step(offsets, place, parts, x):
@@ -235,57 +285,88 @@
     )(offsets, place, *parts, x)
 
 
-def cross_solve(rows, parts, odd, u_ref, w_ref, offs):
+def half_rotation(angles, offs, take_first):
+    halves = [rotate(top, low, angles, offs) for top, low in identity_halves()]
+    return jnp.concatenate([jnp.where(take_first, top, low) for top, low in halves], axis=0)
+
+
+def arrive_kernel(step, offs_ref, place_ref, u_ref, w_ref, xw_ref, x_ref, gram_ref):
+    rows = xw_ref.shape[0]
+    slot, pairs = place_ref[0], place_ref[1]
+    odd = (slot & 1) == 1
+    takes_first = jnp.logical_or(jnp.logical_not(odd), slot == pairs - 1)
+    angles = read_record(w_ref[B : B + RECORD, :])
+    w = product(xw_ref[...], half_rotation(angles, step_offsets(offs_ref, step), takes_first))
+    u = u_ref[:rows, :]
+
+    @pl.when(odd)
+    def _():
+        x_ref[:, :B] = u
+        x_ref[:, B:] = w
+
+    @pl.when(jnp.logical_not(odd))
+    def _():
+        x_ref[:, :B] = w
+        x_ref[:, B:] = u
+
+    gram_ref[...] = transposed_dot(u, w)
+
+
+def arrive(step, offsets, place, u, w, xw):
+    return pl.pallas_call(
+        functools.partial(arrive_kernel, step),
+        out_shape=(
+            jax.ShapeDtypeStruct(xw.shape, jnp.float32),
+            jax.ShapeDtypeStruct((B, B), jnp.float32),
+        ),
+        in_specs=[SMEM, SMEM] + [VMEM] * 3,
+        out_specs=(VMEM, VMEM),
+        compiler_params=PARAMS,
+    )(offsets, place, u, w, xw)
+
+
+def cross_solve(u_base, w_base, parts, odd, u_ref, w_ref, offs):
     gram = tree_sum([p[...] for p in parts])
     across = jnp.where(odd, gram, gram.T)
-    gu, gw = u_ref[rows : rows + B, :], w_ref[rows : rows + B, :]
+    gu, gw = u_ref[u_base : u_base + B, :], w_ref[w_base : w_base + B, :]
     return solve(jnp.where(odd, gu, gw), across, jnp.where(odd, gw, gu), offs)
 
 
-def middle_kernel(step, rows, count, offs_ref, place_ref, *refs):
-    parts, (u_ref, w_ref, in_ref, out_ref) = refs[:count], refs[count:]
-    offs = step_offsets(offs_ref, step)
+def older(odd, u_base, w_base, u_ref, w_ref):
+    hu, hw = u_ref[u_base + B :, :], w_ref[w_base + B :, :]
+    return jnp.where(odd, hu, hw), jnp.where(odd, hw, hu)
+
+
+def middle_kernel(step, bases, sent, count, offs_ref, place_ref, *refs):
+    parts, (u_ref, w_ref, x_ref, near_ref, far_ref) = refs[:count], refs[count:]
+    rows = x_ref.shape[0]
     slot = place_ref[0]
     odd = (slot & 1) == 1
-    angles, rotation, first, second = cross_solve(rows, parts, odd, u_ref, w_ref, offs)
-    past = u_ref.shape[0] - rows - B
-    base = rows + B
-
-    def finish(top_ref, low_ref, first_ref, second_ref):
-        first_ref[rows : rows + B, :] = first
-        second_ref[rows : rows + B, :] = second
-        for ref in (first_ref, second_ref):
-            write_record(ref, base, angles)
-            ref[base + RECORD : base + RECORD + past, :] = top_ref[base : base + past, :]
-            ref[base + RECORD + past : base + RECORD + 2 * past, :] = low_ref[base : base + past, :]
-
-        x = product(jnp.concatenate([top_ref[:rows, :], low_ref[:rows, :]], axis=1), rotation)
-        first_ref[:rows, :] = x[:, :B]
-        second_ref[:rows, :] = x[:, B:]
-
-    @pl.when(odd)
-    def _():
-        finish(u_ref, w_ref, out_ref, in_ref)
-
-    @pl.when(jnp.logical_and(jnp.logical_not(odd), slot != 0))
-    def _():
-        finish(w_ref, u_ref, in_ref, out_ref)
-
-    @pl.when(slot == 0)
-    def _():
-        finish(w_ref, u_ref, out_ref, in_ref)
-
-
-def middle_step(step, rows, offsets, place, parts, u, w):
-    past = u.shape[0] - rows - B
-    message = jax.ShapeDtypeStruct((rows + B + RECORD + 2 * past, B), jnp.float32)
-    return pl.pallas_call(
-        functools.partial(middle_kernel, step, rows, len(parts)),
-        out_shape=(message, message),
-        in_specs=[SMEM, SMEM] + [VMEM] * (len(parts) + 2),
+    offs = step_offsets(offs_ref, step)
+    angles, rotation, first, second = cross_solve(*bases, parts, odd, u_ref, w_ref, offs)
+    past = older(odd, *bases, u_ref, w_ref)
+    far_base = 0 if sent else rows
+    write_messages(near_ref, far_ref, rows, far_base, slot, first, second, angles, past)
+    if not sent:
+        write_blocks(near_ref, far_ref, rows, slot, product(x_ref[...], rotation))
+        return
+    takes_first = jnp.logical_and(jnp.logical_not(odd), slot != 0)
+    half = jnp.where(takes_first, rotation[:, :B], rotation[:, B:])
+    near_ref[:rows, :] = product(x_ref[...], half)
+
+
+def middle_step(step, bases, sent, offsets, place, parts, u, w, x):
+    rows = x.shape[0]
+    small = B + RECORD + 2 * (u.shape[0] - bases[0] - B)
+    near = jax.ShapeDtypeStruct((rows + small, B), jnp.float32)
+    far = jax.ShapeDtypeStruct((small, B), jnp.float32) if sent else near
+    return pl.pallas_call(
+        functools.partial(middle_kernel, step, bases, sent, len(parts)),
+        out_shape=(near, far),
+        in_specs=[SMEM, SMEM] + [VMEM] * (len(parts) + 3),
         out_specs=(VMEM, VMEM),
         compiler_params=PARAMS,
-    )(offsets, place, *parts, u, w)
+    )(offsets, place, *parts, u, w, x)
 
 
 def came_from(slot, is_first, pairs):
@@ -299,42 +380,39 @@
     slot, pairs, part = place_ref[0], place_ref[1], place_ref[2]
     odd = (slot & 1) == 1
     held_slots = out_ref.shape[0] // (2 * B)
-    base = rows + B
-    past = u_ref.shape[0] - base
-    out_ref[...] = jnp.zeros_like(out_ref)
     unit = jnp.where(eye_mask(), 1.0, 0.0)
-
-    def descend(block, node, was_first, step, history, columns):
-        zero = jnp.zeros_like(block)
-
-        def turned():
-            return rotate_back(
+    zero = jnp.zeros_like(unit)
+    pasts = older(odd, rows, rows, u_ref, w_ref)
+    nodes = [
+        (unit, *came_from(slot, is_first, pairs), past, at)
+        for is_first, past, at in ((True, pasts[0], 0), (False, pasts[1], B))
+    ]
+    for step in reversed(range(STEPS - 1)):
+        offs = step_offsets(offs_ref, step)
+        below = []
+        for block, node, was_first, past, at in nodes:
+            top, low = rotate_back(
                 jnp.where(was_first, block, zero),
                 jnp.where(was_first, zero, block),
-                read_record(history[:RECORD]),
-                step_offsets(offs_ref, step),
+                read_record(past[:RECORD]),
+                offs,
             )
-
-        if step == 0:
-
-            @pl.when(node // held_slots == part)
-            def _():
-                at = pl.multiple_of((node - part * held_slots) * (2 * B), 2 * B)
-                top, low = turned()
-                out_ref[pl.ds(at, B), columns] += top.T
-                out_ref[pl.ds(at + B, B), columns] += low.T
-
-            return
-        top, low = turned()
-        half = (history.shape[0] - RECORD) // 2
-        older = (history[RECORD : RECORD + half], history[RECORD + half :])
-        descend(top, *came_from(node, True, pairs), step - 1, older[0], columns)
-        descend(low, *came_from(node, False, pairs), step - 1, older[1], columns)
-
-    hu, hw = u_ref[base : base + past, :], w_ref[base : base + past, :]
-    top_history, low_history = jnp.where(odd, hu, hw), jnp.where(odd, hw, hu)
-    descend(unit, *came_from(slot, True, pairs), STEPS - 2, top_history, slice(0, B))
-    descend(unit, *came_from(slot, False, pairs), STEPS - 2, low_history, slice(B, 2 * B))
+            if step == 0:
+                below.append((top, low, node, at))
+                continue
+            half = (past.shape[0] - RECORD) // 2
+            top_past, low_past = past[RECORD : RECORD + half], past[RECORD + half :]
+            below.append((top, *came_from(node, True, pairs), top_past, at))
+            below.append((low, *came_from(node, False, pairs), low_past, at))
+        nodes = below
+    out_ref[...] = jnp.zeros_like(out_ref)
+    for top, low, node, column in nodes:
+
+        @pl.when(node // held_slots == part)
+        def _():
+            at = pl.multiple_of((node - part * held_slots) * (2 * B), 2 * B)
+            out_ref[pl.ds(at, B), column : column + B] += top.T
+            out_ref[pl.ds(at + B, B), column : column + B] += low.T
 
 
 def vectors_before_last(rows, height, offsets, place, u, w):
@@ -351,7 +429,7 @@
     parts, (u_ref, w_ref, v_ref, x_out, v_out) = refs[:count], refs[count:]
     offs = step_offsets(offs_ref, STEPS - 1)
     odd = (place_ref[0] & 1) == 1
-    _, rotation, _, _ = cross_solve(rows, parts, odd, u_ref, w_ref, offs)
+    _, rotation, _, _ = cross_solve(rows, rows, parts, odd, u_ref, w_ref, offs)
 
     @pl.when(odd)
     def _():
@@ -404,17 +482,20 @@
 
     terms = in_stages(whole_gram(whitened), given)
     near, far = first_step(offsets, place[given], terms, whitened)
-    before = given
-    for step in range(1, STEPS):
-        layout = given if step == STEPS - 1 else crossed
-        u = send(near, before, layout, inner)
-        w = send(far, before, layout, outer)
-        cross = cross_gram(rows, u, w)
-        if step < STEPS - 1:
-            terms = at_once(cross, layout)
-            near, far = middle_step(step, rows, offsets, place[layout], terms, u, w)
-        before = layout
-    terms = in_stages(cross, given)
+    u = send(near, given, crossed, inner)
+    w = send(far, given, crossed, outer)
+    x, cross = joined_gram(rows, place[crossed], u, w)
+    ahead = send(x, crossed, crossed, outer)
+    terms = at_once(cross, crossed)
+    near, far = middle_step(1, (rows, rows), True, offsets, place[crossed], terms, u, w, x)
+    u = send(near, crossed, crossed, inner)
+    w = send(far, crossed, crossed, outer)
+    x, cross = arrive(1, offsets, place[crossed], u, w, ahead)
+    terms = at_once(cross, crossed)
+    near, far = middle_step(2, (rows, 0), False, offsets, place[crossed], terms, u, w, x)
+    u = send(near, crossed, given, inner)
+    w = send(far, crossed, given, outer)
+    terms = in_stages(cross_gram(rows, u, w), given)
     vectors = vectors_before_last(rows, height, offsets, place[given], u, w)
     return last_step(rows, offsets, place[given], terms, u, w, vectors)
 

time: 95.8 us -> 92.7 us (0.968)
  the two profiles are of different devices: /device:TPU:0 before, /device:TPU:20 now
where the time goes in v2:
time: 92.7 us; the launch traced here: 92.5 us
  waiting for transfers between devices  48.5 us (52%)
  starting transfers between devices  22.2 us (24%)
  Pallas kernels  19.6 us (21%)
  local copies, waits for them, and re-layouts  1.23 us (1%)
    ppermute x17, waiting for transfers between devices, send(): return lax.ppermute(x, AXES, route(source, target, change))  48.5 us
    ppermute x17, starting transfers between devices, send(): return lax.ppermute(x, AXES, route(source, target, change))  22.2 us
    pallas_call x2, Pallas kernels, middle_step(): pl.pallas_call(functools.partial(middle_kernel, step, bases, sent, len(pa...  4.96 us
    pallas_call x1, Pallas kernels, last_step(): pl.pallas_call(functools.partial(last_kernel, rows, len(parts)), out_shap...  3.75 us
    pallas_call x1, Pallas kernels, arrive(): pl.pallas_call(functools.partial(arrive_kernel, step), out_shape=(jax.Sha...  2.97 us
    pallas_call x1, Pallas kernels, first_step(): pl.pallas_call(functools.partial(first_kernel, len(parts)), out_shape=(me...  2.44 us
    pallas_call x1, Pallas kernels, vectors_before_last(): pl.pallas_call(functools.partial(vectors_kernel, rows), out_shape=jax.Sha...  2.34 us
  transfers between devices with their start and end apart: 17, of which 14 were waited for; matrix products, arithmetic and copies ran while one was open for 0% of the time, Pallas kernels for 5%

profile of v2, /device:TPU:20, one launch (start us, length us, event | category | flops | bytes accessed | tf_op | source)
XLA Modules:
  0.0 92.5 jit_solution(116036467572151322)
XLA Ops:
  0.6 0.0 copy-start
  0.6 1.2 %copy-done = f32[1024,256]{1,0:T(8,128)S(1)} copy-done((f32[1024,256]{1,0:T(8,128)S(1)}, f32[1024,256]{1,0:T(8,128)}, u32[]{:S(2)}) %copy-start) | copy-done | bytes 1048600
  1.9 1.2 %shard_map.41 = f32[384,128]{1,0:T(8,128)S(1)} custom-call(f32[1024,256]{1,0:T(8,128)S(1)} %copy-done), custom_call_target="tpu_custom_call" | custom-call | tf_op jit(solution)/shard_map/pallas_call | solution.py:186
  3.0 0.1 collective-permute-start
  3.1 1.4 %collective-permute-done = f32[384,128]{1,0:T(8,128)S(1)} collective-permute-done((f32[384,128]{1,0:T(8,128)S(1)}, f32[384,128]{1,0:T(8,128)S(1)}, u32[]{:S(2)}, u32[]{:S(2)}) %collective-permute-start) | collective-permute-done | bytes 196640 | tf_op jit(solution)/shard_map/ppermute | solution.py:50
  4.6 1.6 %collective-permute-start.1 = (f32[384,128]{1,0:T(8,128)S(1)}, f32[384,128]{1,0:T(8,128)S(1)}, u32[]{:S(2)}, u32[]{:S(2)}) collective-permute-start(f32[384,128]{1,0:T(8,128)S(1)} %add.6.refs_0_), channel_id=1, source_target_pairs={{0,2},{1,3},{2,0},{3,1},{4,6},{5,7},{6,4},{7,5},{8,10},{9,11},{10,... | collective-permute-start | bytes 589832 | tf_op jit(solution)/shard_map/ppermute | solution.py:50
  6.1 0.1 fusion.place_ref
  6.2 5.4 %collective-permute-done.1.refs_1_ = f32[384,128]{1,0:T(8,128)S(1)} collective-permute-done((f32[384,128]{1,0:T(8,128)S(1)}, f32[384,128]{1,0:T(8,128)S(1)}, u32[]{:S(2)}, u32[]{:S(2)}) %collective-permute-start.1) | collective-permute-done | bytes 196640 | tf_op jit(solution)/shard_map/ppermute | solution.py:50
  11.6 0.0 copy-done.1
  11.6 2.4 %shard_map.42 = (f32[1160,128]{1,0:T(8,128)S(1)}, f32[1160,128]{1,0:T(8,128)S(1)}) custom-call(s32[4,4]{1,0:T(4,128)S(1)} %copy-done.2, s32[3]{0:T(128)S(1)} %fusion.place_ref, f32[384,128]{1,0:T(8,128)S(1)} %add.6.refs_0_, f32[384,128]{1,0:T(8,128)S(1)} %collective-permute-done.1.refs_1_, f32[1024,256]{1,0:T(8,128)S(1)} %copy-done.1), custom_call_target="tpu_custom_call" | custom-call | tf_op jit(solution)/shard_map/pallas_call | solution.py:279
  14.0 0.5 collective-permute-start.2
  14.6 2.9 %collective-permute-start.3 = (f32[1160,128]{1,0:T(8,128)S(1)}, f32[1160,128]{1,0:T(8,128)S(1)}, u32[]{:S(2)}, u32[]{:S(2)}) collective-permute-start(f32[1160,128]{1,0:T(8,128)S(1)} %get-tuple-element.13), channel_id=1, source_target_pairs={{0,0},{1,4},{2,2},{3,6},{4,8},{5,12},{6,10},{7,14},{8,1},{9,5},{10... | collective-permute-start | bytes 1781768 | tf_op jit(solution)/shard_map/ppermute | solution.py:50
  17.5 0.1 fusion.1.place_ref
  17.6 7.8 %collective-permute-done.2.u_ref.refs_4_ = f32[1160,128]{1,0:T(8,128)S(1)} collective-permute-done((f32[1160,128]{1,0:T(8,128)S(1)}, f32[1160,128]{1,0:T(8,128)S(1)}, u32[]{:S(2)}, u32[]{:S(2)}) %collective-permute-start.2) | collective-permute-done | bytes 593952 | tf_op jit(solution)/shard_map/ppermute | solution.py:50
  25.4 6.7 %collective-permute-done.3.w_ref.refs_5_ = f32[1160,128]{1,0:T(8,128)S(1)} collective-permute-done((f32[1160,128]{1,0:T(8,128)S(1)}, f32[1160,128]{1,0:T(8,128)S(1)}, u32[]{:S(2)}, u32[]{:S(2)}) %collective-permute-start.3) | collective-permute-done | bytes 593952 | tf_op jit(solution)/shard_map/ppermute | solution.py:50
  32.1 1.3 %shard_map.43 = (f32[1024,256]{1,0:T(8,128)S(1)}, f32[128,128]{1,0:T(8,128)S(1)}) custom-call(s32[3]{0:T(128)S(1)} %fusion.1.place_ref, f32[1160,128]{1,0:T(8,128)S(1)} %collective-permute-done.2.u_ref.refs_4_, f32[1160,128]{1,0:T(8,128)S(1)} %collective-permute-done.3.w_ref.refs_5_), custom_call_target="tpu_custom_call" | custom-call | tf_op jit(solution)/shard_map/pallas_call | solution.py:228
  33.4 2.0 %collective-permute-start.9 = (f32[1024,256]{1,0:T(8,128)S(1)}, f32[1024,256]{1,0:T(8,128)S(1)}, u32[]{:S(2)}, u32[]{:S(2)}) collective-permute-start(f32[1024,256]{1,0:T(8,128)S(1)} %get-tuple-element.15.refs_6_), channel_id=1, source_target_pairs={{0,0},{4,4},{2,2},{6,6},{1,8},{5,12},{3,10},{7,14},{8,1},{12,5},{1... | collective-permute-start | bytes 3145736 | tf_op jit(solution)/shard_map/ppermute | solution.py:50
  35.4 2.4 %collective-permute-start.6 = (f32[128,128]{1,0:T(8,128)S(1)}, f32[128,128]{1,0:T(8,128)S(1)}, u32[]{:S(2)}, u32[]{:S(2)}) collective-permute-start(f32[128,128]{1,0:T(8,128)S(1)} %get-tuple-element.14.refs_0_), channel_id=1, source_target_pairs={{0,6},{4,2},{2,4},{6,0},{1,7},{5,3},{3,5},{7,1},{8,14},{12,10},{10... | collective-permute-start | bytes 196616 | tf_op jit(solution)/shard_map/ppermute | solution.py:50
  37.9 0.5 collective-permute-start.5
  38.4 0.6 collective-permute-start.4
  39.0 1.7 %collective-permute-done.6.refs_3_ = f32[128,128]{1,0:T(8,128)S(1)} collective-permute-done((f32[128,128]{1,0:T(8,128)S(1)}, f32[128,128]{1,0:T(8,128)S(1)}, u32[]{:S(2)}, u32[]{:S(2)}) %collective-permute-start.6) | collective-permute-done | bytes 65568 | tf_op jit(solution)/shard_map/ppermute | solution.py:50
  40.7 1.6 %collective-permute-done.5.refs_2_ = f32[128,128]{1,0:T(8,128)S(1)} collective-permute-done((f32[128,128]{1,0:T(8,128)S(1)}, f32[128,128]{1,0:T(8,128)S(1)}, u32[]{:S(2)}, u32[]{:S(2)}) %collective-permute-start.5) | collective-permute-done | bytes 65568 | tf_op jit(solution)/shard_map/ppermute | solution.py:50
  42.2 0.4 collective-permute-done.4.refs_1_
  42.7 2.5 %shard_map.44 = (f32[1176,128]{1,0:T(8,128)S(1)}, f32[152,128]{1,0:T(8,128)S(1)}) custom-call(s32[4,4]{1,0:T(4,128)S(1)} %copy-done.2, s32[3]{0:T(128)S(1)} %fusion.1.place_ref, f32[128,128]{1,0:T(8,128)S(1)} %get-tuple-element.14.refs_0_, f32[128,128]{1,0:T(8,128)S(1)} %collective-permute-done.4.refs_1_, f32[128,128]{1,0:T(8,128)S(1)} %collective-permute-done.5.refs_2_, ...), custom_call_target="tpu_custom_call" | custom-call | tf_op jit(solution)/shard_map/pallas_call | solution.py:363
  45.1 2.1 %collective-permute-start.7 = (f32[1176,128]{1,0:T(8,128)S(1)}, f32[1176,128]{1,0:T(8,128)S(1)}, u32[]{:S(2)}, u32[]{:S(2)}) collective-permute-start(f32[1176,128]{1,0:T(8,128)S(1)} %get-tuple-element.16), channel_id=1, source_target_pairs={{0,1},{4,5},{2,3},{6,7},{1,0},{5,4},{3,2},{7,6},{8,9},{12,13},{10,... | collective-permute-start | bytes 1806344 | tf_op jit(solution)/shard_map/ppermute | solution.py:50
  47.3 1.9 %collective-permute-start.8 = (f32[152,128]{1,0:T(8,128)S(1)}, f32[152,128]{1,0:T(8,128)S(1)}, u32[]{:S(2)}, u32[]{:S(2)}) collective-permute-start(f32[152,128]{1,0:T(8,128)S(1)} %get-tuple-element.17), channel_id=1, source_target_pairs={{0,0},{4,4},{2,2},{6,6},{1,8},{5,12},{3,10},{7,14},{8,1},{12,5},{1... | collective-permute-start | bytes 233480 | tf_op jit(solution)/shard_map/ppermute | solution.py:50
  49.2 3.8 %collective-permute-done.8.w_ref.refs_5_ = f32[152,128]{1,0:T(8,128)S(1)} collective-permute-done((f32[152,128]{1,0:T(8,128)S(1)}, f32[152,128]{1,0:T(8,128)S(1)}, u32[]{:S(2)}, u32[]{:S(2)}) %collective-permute-start.8) | collective-permute-done | bytes 77856 | tf_op jit(solution)/shard_map/ppermute | solution.py:50
  53.0 0.0 collective-permute-done.7.u_ref.refs_4_
  53.0 0.0 collective-permute-done.9.xw_ref
  53.0 3.0 %shard_map.45 = (f32[1024,256]{1,0:T(8,128)S(1)}, f32[128,128]{1,0:T(8,128)S(1)}) custom-call(s32[4,4]{1,0:T(4,128)S(1)} %copy-done.2, s32[3]{0:T(128)S(1)} %fusion.1.place_ref, f32[1176,128]{1,0:T(8,128)S(1)} %collective-permute-done.7.u_ref.refs_4_, f32[152,128]{1,0:T(8,128)S(1)} %collective-permute-done.8.w_ref.refs_5_, ...), custom_call_target="tpu_custom_call" | custom-call | tf_op jit(solution)/shard_map/pallas_call | solution.py:316
  56.0 2.3 %collective-permute-start.12 = (f32[128,128]{1,0:T(8,128)S(1)}, f32[128,128]{1,0:T(8,128)S(1)}, u32[]{:S(2)}, u32[]{:S(2)}) collective-permute-start(f32[128,128]{1,0:T(8,128)S(1)} %get-tuple-element.18.refs_0_), channel_id=1, source_target_pairs={{0,6},{4,2},{2,4},{6,0},{1,7},{5,3},{3,5},{7,1},{8,14},{12,10},{10... | collective-permute-start | bytes 196616 | tf_op jit(solution)/shard_map/ppermute | solution.py:50
  58.3 0.5 collective-permute-start.11
  58.8 0.7 collective-permute-start.10
  59.5 2.1 %collective-permute-done.12.refs_3_ = f32[128,128]{1,0:T(8,128)S(1)} collective-permute-done((f32[128,128]{1,0:T(8,128)S(1)}, f32[128,128]{1,0:T(8,128)S(1)}, u32[]{:S(2)}, u32[]{:S(2)}) %collective-permute-start.12) | collective-permute-done | bytes 65568 | tf_op jit(solution)/shard_map/ppermute | solution.py:50
  61.6 1.0 %collective-permute-done.11.refs_2_ = f32[128,128]{1,0:T(8,128)S(1)} collective-permute-done((f32[128,128]{1,0:T(8,128)S(1)}, f32[128,128]{1,0:T(8,128)S(1)}, u32[]{:S(2)}, u32[]{:S(2)}) %collective-permute-start.11) | collective-permute-done | bytes 65568 | tf_op jit(solution)/shard_map/ppermute | solution.py:50
  62.5 0.5 collective-permute-done.10.refs_1_
  63.1 2.5 %shard_map.46 = (f32[1208,128]{1,0:T(8,128)S(1)}, f32[1208,128]{1,0:T(8,128)S(1)}) custom-call(s32[4,4]{1,0:T(4,128)S(1)} %copy-done.2, s32[3]{0:T(128)S(1)} %fusion.1.place_ref, f32[128,128]{1,0:T(8,128)S(1)} %get-tuple-element.18.refs_0_, f32[128,128]{1,0:T(8,128)S(1)} %collective-permute-done.10.refs_1_, f32[128,128]{1,0:T(8,128)S(1)} %collective-permute-done.11.refs_2_, ...), custom_call_target="tpu_custom_call" | custom-call | tf_op jit(solution)/shard_map/pallas_call | solution.py:363
  65.6 0.0 collective-permute-start.13
  65.6 2.3 %collective-permute-start.14 = (f32[1208,128]{1,0:T(8,128)S(1)}, f32[1208,128]{1,0:T(8,128)S(1)}, u32[]{:S(2)}, u32[]{:S(2)}) collective-permute-start(f32[1208,128]{1,0:T(8,128)S(1)} %get-tuple-element.21), channel_id=1, source_target_pairs={{0,0},{4,1},{2,2},{6,3},{1,8},{5,9},{3,10},{7,11},{8,4},{12,5},{10... | collective-permute-start | bytes 1855496 | tf_op jit(solution)/shard_map/ppermute | solution.py:50
  68.0 14.5 %collective-permute-done.13.u_ref.refs_2_ = f32[1208,128]{1,0:T(8,128)S(1)} collective-permute-done((f32[1208,128]{1,0:T(8,128)S(1)}, f32[1208,128]{1,0:T(8,128)S(1)}, u32[]{:S(2)}, u32[]{:S(2)}) %collective-permute-start.13) | collective-permute-done | bytes 618528 | tf_op jit(solution)/shard_map/ppermute | solution.py:50
  82.4 0.0 collective-permute-done.14.w_ref.refs_3_
  82.4 0.6 shard_map.47
  83.1 0.1 collective-permute-start.15
  83.1 1.2 %collective-permute-done.15 = f32[128,128]{1,0:T(8,128)S(1)} collective-permute-done((f32[128,128]{1,0:T(8,128)S(1)}, f32[128,128]{1,0:T(8,128)S(1)}, u32[]{:S(2)}, u32[]{:S(2)}) %collective-permute-start.15) | collective-permute-done | bytes 65568 | tf_op jit(solution)/shard_map/ppermute | solution.py:50
  84.4 1.5 %collective-permute-start.16 = (f32[128,128]{1,0:T(8,128)S(1)}, f32[128,128]{1,0:T(8,128)S(1)}, u32[]{:S(2)}, u32[]{:S(2)}) collective-permute-start(f32[128,128]{1,0:T(8,128)S(1)} %add.7.refs_0_), channel_id=1, source_target_pairs={{0,2},{1,3},{2,0},{3,1},{4,6},{5,7},{6,4},{7,5},{8,10},{9,11},{10,... | collective-permute-start | bytes 196616 | tf_op jit(solution)/shard_map/ppermute | solution.py:50
  85.9 2.3 %shard_map.48.refs_4_ = f32[512,256]{1,0:T(8,128)S(1)} custom-call(s32[4,4]{1,0:T(4,128)S(1)} %copy-done.2, s32[3]{0:T(128)S(1)} %fusion.place_ref, f32[1208,128]{1,0:T(8,128)S(1)} %collective-permute-done.13.u_ref.refs_2_, f32[1208,128]{1,0:T(8,128)S(1)} %collective-permute-done.14.w_ref.refs_3_), custom_call_target="tpu_custom_call" | custom-call | tf_op jit(solution)/shard_map/pallas_call | solution.py:419
  88.3 0.4 collective-permute-done.16.refs_1_
  88.7 3.8 %shard_map.49 = (f32[1024,256]{1,0:T(8,128)}, f32[512,256]{1,0:T(8,128)}) custom-call(s32[4,4]{1,0:T(4,128)S(1)} %copy-done.2, s32[3]{0:T(128)S(1)} %fusion.place_ref, f32[128,128]{1,0:T(8,128)S(1)} %add.7.refs_0_, f32[128,128]{1,0:T(8,128)S(1)} %collective-permute-done.16.refs_1_, f32[1208,128]{1,0:T(8,128)S(1)} %collective-permute-done.13.u_ref.refs_2_, ...), custom_call_target="tpu_custom_call" | custom-call | tf_op jit(solution)/shard_map/pallas_call | solution.py:446
  (5 shorter events, 0.0 us)
Async XLA Ops:
  0.6 1.2 %copy-start = (f32[1024,256]{1,0:T(8,128)S(1)}, f32[1024,256]{1,0:T(8,128)}, u32[]{:S(2)}) copy-start(f32[1024,256]{1,0:T(8,128)} %refs_2_.1) | copy-start | bytes 3145732
  1.9 9.7 %copy-start.1 = (f32[1024,256]{1,0:T(8,128)S(1)}, f32[1024,256]{1,0:T(8,128)}, u32[]{:S(2)}) copy-start(f32[1024,256]{1,0:T(8,128)} %refs_2_.1) | copy-start | bytes 3145732
  3.0 1.5 %collective-permute-start = (f32[384,128]{1,0:T(8,128)S(1)}, f32[384,128]{1,0:T(8,128)S(1)}, u32[]{:S(2)}, u32[]{:S(2)}) collective-permute-start(f32[384,128]{1,0:T(8,128)S(1)} %shard_map.41), channel_id=1, source_target_pairs={{0,1},{1,0},{2,3},{3,2},{4,5},{5,4},{6,7},{7,6},{8,9},{9,8},{10,11... | collective-permute-start | bytes 589832 | tf_op jit(solution)/shard_map/ppermute | solution.py:50
  4.6 7.0 %collective-permute-start.1 = (f32[384,128]{1,0:T(8,128)S(1)}, f32[384,128]{1,0:T(8,128)S(1)}, u32[]{:S(2)}, u32[]{:S(2)}) collective-permute-start(f32[384,128]{1,0:T(8,128)S(1)} %add.6.refs_0_), channel_id=1, source_target_pairs={{0,2},{1,3},{2,0},{3,1},{4,6},{5,7},{6,4},{7,5},{8,10},{9,11},{10,... | collective-permute-start | bytes 589832 | tf_op jit(solution)/shard_map/ppermute | solution.py:50
  6.1 5.5 %copy-start.2 = (s32[4,4]{1,0:T(4,128)S(1)}, s32[4,4]{1,0:T(4,128)}, u32[]{:S(2)}) copy-start(s32[4,4]{1,0:T(4,128)} %offs_ref.11) | copy-start | bytes 196
  14.0 11.4 %collective-permute-start.2 = (f32[1160,128]{1,0:T(8,128)S(1)}, f32[1160,128]{1,0:T(8,128)S(1)}, u32[]{:S(2)}, u32[]{:S(2)}) collective-permute-start(f32[1160,128]{1,0:T(8,128)S(1)} %get-tuple-element.12), channel_id=1, source_target_pairs={{0,1},{1,5},{2,3},{3,7},{4,0},{5,4},{6,2},{7,6},{8,9},{9,13},{10,1... | collective-permute-start | bytes 1781768 | tf_op jit(solution)/shard_map/ppermute | solution.py:50
  14.6 17.6 %collective-permute-start.3 = (f32[1160,128]{1,0:T(8,128)S(1)}, f32[1160,128]{1,0:T(8,128)S(1)}, u32[]{:S(2)}, u32[]{:S(2)}) collective-permute-start(f32[1160,128]{1,0:T(8,128)S(1)} %get-tuple-element.13), channel_id=1, source_target_pairs={{0,0},{1,4},{2,2},{3,6},{4,8},{5,12},{6,10},{7,14},{8,1},{9,5},{10... | collective-permute-start | bytes 1781768 | tf_op jit(solution)/shard_map/ppermute | solution.py:50
  33.4 19.5 %collective-permute-start.9 = (f32[1024,256]{1,0:T(8,128)S(1)}, f32[1024,256]{1,0:T(8,128)S(1)}, u32[]{:S(2)}, u32[]{:S(2)}) collective-permute-start(f32[1024,256]{1,0:T(8,128)S(1)} %get-tuple-element.15.refs_6_), channel_id=1, source_target_pairs={{0,0},{4,4},{2,2},{6,6},{1,8},{5,12},{3,10},{7,14},{8,1},{12,5},{1... | collective-permute-start | bytes 3145736 | tf_op jit(solution)/shard_map/ppermute | solution.py:50
  35.4 5.2 %collective-permute-start.6 = (f32[128,128]{1,0:T(8,128)S(1)}, f32[128,128]{1,0:T(8,128)S(1)}, u32[]{:S(2)}, u32[]{:S(2)}) collective-permute-start(f32[128,128]{1,0:T(8,128)S(1)} %get-tuple-element.14.refs_0_), channel_id=1, source_target_pairs={{0,6},{4,2},{2,4},{6,0},{1,7},{5,3},{3,5},{7,1},{8,14},{12,10},{10... | collective-permute-start | bytes 196616 | tf_op jit(solution)/shard_map/ppermute | solution.py:50
  37.9 4.4 %collective-permute-start.5 = (f32[128,128]{1,0:T(8,128)S(1)}, f32[128,128]{1,0:T(8,128)S(1)}, u32[]{:S(2)}, u32[]{:S(2)}) collective-permute-start(f32[128,128]{1,0:T(8,128)S(1)} %get-tuple-element.14.refs_0_), channel_id=1, source_target_pairs={{0,2},{4,6},{2,0},{6,4},{1,3},{5,7},{3,1},{7,5},{8,10},{12,14},{10... | collective-permute-start | bytes 196616 | tf_op jit(solution)/shard_map/ppermute | solution.py:50
  38.4 4.3 %collective-permute-start.4 = (f32[128,128]{1,0:T(8,128)S(1)}, f32[128,128]{1,0:T(8,128)S(1)}, u32[]{:S(2)}, u32[]{:S(2)}) collective-permute-start(f32[128,128]{1,0:T(8,128)S(1)} %get-tuple-element.14.refs_0_), channel_id=1, source_target_pairs={{0,4},{4,0},{2,6},{6,2},{1,5},{5,1},{3,7},{7,3},{8,12},{12,8},{10,... | collective-permute-start | bytes 196616 | tf_op jit(solution)/shard_map/ppermute | solution.py:50
  45.1 7.9 %collective-permute-start.7 = (f32[1176,128]{1,0:T(8,128)S(1)}, f32[1176,128]{1,0:T(8,128)S(1)}, u32[]{:S(2)}, u32[]{:S(2)}) collective-permute-start(f32[1176,128]{1,0:T(8,128)S(1)} %get-tuple-element.16), channel_id=1, source_target_pairs={{0,1},{4,5},{2,3},{6,7},{1,0},{5,4},{3,2},{7,6},{8,9},{12,13},{10,... | collective-permute-start | bytes 1806344 | tf_op jit(solution)/shard_map/ppermute | solution.py:50
  47.3 5.7 %collective-permute-start.8 = (f32[152,128]{1,0:T(8,128)S(1)}, f32[152,128]{1,0:T(8,128)S(1)}, u32[]{:S(2)}, u32[]{:S(2)}) collective-permute-start(f32[152,128]{1,0:T(8,128)S(1)} %get-tuple-element.17), channel_id=1, source_target_pairs={{0,0},{4,4},{2,2},{6,6},{1,8},{5,12},{3,10},{7,14},{8,1},{12,5},{1... | collective-permute-start | bytes 233480 | tf_op jit(solution)/shard_map/ppermute | solution.py:50
  56.0 5.6 %collective-permute-start.12 = (f32[128,128]{1,0:T(8,128)S(1)}, f32[128,128]{1,0:T(8,128)S(1)}, u32[]{:S(2)}, u32[]{:S(2)}) collective-permute-start(f32[128,128]{1,0:T(8,128)S(1)} %get-tuple-element.18.refs_0_), channel_id=1, source_target_pairs={{0,6},{4,2},{2,4},{6,0},{1,7},{5,3},{3,5},{7,1},{8,14},{12,10},{10... | collective-permute-start | bytes 196616 | tf_op jit(solution)/shard_map/ppermute | solution.py:50
  58.3 4.3 %collective-permute-start.11 = (f32[128,128]{1,0:T(8,128)S(1)}, f32[128,128]{1,0:T(8,128)S(1)}, u32[]{:S(2)}, u32[]{:S(2)}) collective-permute-start(f32[128,128]{1,0:T(8,128)S(1)} %get-tuple-element.18.refs_0_), channel_id=1, source_target_pairs={{0,2},{4,6},{2,0},{6,4},{1,3},{5,7},{3,1},{7,5},{8,10},{12,14},{10... | collective-permute-start | bytes 196616 | tf_op jit(solution)/shard_map/ppermute | solution.py:50
  58.8 4.3 %collective-permute-start.10 = (f32[128,128]{1,0:T(8,128)S(1)}, f32[128,128]{1,0:T(8,128)S(1)}, u32[]{:S(2)}, u32[]{:S(2)}) collective-permute-start(f32[128,128]{1,0:T(8,128)S(1)} %get-tuple-element.18.refs_0_), channel_id=1, source_target_pairs={{0,4},{4,0},{2,6},{6,2},{1,5},{5,1},{3,7},{7,3},{8,12},{12,8},{10,... | collective-permute-start | bytes 196616 | tf_op jit(solution)/shard_map/ppermute | solution.py:50
  65.6 16.8 %collective-permute-start.13 = (f32[1208,128]{1,0:T(8,128)S(1)}, f32[1208,128]{1,0:T(8,128)S(1)}, u32[]{:S(2)}, u32[]{:S(2)}) collective-permute-start(f32[1208,128]{1,0:T(8,128)S(1)} %get-tuple-element.20), channel_id=1, source_target_pairs={{0,4},{4,5},{2,6},{6,7},{1,0},{5,1},{3,2},{7,3},{8,12},{12,13},{10... | collective-permute-start | bytes 1855496 | tf_op jit(solution)/shard_map/ppermute | solution.py:50
  65.6 16.8 %collective-permute-start.14 = (f32[1208,128]{1,0:T(8,128)S(1)}, f32[1208,128]{1,0:T(8,128)S(1)}, u32[]{:S(2)}, u32[]{:S(2)}) collective-permute-start(f32[1208,128]{1,0:T(8,128)S(1)} %get-tuple-element.21), channel_id=1, source_target_pairs={{0,0},{4,1},{2,2},{6,3},{1,8},{5,9},{3,10},{7,11},{8,4},{12,5},{10... | collective-permute-start | bytes 1855496 | tf_op jit(solution)/shard_map/ppermute | solution.py:50
  83.1 1.3 %collective-permute-start.15 = (f32[128,128]{1,0:T(8,128)S(1)}, f32[128,128]{1,0:T(8,128)S(1)}, u32[]{:S(2)}, u32[]{:S(2)}) collective-permute-start(f32[128,128]{1,0:T(8,128)S(1)} %shard_map.47), channel_id=1, source_target_pairs={{0,1},{1,0},{2,3},{3,2},{4,5},{5,4},{6,7},{7,6},{8,9},{9,8},{10,11... | collective-permute-start | bytes 196616 | tf_op jit(solution)/shard_map/ppermute | solution.py:50
  84.4 4.3 %collective-permute-start.16 = (f32[128,128]{1,0:T(8,128)S(1)}, f32[128,128]{1,0:T(8,128)S(1)}, u32[]{:S(2)}, u32[]{:S(2)}) collective-permute-start(f32[128,128]{1,0:T(8,128)S(1)} %add.7.refs_0_), channel_id=1, source_target_pairs={{0,2},{1,3},{2,0},{3,1},{4,6},{5,7},{6,4},{7,5},{8,10},{9,11},{10,... | collective-permute-start | bytes 196616 | tf_op jit(solution)/shard_map/ppermute | solution.py:50

commit v3 on v2

v3 whole, which is shorter than its diff:
```python
import functools

import jax
import jax.numpy as jnp
from jax import lax
from jax.experimental import pallas as pl
from jax.experimental.pallas import tpu as pltpu
from jax.sharding import PartitionSpec as P

B = 128
ROUNDS = 4
STEPS = 4
RECORD = 2 * ROUNDS
HALF = B // 2
PACKED = HALF + 8
AXES = ("pair", "row")
PARAMS = pltpu.CompilerParams(vmem_limit_bytes=40 * 1024 * 1024)
VMEM = pl.BlockSpec(memory_space=pltpu.VMEM)


def given(slot, part):
    return slot, part


def crossed(slot, part):
    return (slot & ~1) | (part & 1), (part & ~1) | (slot & 1)


def route(source, target, change, swap=True):
    pairs, rows = lax.axis_size("pair"), lax.axis_size("row")
    line = []
    for slot in range(pairs):
        for part in range(rows):
            a = source(slot, part)
            b = target(*change(slot, part, pairs))
            if swap and a == b:
                b = a[0], a[1] ^ (rows // 2)
            line.append((a[0] * rows + a[1], b[0] * rows + b[1]))
    return line


def inner(slot, part, pairs):
    return slot ^ 1, part


def outer(slot, part, pairs):
    if slot == 0 or slot == pairs - 1:
        return slot, part
    return (slot + 1 if slot & 1 else slot - 1), part


def send(x, source, target, change, swap=True):
    return lax.ppermute(x, AXES, route(source, target, change, swap))


def other_part(distance):
    return lambda slot, part, pairs: (slot, part ^ distance)


def eye_mask():
    shape = (B, B)
    return lax.broadcasted_iota(jnp.int32, shape, 0) == lax.broadcasted_iota(jnp.int32, shape, 1)


def identity_halves():
    unit = jnp.where(eye_mask(), 1.0, 0.0)
    return [(unit, jnp.zeros_like(unit)), (jnp.zeros_like(unit), unit)]


def diagonal(mask, block):
    return jnp.sum(jnp.where(mask, block, 0.0), axis=0, keepdims=True)


def as_column(mask, row):
    return jnp.sum(jnp.where(mask, jnp.broadcast_to(row, (B, B)), 0.0), axis=1, keepdims=True)


def solve(first, across, second, offs):
    mask = eye_mask()
    angles = []
    turns = identity_halves()
    held = 0
    for r in range(ROUNDS):
        turn = (held - offs[r]) & (B - 1)
        held = offs[r]
        across = pltpu.roll(across, turn, 1)
        second = pltpu.roll(pltpu.roll(second, turn, 1), turn, 0)
        turns = [(top, pltpu.roll(low, turn, 1)) for top, low in turns]
        a = diagonal(mask, first)
        d = diagonal(mask, second)
        c0 = diagonal(mask, across)
        h = 0.5 * (d - a)
        radius = jnp.sqrt(h * h + c0 * c0)
        sg = jnp.where(h >= 0, 1.0, -1.0)
        t = -sg * c0 / (jnp.abs(h) + radius + 1e-06 * (a + d))
        c = 1.0 / jnp.sqrt(1.0 + t * t)
        s = t * c
        angles.append((c, s))
        cc, sc = as_column(mask, c), as_column(mask, s)
        below = across.T
        first1 = first * c + across * s
        across1 = across * c - first * s
        below1 = below * c + second * s
        second1 = second * c - below * s
        first = cc * first1 + sc * below1
        across = cc * across1 + sc * second1
        second = cc * second1 - sc * across1
        turns = [(c * top + s * low, c * low - s * top) for top, low in turns]
    second = pltpu.roll(pltpu.roll(second, held, 1), held, 0)
    turns = [(top, pltpu.roll(low, held, 1)) for top, low in turns]
    rotation = jnp.concatenate([jnp.concatenate(t, axis=1) for t in turns], axis=0)
    return angles, rotation, first, second


def rotate(first, second, angles, offs):
    held = 0
    for r in range(ROUNDS):
        c, s = angles[r]
        second = pltpu.roll(second, (held - offs[r]) & (B - 1), 1)
        held = offs[r]
        first, second = c * first + s * second, c * second - s * first
    return first, pltpu.roll(second, held, 1)


def rotate_back(first, second, angles, offs):
    held = 0
    for r in reversed(range(ROUNDS)):
        c, s = angles[r]
        second = pltpu.roll(second, (held - offs[r]) & (B - 1), 1)
        held = offs[r]
        first, second = c * first - s * second, s * first + c * second
    return first, pltpu.roll(second, held, 1)


def read_record(rows):
    return [(rows[r : r + 1], rows[ROUNDS + r : ROUNDS + r + 1]) for r in range(ROUNDS)]


def write_record(ref, at, angles):
    for r, (c, s) in enumerate(angles):
        ref[at + r : at + r + 1, :] = c
        ref[at + ROUNDS + r : at + ROUNDS + r + 1, :] = s


def index(shape, axis):
    return lax.broadcasted_iota(jnp.int32, shape, axis)


def pack(block):
    shape = (HALF, B)
    low = jnp.logical_and(index(shape, 1) < HALF, index(shape, 0) > index(shape, 1))
    rows = jnp.where(low, pltpu.roll(block[HALF:], HALF, 1), block[:HALF])
    return jnp.concatenate([rows, jnp.broadcast_to(diagonal(eye_mask(), block), (8, B))], axis=0)


def unpack(packed):
    rows, diag = packed[:HALF], packed[HALF : HALF + 1]
    turned = jnp.concatenate([rows, rows], axis=0).T
    shape = (HALF, B)
    i, j = index(shape, 0), index(shape, 1)
    left = j < HALF
    top = jnp.where(jnp.logical_and(left, i > j), turned[:HALF], rows)
    right = jnp.where(i > j - HALF, pltpu.roll(rows, HALF, 1), turned[:HALF])
    right = jnp.where(i == j - HALF, jnp.broadcast_to(diag, shape), right)
    return jnp.concatenate([top, jnp.where(left, turned[HALF:], right)], axis=0)


def pack_two(first, second):
    rows, cols = index((B, B), 0), index((B, B), 1)
    return [
        jnp.where(rows <= cols, first, second),
        jnp.broadcast_to(diagonal(eye_mask(), second), (8, B)),
    ]


def unpack_two(block, diag):
    rows, cols = index((B, B), 0), index((B, B), 1)
    turned = block.T
    second = jnp.where(rows > cols, block, turned)
    second = jnp.where(rows == cols, jnp.broadcast_to(diag, (B, B)), second)
    return jnp.where(rows <= cols, block, turned), second


def tree_sum(parts):
    parts = list(parts)
    while len(parts) > 1:
        parts = [parts[i] + parts[i + 1] for i in range(0, len(parts), 2)]
    return parts[0]


def split(x):
    high = x.astype(jnp.bfloat16)
    return high, (x - high.astype(jnp.float32)).astype(jnp.bfloat16)


def product(x, rotation):
    xh, xl = split(x)
    rh, rl = split(rotation)

    def dot(a, b):
        return jnp.dot(a, b, preferred_element_type=jnp.float32)

    return (dot(xl, rh) + dot(xh, rl)) + dot(xh, rh)


def step_offsets(offs_ref, step):
    return [offs_ref[step, r] for r in range(ROUNDS)]


def transposed_dot(left, right):
    return lax.dot_general(
        left,
        right,
        (((0,), (0,)), ((), ())),
        precision=lax.Precision.HIGHEST,
        preferred_element_type=jnp.float32,
    )


JOINED, RAW, EITHER = range(3)


def call(kernel, out_shapes, arrays):
    return pl.pallas_call(
        kernel,
        out_shape=tuple(jax.ShapeDtypeStruct(shape, jnp.float32) for shape in out_shapes),
        in_specs=[VMEM] * len(arrays),
        out_specs=tuple(VMEM for _ in out_shapes),
        compiler_params=PARAMS,
    )(*arrays)


class Place:
    def __init__(self, layout):
        pair, row = lax.axis_index("pair"), lax.axis_index("row")
        self.pairs = lax.axis_size("pair")
        self.slot, self.part = layout(pair, row)
        self.odd = (self.slot & 1) == 1
        self.edge = jnp.logical_or(self.slot == 0, self.slot == self.pairs - 1)
        self.stays = jnp.logical_and(self.edge, ((pair ^ row) & 1) == 0)


def whole_gram_kernel(x_ref, out_ref):
    gram = transposed_dot(x_ref[...], x_ref[...])
    packed, diag = pack_two(gram[:B, :B], gram[B:, B:])
    out_ref[:B, :] = gram[:B, B:]
    out_ref[B : 2 * B, :] = packed
    out_ref[2 * B :, :] = diag


def whole_gram(x):
    return call(whole_gram_kernel, [(2 * B + 8, B)], (x,))[0]


def base_of(way, rows):
    return rows if way == JOINED else 0


def older(odd, mu, mw):
    hu, hw = mu[PACKED:], mw[PACKED:]
    return jnp.where(odd, hu, hw), jnp.where(odd, hw, hu)


def cross_solve(across, odd, mu, mw, offs):
    gu, gw = unpack(mu[:PACKED]), unpack(mw[:PACKED])
    return solve(jnp.where(odd, gu, gw), across, jnp.where(odd, gw, gu), offs)


def turn_kernel(step, goes, layout, count, offs_ref, *refs):
    parts, refs = refs[:count], list(refs[count:])
    place = Place(layout)
    odd = place.odd
    offs = step_offsets(offs_ref, step)
    if step == 0:
        gram = tree_sum([p[...] for p in parts])
        first, second = unpack_two(gram[B : 2 * B], gram[2 * B : 2 * B + 1])
        angles, rotation, first, second = solve(first, gram[:B], second, offs)
        past = ()
    else:
        mu, mw = refs.pop(0)[...], refs.pop(0)[...]
        across = tree_sum([p[...] for p in parts])
        angles, rotation, first, second = cross_solve(across, odd, mu, mw, offs)
        past = older(odd, mu, mw)
    x_ref = refs.pop(0)
    rows = x_ref.shape[0]
    swap = jnp.logical_and(jnp.logical_not(odd), place.slot != 0)
    blocks = []
    for way, near in zip(goes, (True, False)):
        message = refs.pop(0)
        base = base_of(way, rows)
        gives_first = swap if near else jnp.logical_not(swap)
        message[base : base + PACKED, :] = pack(jnp.where(gives_first, first, second))
        at = base + PACKED
        write_record(message, at, angles)
        at += RECORD
        for history in past:
            message[at : at + history.shape[0], :] = history
            at += history.shape[0]
        if way != RAW:
            blocks.append((message if way == JOINED else refs.pop(0), gives_first))
    if len(blocks) == 1:
        (block_ref, gives_first), = blocks
        half = jnp.where(gives_first, rotation[:, :B], rotation[:, B:])
        block_ref[:rows, :] = product(x_ref[...], half)
        return
    x = product(x_ref[...], rotation)
    for block_ref, gives_first in blocks:

        @pl.when(gives_first)
        def _():
            block_ref[:rows, :] = x[:, :B]

        @pl.when(jnp.logical_not(gives_first))
        def _():
            block_ref[:rows, :] = x[:, B:]


def turn(step, goes, layout, offsets, parts, messages, x):
    rows = x.shape[0]
    small = PACKED + RECORD
    if step:
        small += 2 * (messages[0].shape[0] - PACKED)
    shapes = []
    for way in goes:
        shapes.append((base_of(way, rows) + small, B))
        if way == EITHER:
            shapes.append((rows, B))
    kernel = functools.partial(turn_kernel, step, goes, layout, len(parts))
    return call(kernel, shapes, (offsets, *parts, *messages, x))


def half_rotation(angles, offs, take_first):
    halves = [rotate(top, low, angles, offs) for top, low in identity_halves()]
    return jnp.concatenate([jnp.where(take_first, top, low) for top, low in halves], axis=0)


def arrive_kernel(step, came, source, offs_ref, u_ref, w_ref, own_ref, *refs):
    *refs, x_ref, gram_ref, mu_ref, mw_ref = refs
    rows = x_ref.shape[0]
    place = Place(crossed)
    odd = place.odd
    own = place.edge if source is crossed else place.stays
    u_base, w_base = (base_of(way, rows) for way in came)
    mu_ref[...] = u_ref[u_base:, :]
    mw_ref[...] = jnp.where(own, own_ref[w_base:, :], w_ref[w_base:, :])

    def put(first, block):
        @pl.when(first)
        def _():
            x_ref[:, :B] = block

        @pl.when(jnp.logical_not(first))
        def _():
            x_ref[:, B:] = block

    put(odd, u_ref[:rows, :])
    if came[1] == RAW:
        takes_first = jnp.logical_or(jnp.logical_not(odd), place.slot == place.pairs - 1)
        offs = step_offsets(offs_ref, step)
        angles = read_record(mw_ref[PACKED : PACKED + RECORD, :])
        put(jnp.logical_not(odd), product(refs[0][...], half_rotation(angles, offs, takes_first)))
    else:

        @pl.when(own)
        def _():
            put(jnp.logical_not(odd), own_ref[:rows, :])

        @pl.when(jnp.logical_not(own))
        def _():
            put(jnp.logical_not(odd), w_ref[:rows, :])

    gram_ref[...] = transposed_dot(x_ref[:, :B], x_ref[:, B:])


def arrive(step, rows, came, source, offsets, messages, raw=()):
    kernel = functools.partial(arrive_kernel, step, came, source)
    small = messages[0].shape[0] - base_of(came[0], rows)
    shapes = [(rows, 2 * B), (B, B), (small, B), (small, B)]
    return call(kernel, shapes, (offsets, *messages, *raw))


def last_gram_kernel(rows, u_ref, w_ref, own_ref, out_ref):
    own = Place(given).stays

    @pl.when(own)
    def _():
        out_ref[...] = transposed_dot(u_ref[:rows, :], own_ref[:rows, :])

    @pl.when(jnp.logical_not(own))
    def _():
        out_ref[...] = transposed_dot(u_ref[:rows, :], w_ref[:rows, :])


def last_gram(rows, messages):
    return call(functools.partial(last_gram_kernel, rows), [(B, B)], messages)[0]


def settle_kernel(u_ref, w_ref, own_ref, x_ref, mu_ref, mw_ref):
    rows = x_ref.shape[0]
    place = Place(given)
    odd, own = place.odd, place.stays
    u, w = u_ref[...], jnp.where(own, own_ref[...], w_ref[...])
    x_ref[:, :B] = jnp.where(odd, u[:rows], w[:rows])
    x_ref[:, B:] = jnp.where(odd, w[:rows], u[:rows])
    mu_ref[...] = u[rows:]
    mw_ref[...] = w[rows:]


def settle(rows, messages):
    small = messages[0].shape[0] - rows
    shapes = [(rows, 2 * B), (small, B), (small, B)]
    return call(settle_kernel, shapes, messages)


def came_from(slot, is_first, pairs):
    if is_first:
        return jnp.where(slot == 0, 0, slot - 1), slot != 1
    last = slot == pairs - 1
    return jnp.where(last, slot, slot + 1), last


def vectors_kernel(offs_ref, mu_ref, mw_ref, out_ref):
    place = Place(given)
    slot, pairs, part, odd = place.slot, place.pairs, place.part, place.odd
    held_slots = out_ref.shape[0] // (2 * B)
    unit = jnp.where(eye_mask(), 1.0, 0.0)
    zero = jnp.zeros_like(unit)
    pasts = older(odd, mu_ref[...], mw_ref[...])
    nodes = [
        (unit, *came_from(slot, is_first, pairs), past, at)
        for is_first, past, at in ((True, pasts[0], 0), (False, pasts[1], B))
    ]
    for step in reversed(range(STEPS - 1)):
        offs = step_offsets(offs_ref, step)
        below = []
        for block, node, was_first, past, at in nodes:
            top, low = rotate_back(
                jnp.where(was_first, block, zero),
                jnp.where(was_first, zero, block),
                read_record(past[:RECORD]),
                offs,
            )
            if step == 0:
                below.append((top, low, node, at))
                continue
            half = (past.shape[0] - RECORD) // 2
            top_past, low_past = past[RECORD : RECORD + half], past[RECORD + half :]
            below.append((top, *came_from(node, True, pairs), top_past, at))
            below.append((low, *came_from(node, False, pairs), low_past, at))
        nodes = below
    out_ref[...] = jnp.zeros_like(out_ref)
    for top, low, node, column in nodes:

        @pl.when(node // held_slots == part)
        def _():
            at = pl.multiple_of((node - part * held_slots) * (2 * B), 2 * B)
            out_ref[pl.ds(at, B), column : column + B] += top.T
            out_ref[pl.ds(at + B, B), column : column + B] += low.T


def vectors_before_last(height, offsets, messages):
    return call(vectors_kernel, [(height, 2 * B)], (offsets, *messages))[0]


def last_kernel(count, offs_ref, *refs):
    parts, (mu_ref, mw_ref, x_ref, v_ref, x_out, v_out) = refs[:count], refs[count:]
    odd = Place(given).odd
    gram = tree_sum([p[...] for p in parts])
    across = jnp.where(odd, gram, gram.T)
    offs = step_offsets(offs_ref, STEPS - 1)
    _, rotation, _, _ = cross_solve(across, odd, mu_ref[...], mw_ref[...], offs)
    x_out[...] = product(x_ref[...], rotation)
    v_out[...] = product(v_ref[...], rotation)


def last_step(offsets, parts, messages, x, v):
    kernel = functools.partial(last_kernel, len(parts))
    return call(kernel, [x.shape, v.shape], (offsets, *parts, *messages, x, v))


def in_stages(partial, layout):
    distance, count = 1, lax.axis_size("row")
    while 2 * distance < count:
        partial = partial + send(partial, layout, layout, other_part(distance))
        distance *= 2
    if distance < count:
        return [partial, send(partial, layout, layout, other_part(distance))]
    return [partial]


def at_once(partial, layout):
    others = range(1, lax.axis_size("row"))
    return [partial] + [send(partial, layout, layout, other_part(d)) for d in others]


def body(whitened, offsets):
    rows, width = whitened.shape
    height = lax.axis_size("pair") * width // lax.axis_size("row")

    terms = in_stages(whole_gram(whitened), given)
    ways = (JOINED, JOINED)
    near, far = turn(0, ways, given, offsets, terms, (), whitened)
    w = send(far, given, crossed, outer)
    u = send(near, given, crossed, inner)
    x, cross, mu, mw = arrive(0, rows, ways, given, offsets, (u, w, far))

    raw = send(x, crossed, crossed, outer, swap=False)
    terms = at_once(cross, crossed)
    ways = (JOINED, RAW)
    near, far = turn(1, ways, crossed, offsets, terms, (mu, mw), x)
    w = send(far, crossed, crossed, outer)
    u = send(near, crossed, crossed, inner)
    x, cross, mu, mw = arrive(1, rows, ways, crossed, offsets, (u, w, far), (raw,))

    terms = at_once(cross, crossed)
    near, far = turn(2, (JOINED, JOINED), crossed, offsets, terms, (mu, mw), x)
    w = send(far, crossed, given, outer)
    u = send(near, crossed, given, inner)
    terms = in_stages(last_gram(rows, (u, w, far)), given)
    x, mu, mw = settle(rows, (u, w, far))
    vectors = vectors_before_last(height, offsets, (mu, mw))
    return last_step(offsets, terms, (mu, mw), x, vectors)


def solution(mesh):
    in_specs = (P("row", "pair"), P())
    out_specs = (P("row", "pair"), P("row", "pair"))
    return jax.shard_map(body, mesh=mesh, in_specs=in_specs, out_specs=out_specs, check_vma=False)
```

time: 92.7 us -> 85.9 us (0.927)
  the two profiles are of different devices: /device:TPU:20 before, /device:TPU:0 now
where the time goes in v3:
time: 85.9 us; the launch traced here: 85.4 us
  waiting for transfers between devices  36.9 us (43%)
  starting transfers between devices  29.5 us (34%)
  Pallas kernels  17 us (20%)
  local copies, waits for them, and re-layouts  1.22 us (1%)
    ppermute x17, waiting for transfers between devices, send(): return lax.ppermute(x, AXES, route(source, target, change, swap))  36.9 us
    ppermute x17, starting transfers between devices, send(): return lax.ppermute(x, AXES, route(source, target, change, swap))  29.5 us
    pallas_call x10, Pallas kernels, call(): pl.pallas_call(kernel, out_shape=tuple((jax.ShapeDtypeStruct(shape, jnp.f...  17 us
  transfers between devices with their start and end apart: 17, of which 14 were waited for; matrix products, arithmetic and copies ran while one was open for 0% of the time, Pallas kernels for 5%

profile of v3, /device:TPU:0, one launch (start us, length us, event | category | flops | bytes accessed | tf_op | source)
XLA Modules:
  0.0 85.4 jit_solution(1269466517439183435)
XLA Ops:
  0.6 0.0 copy-start
  0.6 1.2 %copy-done = f32[1024,256]{1,0:T(8,128)S(1)} copy-done((f32[1024,256]{1,0:T(8,128)S(1)}, f32[1024,256]{1,0:T(8,128)}, u32[]{:S(2)}) %copy-start) | copy-done | bytes 1048600
  1.9 1.2 %shard_map.41 = f32[264,128]{1,0:T(8,128)S(1)} custom-call(f32[1024,256]{1,0:T(8,128)S(1)} %copy-done), custom_call_target="tpu_custom_call" | custom-call | tf_op jit(solution)/shard_map/pallas_call | solution.py:224
  3.0 0.0 copy-start.1
  3.1 0.5 collective-permute-start
  3.6 1.0 %collective-permute-done = f32[264,128]{1,0:T(8,128)S(1)} collective-permute-done((f32[264,128]{1,0:T(8,128)S(1)}, f32[264,128]{1,0:T(8,128)S(1)}, u32[]{:S(2)}, u32[]{:S(2)}) %collective-permute-start) | collective-permute-done | bytes 135200 | tf_op jit(solution)/shard_map/ppermute | solution.py:53
  4.6 2.9 %collective-permute-start.1 = (f32[264,128]{1,0:T(8,128)S(1)}, f32[264,128]{1,0:T(8,128)S(1)}, u32[]{:S(2)}, u32[]{:S(2)}) collective-permute-start(f32[264,128]{1,0:T(8,128)S(1)} %add.6.refs_0_), channel_id=1, source_target_pairs={{0,2},{1,3},{2,0},{3,1},{4,6},{5,7},{6,4},{7,5},{8,10},{9,11},{10,... | collective-permute-start | bytes 405512 | tf_op jit(solution)/shard_map/ppermute | solution.py:53
  7.5 3.9 %collective-permute-done.1.refs_1_ = f32[264,128]{1,0:T(8,128)S(1)} collective-permute-done((f32[264,128]{1,0:T(8,128)S(1)}, f32[264,128]{1,0:T(8,128)S(1)}, u32[]{:S(2)}, u32[]{:S(2)}) %collective-permute-start.1) | collective-permute-done | bytes 135200 | tf_op jit(solution)/shard_map/ppermute | solution.py:53
  11.4 0.0 copy-done.1
  11.4 2.0 %shard_map.42 = (f32[1104,128]{1,0:T(8,128)S(1)}, f32[1104,128]{1,0:T(8,128)S(1)}) custom-call(s32[4,4]{1,0:T(4,128)S(1)} %copy-done.1, f32[264,128]{1,0:T(8,128)S(1)} %add.6.refs_0_, f32[264,128]{1,0:T(8,128)S(1)} %collective-permute-done.1.refs_1_, f32[1024,256]{1,0:T(8,128)S(1)} %copy-done), custom_call_target="tpu_custom_call" | custom-call | tf_op jit(solution)/shard_map/pallas_call | solution.py:224
  13.4 0.0 collective-permute-start.2
  13.4 1.8 %collective-permute-start.3 = (f32[1104,128]{1,0:T(8,128)S(1)}, f32[1104,128]{1,0:T(8,128)S(1)}, u32[]{:S(2)}, u32[]{:S(2)}) collective-permute-start(f32[1104,128]{1,0:T(8,128)S(1)} %get-tuple-element.20.own_ref), channel_id=1, source_target_pairs={{0,2},{1,4},{2,0},{3,6},{4,8},{5,12},{6,10},{7,14},{8,1},{9,5},{10... | collective-permute-start | bytes 1695752 | tf_op jit(solution)/shard_map/ppermute | solution.py:53
  15.2 7.8 %collective-permute-done.2.u_ref = f32[1104,128]{1,0:T(8,128)S(1)} collective-permute-done((f32[1104,128]{1,0:T(8,128)S(1)}, f32[1104,128]{1,0:T(8,128)S(1)}, u32[]{:S(2)}, u32[]{:S(2)}) %collective-permute-start.2) | collective-permute-done | bytes 565280 | tf_op jit(solution)/shard_map/ppermute | solution.py:53
  23.0 0.1 collective-permute-done.3.w_ref
  23.1 0.8 shard_map.43
  23.9 0.7 collective-permute-start.9
  24.6 13.2 %collective-permute-start.6 = (f32[128,128]{1,0:T(8,128)S(1)}, f32[128,128]{1,0:T(8,128)S(1)}, u32[]{:S(2)}, u32[]{:S(2)}) collective-permute-start(f32[128,128]{1,0:T(8,128)S(1)} %get-tuple-element.21.refs_0_), channel_id=1, source_target_pairs={{0,6},{4,2},{2,4},{6,0},{1,7},{5,3},{3,5},{7,1},{8,14},{12,10},{10... | collective-permute-start | bytes 196616 | tf_op jit(solution)/shard_map/ppermute | solution.py:53
  37.8 0.5 collective-permute-start.5
  38.3 0.1 collective-permute-start.4
  38.4 2.3 %collective-permute-done.6.refs_3_ = f32[128,128]{1,0:T(8,128)S(1)} collective-permute-done((f32[128,128]{1,0:T(8,128)S(1)}, f32[128,128]{1,0:T(8,128)S(1)}, u32[]{:S(2)}, u32[]{:S(2)}) %collective-permute-start.6) | collective-permute-done | bytes 65568 | tf_op jit(solution)/shard_map/ppermute | solution.py:53
  40.7 1.3 %collective-permute-done.5.refs_2_ = f32[128,128]{1,0:T(8,128)S(1)} collective-permute-done((f32[128,128]{1,0:T(8,128)S(1)}, f32[128,128]{1,0:T(8,128)S(1)}, u32[]{:S(2)}, u32[]{:S(2)}) %collective-permute-start.5) | collective-permute-done | bytes 65568 | tf_op jit(solution)/shard_map/ppermute | solution.py:53
  42.0 0.5 collective-permute-done.4.refs_1_
  42.6 2.0 %shard_map.44 = (f32[1120,128]{1,0:T(8,128)S(1)}, f32[96,128]{1,0:T(8,128)S(1)}) custom-call(s32[4,4]{1,0:T(4,128)S(1)} %copy-done.1, f32[128,128]{1,0:T(8,128)S(1)} %get-tuple-element.21.refs_0_, f32[128,128]{1,0:T(8,128)S(1)} %collective-permute-done.4.refs_1_, f32[128,128]{1,0:T(8,128)S(1)} %collective-permute-done.5.refs_2_, ...), custom_call_target="tpu_custom_call" | custom-call | tf_op jit(solution)/shard_map/pallas_call | solution.py:224
  44.6 0.1 collective-permute-start.7
  44.6 1.6 %collective-permute-start.8 = (f32[96,128]{1,0:T(8,128)S(1)}, f32[96,128]{1,0:T(8,128)S(1)}, u32[]{:S(2)}, u32[]{:S(2)}) collective-permute-start(f32[96,128]{1,0:T(8,128)S(1)} %get-tuple-element.26.own_ref), channel_id=1, source_target_pairs={{0,2},{4,6},{2,0},{6,4},{1,8},{5,12},{3,10},{7,14},{8,1},{12,5},{1... | collective-permute-start | bytes 147464 | tf_op jit(solution)/shard_map/ppermute | solution.py:53
  46.2 2.6 %collective-permute-done.8.w_ref = f32[96,128]{1,0:T(8,128)S(1)} collective-permute-done((f32[96,128]{1,0:T(8,128)S(1)}, f32[96,128]{1,0:T(8,128)S(1)}, u32[]{:S(2)}, u32[]{:S(2)}) %collective-permute-start.8) | collective-permute-done | bytes 49184 | tf_op jit(solution)/shard_map/ppermute | solution.py:53
  48.8 0.0 collective-permute-done.7.u_ref
  48.8 0.0 collective-permute-done.9.refs_0_
  48.8 2.4 %shard_map.45 = (f32[1024,256]{1,0:T(8,128)S(1)}, f32[128,128]{1,0:T(8,128)S(1)}, f32[96,128]{1,0:T(8,128)S(1)}, f32[96,128]{1,0:T(8,128)S(1)}) custom-call(s32[4,4]{1,0:T(4,128)S(1)} %copy-done.1, f32[1120,128]{1,0:T(8,128)S(1)} %collective-permute-done.7.u_ref, f32[96,128]{1,0:T(8,128)S(1)} %collective-permute-done.8.w_ref, ...), custom_call_target="tpu_custom_call" | custom-call | tf_op jit(solution)/shard_map/pallas_call | solution.py:224
  51.2 1.7 %collective-permute-start.12 = (f32[128,128]{1,0:T(8,128)S(1)}, f32[128,128]{1,0:T(8,128)S(1)}, u32[]{:S(2)}, u32[]{:S(2)}) collective-permute-start(f32[128,128]{1,0:T(8,128)S(1)} %get-tuple-element.27.refs_0_), channel_id=1, source_target_pairs={{0,6},{4,2},{2,4},{6,0},{1,7},{5,3},{3,5},{7,1},{8,14},{12,10},{10... | collective-permute-start | bytes 196616 | tf_op jit(solution)/shard_map/ppermute | solution.py:53
  53.0 0.5 collective-permute-start.11
  53.5 1.3 %collective-permute-start.10 = (f32[128,128]{1,0:T(8,128)S(1)}, f32[128,128]{1,0:T(8,128)S(1)}, u32[]{:S(2)}, u32[]{:S(2)}) collective-permute-start(f32[128,128]{1,0:T(8,128)S(1)} %get-tuple-element.27.refs_0_), channel_id=1, source_target_pairs={{0,4},{4,0},{2,6},{6,2},{1,5},{5,1},{3,7},{7,3},{8,12},{12,8},{10,... | collective-permute-start | bytes 196616 | tf_op jit(solution)/shard_map/ppermute | solution.py:53
  54.8 1.9 %collective-permute-done.12.refs_3_ = f32[128,128]{1,0:T(8,128)S(1)} collective-permute-done((f32[128,128]{1,0:T(8,128)S(1)}, f32[128,128]{1,0:T(8,128)S(1)}, u32[]{:S(2)}, u32[]{:S(2)}) %collective-permute-start.12) | collective-permute-done | bytes 65568 | tf_op jit(solution)/shard_map/ppermute | solution.py:53
  56.7 1.2 %collective-permute-done.11.refs_2_ = f32[128,128]{1,0:T(8,128)S(1)} collective-permute-done((f32[128,128]{1,0:T(8,128)S(1)}, f32[128,128]{1,0:T(8,128)S(1)}, u32[]{:S(2)}, u32[]{:S(2)}) %collective-permute-start.11) | collective-permute-done | bytes 65568 | tf_op jit(solution)/shard_map/ppermute | solution.py:53
  57.8 0.7 collective-permute-done.10.refs_1_
  58.6 2.1 %shard_map.46 = (f32[1152,128]{1,0:T(8,128)S(1)}, f32[1152,128]{1,0:T(8,128)S(1)}) custom-call(s32[4,4]{1,0:T(4,128)S(1)} %copy-done.1, f32[128,128]{1,0:T(8,128)S(1)} %get-tuple-element.27.refs_0_, f32[128,128]{1,0:T(8,128)S(1)} %collective-permute-done.10.refs_1_, f32[128,128]{1,0:T(8,128)S(1)} %collective-permute-done.11.refs_2_, ...), custom_call_target="tpu_custom_call" | custom-call | tf_op jit(solution)/shard_map/pallas_call | solution.py:224
  60.6 1.2 %collective-permute-start.13 = (f32[1152,128]{1,0:T(8,128)S(1)}, f32[1152,128]{1,0:T(8,128)S(1)}, u32[]{:S(2)}, u32[]{:S(2)}) collective-permute-start(f32[1152,128]{1,0:T(8,128)S(1)} %get-tuple-element.31), channel_id=1, source_target_pairs={{0,4},{4,5},{2,6},{6,7},{1,0},{5,1},{3,2},{7,3},{8,12},{12,13},{10... | collective-permute-start | bytes 1769480 | tf_op jit(solution)/shard_map/ppermute | solution.py:53
  61.8 1.5 %collective-permute-start.14 = (f32[1152,128]{1,0:T(8,128)S(1)}, f32[1152,128]{1,0:T(8,128)S(1)}, u32[]{:S(2)}, u32[]{:S(2)}) collective-permute-start(f32[1152,128]{1,0:T(8,128)S(1)} %get-tuple-element.32.own_ref), channel_id=1, source_target_pairs={{0,2},{4,1},{2,0},{6,3},{1,8},{5,9},{3,10},{7,11},{8,4},{12,5},{10... | collective-permute-start | bytes 1769480 | tf_op jit(solution)/shard_map/ppermute | solution.py:53
  63.3 12.2 %collective-permute-done.13.u_ref = f32[1152,128]{1,0:T(8,128)S(1)} collective-permute-done((f32[1152,128]{1,0:T(8,128)S(1)}, f32[1152,128]{1,0:T(8,128)S(1)}, u32[]{:S(2)}, u32[]{:S(2)}) %collective-permute-start.13) | collective-permute-done | bytes 589856 | tf_op jit(solution)/shard_map/ppermute | solution.py:53
  75.5 0.0 collective-permute-done.14.w_ref
  75.6 0.8 shard_map.47
  76.4 0.3 collective-permute-start.15
  76.7 1.0 %collective-permute-done.15 = f32[128,128]{1,0:T(8,128)S(1)} collective-permute-done((f32[128,128]{1,0:T(8,128)S(1)}, f32[128,128]{1,0:T(8,128)S(1)}, u32[]{:S(2)}, u32[]{:S(2)}) %collective-permute-start.15) | collective-permute-done | bytes 65568 | tf_op jit(solution)/shard_map/ppermute | solution.py:53
  77.7 1.6 %collective-permute-start.16 = (f32[128,128]{1,0:T(8,128)S(1)}, f32[128,128]{1,0:T(8,128)S(1)}, u32[]{:S(2)}, u32[]{:S(2)}) collective-permute-start(f32[128,128]{1,0:T(8,128)S(1)} %add.7.refs_0_), channel_id=1, source_target_pairs={{0,2},{1,3},{2,0},{3,1},{4,6},{5,7},{6,4},{7,5},{8,10},{9,11},{10,... | collective-permute-start | bytes 196616 | tf_op jit(solution)/shard_map/ppermute | solution.py:53
  79.3 0.1 shard_map.48
  79.4 2.3 %shard_map.49.refs_5_ = f32[512,256]{1,0:T(8,128)S(1)} custom-call(s32[4,4]{1,0:T(4,128)S(1)} %copy-done.1, f32[128,128]{1,0:T(8,128)S(1)} %get-tuple-element.33.mu_ref.refs_2_, f32[128,128]{1,0:T(8,128)S(1)} %get-tuple-element.34.mw_ref.refs_3_), custom_call_target="tpu_custom_call" | custom-call | tf_op jit(solution)/shard_map/pallas_call | solution.py:224
  81.7 0.3 collective-permute-done.16.refs_1_
  82.0 3.3 %shard_map.50 = (f32[1024,256]{1,0:T(8,128)}, f32[512,256]{1,0:T(8,128)}) custom-call(s32[4,4]{1,0:T(4,128)S(1)} %copy-done.1, f32[128,128]{1,0:T(8,128)S(1)} %add.7.refs_0_, f32[128,128]{1,0:T(8,128)S(1)} %collective-permute-done.16.refs_1_, f32[128,128]{1,0:T(8,128)S(1)} %get-tuple-element.33.mu_ref.refs_2_, ...), custom_call_target="tpu_custom_call" | custom-call | tf_op jit(solution)/shard_map/pallas_call | solution.py:224
  (2 shorter events, 0.0 us)
Async XLA Ops:
  0.6 1.2 %copy-start = (f32[1024,256]{1,0:T(8,128)S(1)}, f32[1024,256]{1,0:T(8,128)}, u32[]{:S(2)}) copy-start(f32[1024,256]{1,0:T(8,128)} %refs_2_.1) | copy-start | bytes 3145732
  3.0 8.4 %copy-start.1 = (s32[4,4]{1,0:T(4,128)S(1)}, s32[4,4]{1,0:T(4,128)}, u32[]{:S(2)}) copy-start(s32[4,4]{1,0:T(4,128)} %offs_ref.13) | copy-start | bytes 196
  3.1 1.5 %collective-permute-start = (f32[264,128]{1,0:T(8,128)S(1)}, f32[264,128]{1,0:T(8,128)S(1)}, u32[]{:S(2)}, u32[]{:S(2)}) collective-permute-start(f32[264,128]{1,0:T(8,128)S(1)} %shard_map.41), channel_id=1, source_target_pairs={{0,1},{1,0},{2,3},{3,2},{4,5},{5,4},{6,7},{7,6},{8,9},{9,8},{10,11... | collective-permute-start | bytes 405512 | tf_op jit(solution)/shard_map/ppermute | solution.py:53
  4.6 6.8 %collective-permute-start.1 = (f32[264,128]{1,0:T(8,128)S(1)}, f32[264,128]{1,0:T(8,128)S(1)}, u32[]{:S(2)}, u32[]{:S(2)}) collective-permute-start(f32[264,128]{1,0:T(8,128)S(1)} %add.6.refs_0_), channel_id=1, source_target_pairs={{0,2},{1,3},{2,0},{3,1},{4,6},{5,7},{6,4},{7,5},{8,10},{9,11},{10,... | collective-permute-start | bytes 405512 | tf_op jit(solution)/shard_map/ppermute | solution.py:53
  13.4 9.6 %collective-permute-start.2 = (f32[1104,128]{1,0:T(8,128)S(1)}, f32[1104,128]{1,0:T(8,128)S(1)}, u32[]{:S(2)}, u32[]{:S(2)}) collective-permute-start(f32[1104,128]{1,0:T(8,128)S(1)} %get-tuple-element.19), channel_id=1, source_target_pairs={{0,1},{1,5},{2,3},{3,7},{4,0},{5,4},{6,2},{7,6},{8,9},{9,13},{10,1... | collective-permute-start | bytes 1695752 | tf_op jit(solution)/shard_map/ppermute | solution.py:53
  13.4 9.7 %collective-permute-start.3 = (f32[1104,128]{1,0:T(8,128)S(1)}, f32[1104,128]{1,0:T(8,128)S(1)}, u32[]{:S(2)}, u32[]{:S(2)}) collective-permute-start(f32[1104,128]{1,0:T(8,128)S(1)} %get-tuple-element.20.own_ref), channel_id=1, source_target_pairs={{0,2},{1,4},{2,0},{3,6},{4,8},{5,12},{6,10},{7,14},{8,1},{9,5},{10... | collective-permute-start | bytes 1695752 | tf_op jit(solution)/shard_map/ppermute | solution.py:53
  23.9 24.9 %collective-permute-start.9 = (f32[1024,256]{1,0:T(8,128)S(1)}, f32[1024,256]{1,0:T(8,128)S(1)}, u32[]{:S(2)}, u32[]{:S(2)}) collective-permute-start(f32[1024,256]{1,0:T(8,128)S(1)} %get-tuple-element.24.refs_6_), channel_id=1, source_target_pairs={{0,0},{4,4},{2,2},{6,6},{1,8},{5,12},{3,10},{7,14},{8,1},{12,5},{1... | collective-permute-start | bytes 3145736 | tf_op jit(solution)/shard_map/ppermute | solution.py:53
  24.6 16.1 %collective-permute-start.6 = (f32[128,128]{1,0:T(8,128)S(1)}, f32[128,128]{1,0:T(8,128)S(1)}, u32[]{:S(2)}, u32[]{:S(2)}) collective-permute-start(f32[128,128]{1,0:T(8,128)S(1)} %get-tuple-element.21.refs_0_), channel_id=1, source_target_pairs={{0,6},{4,2},{2,4},{6,0},{1,7},{5,3},{3,5},{7,1},{8,14},{12,10},{10... | collective-permute-start | bytes 196616 | tf_op jit(solution)/shard_map/ppermute | solution.py:53
  37.8 4.3 %collective-permute-start.5 = (f32[128,128]{1,0:T(8,128)S(1)}, f32[128,128]{1,0:T(8,128)S(1)}, u32[]{:S(2)}, u32[]{:S(2)}) collective-permute-start(f32[128,128]{1,0:T(8,128)S(1)} %get-tuple-element.21.refs_0_), channel_id=1, source_target_pairs={{0,2},{4,6},{2,0},{6,4},{1,3},{5,7},{3,1},{7,5},{8,10},{12,14},{10... | collective-permute-start | bytes 196616 | tf_op jit(solution)/shard_map/ppermute | solution.py:53
  38.3 4.3 %collective-permute-start.4 = (f32[128,128]{1,0:T(8,128)S(1)}, f32[128,128]{1,0:T(8,128)S(1)}, u32[]{:S(2)}, u32[]{:S(2)}) collective-permute-start(f32[128,128]{1,0:T(8,128)S(1)} %get-tuple-element.21.refs_0_), channel_id=1, source_target_pairs={{0,4},{4,0},{2,6},{6,2},{1,5},{5,1},{3,7},{7,3},{8,12},{12,8},{10,... | collective-permute-start | bytes 196616 | tf_op jit(solution)/shard_map/ppermute | solution.py:53
  44.6 4.2 %collective-permute-start.7 = (f32[1120,128]{1,0:T(8,128)S(1)}, f32[1120,128]{1,0:T(8,128)S(1)}, u32[]{:S(2)}, u32[]{:S(2)}) collective-permute-start(f32[1120,128]{1,0:T(8,128)S(1)} %get-tuple-element.25), channel_id=1, source_target_pairs={{0,1},{4,5},{2,3},{6,7},{1,0},{5,4},{3,2},{7,6},{8,9},{12,13},{10,... | collective-permute-start | bytes 1720328 | tf_op jit(solution)/shard_map/ppermute | solution.py:53
  44.6 4.2 %collective-permute-start.8 = (f32[96,128]{1,0:T(8,128)S(1)}, f32[96,128]{1,0:T(8,128)S(1)}, u32[]{:S(2)}, u32[]{:S(2)}) collective-permute-start(f32[96,128]{1,0:T(8,128)S(1)} %get-tuple-element.26.own_ref), channel_id=1, source_target_pairs={{0,2},{4,6},{2,0},{6,4},{1,8},{5,12},{3,10},{7,14},{8,1},{12,5},{1... | collective-permute-start | bytes 147464 | tf_op jit(solution)/shard_map/ppermute | solution.py:53
  51.2 5.4 %collective-permute-start.12 = (f32[128,128]{1,0:T(8,128)S(1)}, f32[128,128]{1,0:T(8,128)S(1)}, u32[]{:S(2)}, u32[]{:S(2)}) collective-permute-start(f32[128,128]{1,0:T(8,128)S(1)} %get-tuple-element.27.refs_0_), channel_id=1, source_target_pairs={{0,6},{4,2},{2,4},{6,0},{1,7},{5,3},{3,5},{7,1},{8,14},{12,10},{10... | collective-permute-start | bytes 196616 | tf_op jit(solution)/shard_map/ppermute | solution.py:53
  53.0 4.9 %collective-permute-start.11 = (f32[128,128]{1,0:T(8,128)S(1)}, f32[128,128]{1,0:T(8,128)S(1)}, u32[]{:S(2)}, u32[]{:S(2)}) collective-permute-start(f32[128,128]{1,0:T(8,128)S(1)} %get-tuple-element.27.refs_0_), channel_id=1, source_target_pairs={{0,2},{4,6},{2,0},{6,4},{1,3},{5,7},{3,1},{7,5},{8,10},{12,14},{10... | collective-permute-start | bytes 196616 | tf_op jit(solution)/shard_map/ppermute | solution.py:53
  53.5 5.1 %collective-permute-start.10 = (f32[128,128]{1,0:T(8,128)S(1)}, f32[128,128]{1,0:T(8,128)S(1)}, u32[]{:S(2)}, u32[]{:S(2)}) collective-permute-start(f32[128,128]{1,0:T(8,128)S(1)} %get-tuple-element.27.refs_0_), channel_id=1, source_target_pairs={{0,4},{4,0},{2,6},{6,2},{1,5},{5,1},{3,7},{7,3},{8,12},{12,8},{10,... | collective-permute-start | bytes 196616 | tf_op jit(solution)/shard_map/ppermute | solution.py:53
  60.6 14.9 %collective-permute-start.13 = (f32[1152,128]{1,0:T(8,128)S(1)}, f32[1152,128]{1,0:T(8,128)S(1)}, u32[]{:S(2)}, u32[]{:S(2)}) collective-permute-start(f32[1152,128]{1,0:T(8,128)S(1)} %get-tuple-element.31), channel_id=1, source_target_pairs={{0,4},{4,5},{2,6},{6,7},{1,0},{5,1},{3,2},{7,3},{8,12},{12,13},{10... | collective-permute-start | bytes 1769480 | tf_op jit(solution)/shard_map/ppermute | solution.py:53
  61.8 13.7 %collective-permute-start.14 = (f32[1152,128]{1,0:T(8,128)S(1)}, f32[1152,128]{1,0:T(8,128)S(1)}, u32[]{:S(2)}, u32[]{:S(2)}) collective-permute-start(f32[1152,128]{1,0:T(8,128)S(1)} %get-tuple-element.32.own_ref), channel_id=1, source_target_pairs={{0,2},{4,1},{2,0},{6,3},{1,8},{5,9},{3,10},{7,11},{8,4},{12,5},{10... | collective-permute-start | bytes 1769480 | tf_op jit(solution)/shard_map/ppermute | solution.py:53
  76.4 1.3 %collective-permute-start.15 = (f32[128,128]{1,0:T(8,128)S(1)}, f32[128,128]{1,0:T(8,128)S(1)}, u32[]{:S(2)}, u32[]{:S(2)}) collective-permute-start(f32[128,128]{1,0:T(8,128)S(1)} %shard_map.47), channel_id=1, source_target_pairs={{0,1},{1,0},{2,3},{3,2},{4,5},{5,4},{6,7},{7,6},{8,9},{9,8},{10,11... | collective-permute-start | bytes 196616 | tf_op jit(solution)/shard_map/ppermute | solution.py:53
  77.7 4.3 %collective-permute-start.16 = (f32[128,128]{1,0:T(8,128)S(1)}, f32[128,128]{1,0:T(8,128)S(1)}, u32[]{:S(2)}, u32[]{:S(2)}) collective-permute-start(f32[128,128]{1,0:T(8,128)S(1)} %add.7.refs_0_), channel_id=1, source_target_pairs={{0,2},{1,3},{2,0},{3,1},{4,6},{5,7},{6,4},{7,5},{8,10},{9,11},{10,... | collective-permute-start | bytes 196616 | tf_op jit(solution)/shard_map/ppermute | solution.py:53

commit v4 on v3

--- a/solution.py
+++ b/solution.py
@@ -237,7 +237,8 @@
         self.slot, self.part = layout(pair, row)
         self.odd = (self.slot & 1) == 1
         self.edge = jnp.logical_or(self.slot == 0, self.slot == self.pairs - 1)
-        self.stays = jnp.logical_and(self.edge, ((pair ^ row) & 1) == 0)
+        self.same = ((pair ^ row) & 1) == 0
+        self.stays = jnp.logical_and(self.edge, self.same)
 
 
 def whole_gram_kernel(x_ref, out_ref):
@@ -353,7 +354,10 @@
         def _():
             x_ref[:, B:] = block
 
-    put(odd, u_ref[:rows, :])
+    if came[0] == JOINED:
+        put(odd, u_ref[:rows, :])
+    else:
+        put(odd, refs[0][...])
     if came[1] == RAW:
         takes_first = jnp.logical_or(jnp.logical_not(odd), place.slot == place.pairs - 1)
         offs = step_offsets(offs_ref, step)
@@ -370,6 +374,26 @@
             put(jnp.logical_not(odd), w_ref[:rows, :])
 
     gram_ref[...] = transposed_dot(x_ref[:, :B], x_ref[:, B:])
+
+
+def ready_kernel(step, offs_ref, u_ref, block_ref, raw_ref, out_ref):
+    place = Place(crossed)
+
+    @pl.when(place.same)
+    def _():
+        takes_first = jnp.logical_and(place.odd, place.slot != 1)
+        angles = read_record(u_ref[PACKED : PACKED + RECORD, :])
+        half = half_rotation(angles, step_offsets(offs_ref, step), takes_first)
+        out_ref[...] = product(raw_ref[...], half)
+
+    @pl.when(jnp.logical_not(place.same))
+    def _():
+        out_ref[...] = block_ref[...]
+
+
+def ready(step, offsets, u, block, raw):
+    kernel = functools.partial(ready_kernel, step)
+    return call(kernel, [block.shape], (offsets, u, block, raw))[0]
 
 
 def arrive(step, rows, came, source, offsets, messages, raw=()):
@@ -497,12 +521,15 @@
     rows, width = whitened.shape
     height = lax.axis_size("pair") * width // lax.axis_size("row")
 
+    raw = send(whitened, given, crossed, inner)
     terms = in_stages(whole_gram(whitened), given)
-    ways = (JOINED, JOINED)
-    near, far = turn(0, ways, given, offsets, terms, (), whitened)
+    ways = (EITHER, JOINED)
+    near, block, far = turn(0, ways, given, offsets, terms, (), whitened)
     w = send(far, given, crossed, outer)
     u = send(near, given, crossed, inner)
-    x, cross, mu, mw = arrive(0, rows, ways, given, offsets, (u, w, far))
+    block = send(block, given, given, other_part(1))
+    block = ready(0, offsets, u, block, raw)
+    x, cross, mu, mw = arrive(0, rows, ways, given, offsets, (u, w, far), (block,))
 
     raw = send(x, crossed, crossed, outer, swap=False)
     terms = at_once(cross, crossed)

time: 85.9 us -> 83.1 us (0.967)
  starting transfers between devices: 29.5 us -> 26.5 us
  Pallas kernels: 17 us -> 18 us
    ppermute x17 -> x19, starting transfers between devices: 29.5 us -> 26.5 us  [send(): return lax.ppermute(x, AXES, route(source, target, change, swap))]
    pallas_call x10 -> x11, Pallas kernels: 17 us -> 18 us  [call(): pl.pallas_call(kernel, out_shape=tuple((jax.ShapeDtypeStruct(shape, jnp.f...]
    ppermute x17 -> x19, waiting for transfers between devices: 36.9 us -> 36.1 us  [send(): return lax.ppermute(x, AXES, route(source, target, change, swap))]
  transfers between devices with their start and end apart: 17 -> 19, of which waited for: 14 -> 13; matrix products, arithmetic and copies ran while one was open for 0% -> 0% of each run, Pallas kernels for 5% -> 10%
where the time goes in v4:
time: 83.1 us; the launch traced here: 82.6 us
  waiting for transfers between devices  36.1 us (43%)
  starting transfers between devices  26.5 us (32%)
  Pallas kernels  18 us (22%)
  local copies, waits for them, and re-layouts  1.23 us (1%)
    ppermute x19, waiting for transfers between devices, send(): return lax.ppermute(x, AXES, route(source, target, change, swap))  36.1 us
    ppermute x19, starting transfers between devices, send(): return lax.ppermute(x, AXES, route(source, target, change, swap))  26.5 us
    pallas_call x11, Pallas kernels, call(): pl.pallas_call(kernel, out_shape=tuple((jax.ShapeDtypeStruct(shape, jnp.f...  18 us
  transfers between devices with their start and end apart: 19, of which 13 were waited for; matrix products, arithmetic and copies ran while one was open for 0% of the time, Pallas kernels for 10%

profile of v4, /device:TPU:0, one launch (start us, length us, event | category | flops | bytes accessed | tf_op | source)
XLA Modules:
  0.0 82.6 jit_solution(15904678409147085204)
XLA Ops:
  0.6 0.5 collective-permute-start.5
  1.1 1.2 %copy-done = f32[1024,256]{1,0:T(8,128)S(1)} copy-done((f32[1024,256]{1,0:T(8,128)S(1)}, f32[1024,256]{1,0:T(8,128)}, u32[]{:S(2)}) %copy-start) | copy-done | bytes 1048600
  2.3 1.2 %shard_map.41 = f32[264,128]{1,0:T(8,128)S(1)} custom-call(f32[1024,256]{1,0:T(8,128)S(1)} %copy-done), custom_call_target="tpu_custom_call" | custom-call | tf_op jit(solution)/shard_map/pallas_call | solution.py:224
  3.5 0.0 copy-start.1
  3.5 2.2 %collective-permute-start = (f32[264,128]{1,0:T(8,128)S(1)}, f32[264,128]{1,0:T(8,128)S(1)}, u32[]{:S(2)}, u32[]{:S(2)}) collective-permute-start(f32[264,128]{1,0:T(8,128)S(1)} %shard_map.41), channel_id=1, source_target_pairs={{0,1},{1,0},{2,3},{3,2},{4,5},{5,4},{6,7},{7,6},{8,9},{9,8},{10,11... | collective-permute-start | bytes 405512 | tf_op jit(solution)/shard_map/ppermute | solution.py:53
  5.7 1.0 %collective-permute-done = f32[264,128]{1,0:T(8,128)S(1)} collective-permute-done((f32[264,128]{1,0:T(8,128)S(1)}, f32[264,128]{1,0:T(8,128)S(1)}, u32[]{:S(2)}, u32[]{:S(2)}) %collective-permute-start) | collective-permute-done | bytes 135200 | tf_op jit(solution)/shard_map/ppermute | solution.py:53
  6.7 1.6 %collective-permute-start.1 = (f32[264,128]{1,0:T(8,128)S(1)}, f32[264,128]{1,0:T(8,128)S(1)}, u32[]{:S(2)}, u32[]{:S(2)}) collective-permute-start(f32[264,128]{1,0:T(8,128)S(1)} %add.6.refs_0_), channel_id=1, source_target_pairs={{0,2},{1,3},{2,0},{3,1},{4,6},{5,7},{6,4},{7,5},{8,10},{9,11},{10,... | collective-permute-start | bytes 405512 | tf_op jit(solution)/shard_map/ppermute | solution.py:53
  8.3 4.4 %collective-permute-done.1.refs_1_ = f32[264,128]{1,0:T(8,128)S(1)} collective-permute-done((f32[264,128]{1,0:T(8,128)S(1)}, f32[264,128]{1,0:T(8,128)S(1)}, u32[]{:S(2)}, u32[]{:S(2)}) %collective-permute-start.1) | collective-permute-done | bytes 135200 | tf_op jit(solution)/shard_map/ppermute | solution.py:53
  12.6 2.0 %shard_map.42 = (f32[80,128]{1,0:T(8,128)S(1)}, f32[1024,128]{1,0:T(8,128)S(1)}, f32[1104,128]{1,0:T(8,128)S(1)}) custom-call(s32[4,4]{1,0:T(4,128)S(1)} %copy-done.1, f32[264,128]{1,0:T(8,128)S(1)} %add.6.refs_0_, f32[264,128]{1,0:T(8,128)S(1)} %collective-permute-done.1.refs_1_, f32[1024,256]{1,0:T(8,128)S(1)} %copy-done), custom_call_target="tpu_custom_call" | custom-call | tf_op jit(solution)/shard_map/pallas_call | solution.py:224
  14.6 1.5 %collective-permute-start.3 = (f32[1104,128]{1,0:T(8,128)S(1)}, f32[1104,128]{1,0:T(8,128)S(1)}, u32[]{:S(2)}, u32[]{:S(2)}) collective-permute-start(f32[1104,128]{1,0:T(8,128)S(1)} %get-tuple-element.21.own_ref), channel_id=1, source_target_pairs={{0,2},{1,4},{2,0},{3,6},{4,8},{5,12},{6,10},{7,14},{8,1},{9,5},{10... | collective-permute-start | bytes 1695752 | tf_op jit(solution)/shard_map/ppermute | solution.py:53
  16.2 0.5 collective-permute-start.2
  16.7 3.5 %collective-permute-done.2.u_ref = f32[80,128]{1,0:T(8,128)S(1)} collective-permute-done((f32[80,128]{1,0:T(8,128)S(1)}, f32[80,128]{1,0:T(8,128)S(1)}, u32[]{:S(2)}, u32[]{:S(2)}) %collective-permute-start.2) | collective-permute-done | bytes 40992 | tf_op jit(solution)/shard_map/ppermute | solution.py:53
  20.2 0.0 collective-permute-done.4.block_ref
  20.2 0.0 collective-permute-done.5.raw_ref
  20.2 1.0 %shard_map.43.refs_0_ = f32[1024,128]{1,0:T(8,128)S(1)} custom-call(s32[4,4]{1,0:T(4,128)S(1)} %copy-done.1, f32[80,128]{1,0:T(8,128)S(1)} %collective-permute-done.2.u_ref, f32[1024,128]{1,0:T(8,128)S(1)} %collective-permute-done.4.block_ref, f32[1024,256]{1,0:T(8,128)S(1)} %collective-permute-done.5.raw_ref), custom_call_target="tpu_custom_call" | custom-call | tf_op jit(solution)/shard_map/pallas_call | solution.py:224
  21.2 3.1 %collective-permute-done.3.w_ref = f32[1104,128]{1,0:T(8,128)S(1)} collective-permute-done((f32[1104,128]{1,0:T(8,128)S(1)}, f32[1104,128]{1,0:T(8,128)S(1)}, u32[]{:S(2)}, u32[]{:S(2)}) %collective-permute-start.3) | collective-permute-done | bytes 565280 | tf_op jit(solution)/shard_map/ppermute | solution.py:53
  24.3 0.8 shard_map.44
  25.1 0.7 collective-permute-start.11
  25.8 7.4 %collective-permute-start.8 = (f32[128,128]{1,0:T(8,128)S(1)}, f32[128,128]{1,0:T(8,128)S(1)}, u32[]{:S(2)}, u32[]{:S(2)}) collective-permute-start(f32[128,128]{1,0:T(8,128)S(1)} %get-tuple-element.23.refs_0_), channel_id=1, source_target_pairs={{0,6},{4,2},{2,4},{6,0},{1,7},{5,3},{3,5},{7,1},{8,14},{12,10},{10... | collective-permute-start | bytes 196616 | tf_op jit(solution)/shard_map/ppermute | solution.py:53
  33.2 0.5 collective-permute-start.7
  33.8 0.1 collective-permute-start.6
  33.9 1.6 %collective-permute-done.8.refs_3_ = f32[128,128]{1,0:T(8,128)S(1)} collective-permute-done((f32[128,128]{1,0:T(8,128)S(1)}, f32[128,128]{1,0:T(8,128)S(1)}, u32[]{:S(2)}, u32[]{:S(2)}) %collective-permute-start.8) | collective-permute-done | bytes 65568 | tf_op jit(solution)/shard_map/ppermute | solution.py:53
  35.5 2.4 %collective-permute-done.7.refs_2_ = f32[128,128]{1,0:T(8,128)S(1)} collective-permute-done((f32[128,128]{1,0:T(8,128)S(1)}, f32[128,128]{1,0:T(8,128)S(1)}, u32[]{:S(2)}, u32[]{:S(2)}) %collective-permute-start.7) | collective-permute-done | bytes 65568 | tf_op jit(solution)/shard_map/ppermute | solution.py:53
  37.8 0.2 collective-permute-done.6.refs_1_
  38.0 2.0 %shard_map.45 = (f32[1120,128]{1,0:T(8,128)S(1)}, f32[96,128]{1,0:T(8,128)S(1)}) custom-call(s32[4,4]{1,0:T(4,128)S(1)} %copy-done.1, f32[128,128]{1,0:T(8,128)S(1)} %get-tuple-element.23.refs_0_, f32[128,128]{1,0:T(8,128)S(1)} %collective-permute-done.6.refs_1_, f32[128,128]{1,0:T(8,128)S(1)} %collective-permute-done.7.refs_2_, ...), custom_call_target="tpu_custom_call" | custom-call | tf_op jit(solution)/shard_map/pallas_call | solution.py:224
  40.0 1.5 %collective-permute-start.9 = (f32[1120,128]{1,0:T(8,128)S(1)}, f32[1120,128]{1,0:T(8,128)S(1)}, u32[]{:S(2)}, u32[]{:S(2)}) collective-permute-start(f32[1120,128]{1,0:T(8,128)S(1)} %get-tuple-element.27), channel_id=1, source_target_pairs={{0,1},{4,5},{2,3},{6,7},{1,0},{5,4},{3,2},{7,6},{8,9},{12,13},{10,... | collective-permute-start | bytes 1720328 | tf_op jit(solution)/shard_map/ppermute | solution.py:53
  41.6 1.5 %collective-permute-start.10 = (f32[96,128]{1,0:T(8,128)S(1)}, f32[96,128]{1,0:T(8,128)S(1)}, u32[]{:S(2)}, u32[]{:S(2)}) collective-permute-start(f32[96,128]{1,0:T(8,128)S(1)} %get-tuple-element.28.own_ref), channel_id=1, source_target_pairs={{0,2},{4,6},{2,0},{6,4},{1,8},{5,12},{3,10},{7,14},{8,1},{12,5},{1... | collective-permute-start | bytes 147464 | tf_op jit(solution)/shard_map/ppermute | solution.py:53
  43.0 2.6 %collective-permute-done.10.w_ref = f32[96,128]{1,0:T(8,128)S(1)} collective-permute-done((f32[96,128]{1,0:T(8,128)S(1)}, f32[96,128]{1,0:T(8,128)S(1)}, u32[]{:S(2)}, u32[]{:S(2)}) %collective-permute-start.10) | collective-permute-done | bytes 49184 | tf_op jit(solution)/shard_map/ppermute | solution.py:53
  45.6 0.0 collective-permute-done.9.u_ref
  45.6 2.4 %shard_map.46 = (f32[1024,256]{1,0:T(8,128)S(1)}, f32[128,128]{1,0:T(8,128)S(1)}, f32[96,128]{1,0:T(8,128)S(1)}, f32[96,128]{1,0:T(8,128)S(1)}) custom-call(s32[4,4]{1,0:T(4,128)S(1)} %copy-done.1, f32[1120,128]{1,0:T(8,128)S(1)} %collective-permute-done.9.u_ref, f32[96,128]{1,0:T(8,128)S(1)} %collective-permute-done.10.w_ref, ...), custom_call_target="tpu_custom_call" | custom-call | tf_op jit(solution)/shard_map/pallas_call | solution.py:224
  48.1 2.3 %collective-permute-start.14 = (f32[128,128]{1,0:T(8,128)S(1)}, f32[128,128]{1,0:T(8,128)S(1)}, u32[]{:S(2)}, u32[]{:S(2)}) collective-permute-start(f32[128,128]{1,0:T(8,128)S(1)} %get-tuple-element.29.refs_0_), channel_id=1, source_target_pairs={{0,6},{4,2},{2,4},{6,0},{1,7},{5,3},{3,5},{7,1},{8,14},{12,10},{10... | collective-permute-start | bytes 196616 | tf_op jit(solution)/shard_map/ppermute | solution.py:53
  50.4 0.5 collective-permute-start.13
  50.9 0.7 collective-permute-start.12
  51.7 1.7 %collective-permute-done.14.refs_3_ = f32[128,128]{1,0:T(8,128)S(1)} collective-permute-done((f32[128,128]{1,0:T(8,128)S(1)}, f32[128,128]{1,0:T(8,128)S(1)}, u32[]{:S(2)}, u32[]{:S(2)}) %collective-permute-start.14) | collective-permute-done | bytes 65568 | tf_op jit(solution)/shard_map/ppermute | solution.py:53
  53.3 2.0 %collective-permute-done.13.refs_2_ = f32[128,128]{1,0:T(8,128)S(1)} collective-permute-done((f32[128,128]{1,0:T(8,128)S(1)}, f32[128,128]{1,0:T(8,128)S(1)}, u32[]{:S(2)}, u32[]{:S(2)}) %collective-permute-start.13) | collective-permute-done | bytes 65568 | tf_op jit(solution)/shard_map/ppermute | solution.py:53
  55.4 0.0 collective-permute-done.12.refs_1_
  55.4 2.1 %shard_map.47 = (f32[1152,128]{1,0:T(8,128)S(1)}, f32[1152,128]{1,0:T(8,128)S(1)}) custom-call(s32[4,4]{1,0:T(4,128)S(1)} %copy-done.1, f32[128,128]{1,0:T(8,128)S(1)} %get-tuple-element.29.refs_0_, f32[128,128]{1,0:T(8,128)S(1)} %collective-permute-done.12.refs_1_, f32[128,128]{1,0:T(8,128)S(1)} %collective-permute-done.13.refs_2_, ...), custom_call_target="tpu_custom_call" | custom-call | tf_op jit(solution)/shard_map/pallas_call | solution.py:224
  57.5 1.6 %collective-permute-start.15 = (f32[1152,128]{1,0:T(8,128)S(1)}, f32[1152,128]{1,0:T(8,128)S(1)}, u32[]{:S(2)}, u32[]{:S(2)}) collective-permute-start(f32[1152,128]{1,0:T(8,128)S(1)} %get-tuple-element.33), channel_id=1, source_target_pairs={{0,4},{4,5},{2,6},{6,7},{1,0},{5,1},{3,2},{7,3},{8,12},{12,13},{10... | collective-permute-start | bytes 1769480 | tf_op jit(solution)/shard_map/ppermute | solution.py:53
  59.0 1.5 %collective-permute-start.16 = (f32[1152,128]{1,0:T(8,128)S(1)}, f32[1152,128]{1,0:T(8,128)S(1)}, u32[]{:S(2)}, u32[]{:S(2)}) collective-permute-start(f32[1152,128]{1,0:T(8,128)S(1)} %get-tuple-element.34.own_ref), channel_id=1, source_target_pairs={{0,2},{4,1},{2,0},{6,3},{1,8},{5,9},{3,10},{7,11},{8,4},{12,5},{10... | collective-permute-start | bytes 1769480 | tf_op jit(solution)/shard_map/ppermute | solution.py:53
  60.6 12.2 %collective-permute-done.15.u_ref = f32[1152,128]{1,0:T(8,128)S(1)} collective-permute-done((f32[1152,128]{1,0:T(8,128)S(1)}, f32[1152,128]{1,0:T(8,128)S(1)}, u32[]{:S(2)}, u32[]{:S(2)}) %collective-permute-start.15) | collective-permute-done | bytes 589856 | tf_op jit(solution)/shard_map/ppermute | solution.py:53
  72.8 0.8 shard_map.48
  73.6 0.2 collective-permute-start.17
  73.8 1.1 %collective-permute-done.17 = f32[128,128]{1,0:T(8,128)S(1)} collective-permute-done((f32[128,128]{1,0:T(8,128)S(1)}, f32[128,128]{1,0:T(8,128)S(1)}, u32[]{:S(2)}, u32[]{:S(2)}) %collective-permute-start.17) | collective-permute-done | bytes 65568 | tf_op jit(solution)/shard_map/ppermute | solution.py:53
  74.9 1.6 %collective-permute-start.18 = (f32[128,128]{1,0:T(8,128)S(1)}, f32[128,128]{1,0:T(8,128)S(1)}, u32[]{:S(2)}, u32[]{:S(2)}) collective-permute-start(f32[128,128]{1,0:T(8,128)S(1)} %add.7.refs_0_), channel_id=1, source_target_pairs={{0,2},{1,3},{2,0},{3,1},{4,6},{5,7},{6,4},{7,5},{8,10},{9,11},{10,... | collective-permute-start | bytes 196616 | tf_op jit(solution)/shard_map/ppermute | solution.py:53
  76.5 0.1 shard_map.49
  76.7 2.3 %shard_map.50.refs_5_ = f32[512,256]{1,0:T(8,128)S(1)} custom-call(s32[4,4]{1,0:T(4,128)S(1)} %copy-done.1, f32[128,128]{1,0:T(8,128)S(1)} %get-tuple-element.35.mu_ref.refs_2_, f32[128,128]{1,0:T(8,128)S(1)} %get-tuple-element.36.mw_ref.refs_3_), custom_call_target="tpu_custom_call" | custom-call | tf_op jit(solution)/shard_map/pallas_call | solution.py:224
  79.0 0.3 collective-permute-done.18.refs_1_
  79.3 3.3 %shard_map.51 = (f32[1024,256]{1,0:T(8,128)}, f32[512,256]{1,0:T(8,128)}) custom-call(s32[4,4]{1,0:T(4,128)S(1)} %copy-done.1, f32[128,128]{1,0:T(8,128)S(1)} %add.7.refs_0_, f32[128,128]{1,0:T(8,128)S(1)} %collective-permute-done.18.refs_1_, f32[128,128]{1,0:T(8,128)S(1)} %get-tuple-element.35.mu_ref.refs_2_, ...), custom_call_target="tpu_custom_call" | custom-call | tf_op jit(solution)/shard_map/pallas_call | solution.py:224
  (7 shorter events, 0.0 us)
Async XLA Ops:
  0.6 19.5 %collective-permute-start.5 = (f32[1024,256]{1,0:T(8,128)}, f32[1024,256]{1,0:T(8,128)S(1)}, u32[]{:S(2)}, u32[]{:S(2)}) collective-permute-start(f32[1024,256]{1,0:T(8,128)} %refs_2_.1), channel_id=1, source_target_pairs={{0,1},{1,5},{2,3},{3,7},{4,0},{5,4},{6,2},{7,6},{8,9},{9,13},{10,1... | collective-permute-start | bytes 3145736 | tf_op jit(solution)/shard_map/ppermute | solution.py:53
  1.1 1.2 %copy-start = (f32[1024,256]{1,0:T(8,128)S(1)}, f32[1024,256]{1,0:T(8,128)}, u32[]{:S(2)}) copy-start(f32[1024,256]{1,0:T(8,128)} %refs_2_.1) | copy-start | bytes 3145732
  3.5 9.1 %copy-start.1 = (s32[4,4]{1,0:T(4,128)S(1)}, s32[4,4]{1,0:T(4,128)}, u32[]{:S(2)}) copy-start(s32[4,4]{1,0:T(4,128)} %offs_ref.15) | copy-start | bytes 196
  3.5 3.2 %collective-permute-start = (f32[264,128]{1,0:T(8,128)S(1)}, f32[264,128]{1,0:T(8,128)S(1)}, u32[]{:S(2)}, u32[]{:S(2)}) collective-permute-start(f32[264,128]{1,0:T(8,128)S(1)} %shard_map.41), channel_id=1, source_target_pairs={{0,1},{1,0},{2,3},{3,2},{4,5},{5,4},{6,7},{7,6},{8,9},{9,8},{10,11... | collective-permute-start | bytes 405512 | tf_op jit(solution)/shard_map/ppermute | solution.py:53
  6.7 5.9 %collective-permute-start.1 = (f32[264,128]{1,0:T(8,128)S(1)}, f32[264,128]{1,0:T(8,128)S(1)}, u32[]{:S(2)}, u32[]{:S(2)}) collective-permute-start(f32[264,128]{1,0:T(8,128)S(1)} %add.6.refs_0_), channel_id=1, source_target_pairs={{0,2},{1,3},{2,0},{3,1},{4,6},{5,7},{6,4},{7,5},{8,10},{9,11},{10,... | collective-permute-start | bytes 405512 | tf_op jit(solution)/shard_map/ppermute | solution.py:53
  14.6 9.7 %collective-permute-start.3 = (f32[1104,128]{1,0:T(8,128)S(1)}, f32[1104,128]{1,0:T(8,128)S(1)}, u32[]{:S(2)}, u32[]{:S(2)}) collective-permute-start(f32[1104,128]{1,0:T(8,128)S(1)} %get-tuple-element.21.own_ref), channel_id=1, source_target_pairs={{0,2},{1,4},{2,0},{3,6},{4,8},{5,12},{6,10},{7,14},{8,1},{9,5},{10... | collective-permute-start | bytes 1695752 | tf_op jit(solution)/shard_map/ppermute | solution.py:53
  16.2 4.0 %collective-permute-start.4 = (f32[1024,128]{1,0:T(8,128)S(1)}, f32[1024,128]{1,0:T(8,128)S(1)}, u32[]{:S(2)}, u32[]{:S(2)}) collective-permute-start(f32[1024,128]{1,0:T(8,128)S(1)} %get-tuple-element.22), channel_id=1, source_target_pairs={{0,1},{1,0},{2,3},{3,2},{4,5},{5,4},{6,7},{7,6},{8,9},{9,8},{10,11... | collective-permute-start | bytes 1572872 | tf_op jit(solution)/shard_map/ppermute | solution.py:53
  16.2 4.0 %collective-permute-start.2 = (f32[80,128]{1,0:T(8,128)S(1)}, f32[80,128]{1,0:T(8,128)S(1)}, u32[]{:S(2)}, u32[]{:S(2)}) collective-permute-start(f32[80,128]{1,0:T(8,128)S(1)} %get-tuple-element.20), channel_id=1, source_target_pairs={{0,1},{1,5},{2,3},{3,7},{4,0},{5,4},{6,2},{7,6},{8,9},{9,13},{10,1... | collective-permute-start | bytes 122888 | tf_op jit(solution)/shard_map/ppermute | solution.py:53
  25.1 20.6 %collective-permute-start.11 = (f32[1024,256]{1,0:T(8,128)S(1)}, f32[1024,256]{1,0:T(8,128)S(1)}, u32[]{:S(2)}, u32[]{:S(2)}) collective-permute-start(f32[1024,256]{1,0:T(8,128)S(1)} %get-tuple-element.26.refs_6_), channel_id=1, source_target_pairs={{0,0},{4,4},{2,2},{6,6},{1,8},{5,12},{3,10},{7,14},{8,1},{12,5},{1... | collective-permute-start | bytes 3145736 | tf_op jit(solution)/shard_map/ppermute | solution.py:53
  25.8 9.6 %collective-permute-start.8 = (f32[128,128]{1,0:T(8,128)S(1)}, f32[128,128]{1,0:T(8,128)S(1)}, u32[]{:S(2)}, u32[]{:S(2)}) collective-permute-start(f32[128,128]{1,0:T(8,128)S(1)} %get-tuple-element.23.refs_0_), channel_id=1, source_target_pairs={{0,6},{4,2},{2,4},{6,0},{1,7},{5,3},{3,5},{7,1},{8,14},{12,10},{10... | collective-permute-start | bytes 196616 | tf_op jit(solution)/shard_map/ppermute | solution.py:53
  33.2 4.6 %collective-permute-start.7 = (f32[128,128]{1,0:T(8,128)S(1)}, f32[128,128]{1,0:T(8,128)S(1)}, u32[]{:S(2)}, u32[]{:S(2)}) collective-permute-start(f32[128,128]{1,0:T(8,128)S(1)} %get-tuple-element.23.refs_0_), channel_id=1, source_target_pairs={{0,2},{4,6},{2,0},{6,4},{1,3},{5,7},{3,1},{7,5},{8,10},{12,14},{10... | collective-permute-start | bytes 196616 | tf_op jit(solution)/shard_map/ppermute | solution.py:53
  33.8 4.3 %collective-permute-start.6 = (f32[128,128]{1,0:T(8,128)S(1)}, f32[128,128]{1,0:T(8,128)S(1)}, u32[]{:S(2)}, u32[]{:S(2)}) collective-permute-start(f32[128,128]{1,0:T(8,128)S(1)} %get-tuple-element.23.refs_0_), channel_id=1, source_target_pairs={{0,4},{4,0},{2,6},{6,2},{1,5},{5,1},{3,7},{7,3},{8,12},{12,8},{10,... | collective-permute-start | bytes 196616 | tf_op jit(solution)/shard_map/ppermute | solution.py:53
  40.0 5.6 %collective-permute-start.9 = (f32[1120,128]{1,0:T(8,128)S(1)}, f32[1120,128]{1,0:T(8,128)S(1)}, u32[]{:S(2)}, u32[]{:S(2)}) collective-permute-start(f32[1120,128]{1,0:T(8,128)S(1)} %get-tuple-element.27), channel_id=1, source_target_pairs={{0,1},{4,5},{2,3},{6,7},{1,0},{5,4},{3,2},{7,6},{8,9},{12,13},{10,... | collective-permute-start | bytes 1720328 | tf_op jit(solution)/shard_map/ppermute | solution.py:53
  41.6 4.1 %collective-permute-start.10 = (f32[96,128]{1,0:T(8,128)S(1)}, f32[96,128]{1,0:T(8,128)S(1)}, u32[]{:S(2)}, u32[]{:S(2)}) collective-permute-start(f32[96,128]{1,0:T(8,128)S(1)} %get-tuple-element.28.own_ref), channel_id=1, source_target_pairs={{0,2},{4,6},{2,0},{6,4},{1,8},{5,12},{3,10},{7,14},{8,1},{12,5},{1... | collective-permute-start | bytes 147464 | tf_op jit(solution)/shard_map/ppermute | solution.py:53
  48.1 5.2 %collective-permute-start.14 = (f32[128,128]{1,0:T(8,128)S(1)}, f32[128,128]{1,0:T(8,128)S(1)}, u32[]{:S(2)}, u32[]{:S(2)}) collective-permute-start(f32[128,128]{1,0:T(8,128)S(1)} %get-tuple-element.29.refs_0_), channel_id=1, source_target_pairs={{0,6},{4,2},{2,4},{6,0},{1,7},{5,3},{3,5},{7,1},{8,14},{12,10},{10... | collective-permute-start | bytes 196616 | tf_op jit(solution)/shard_map/ppermute | solution.py:53
  50.4 5.0 %collective-permute-start.13 = (f32[128,128]{1,0:T(8,128)S(1)}, f32[128,128]{1,0:T(8,128)S(1)}, u32[]{:S(2)}, u32[]{:S(2)}) collective-permute-start(f32[128,128]{1,0:T(8,128)S(1)} %get-tuple-element.29.refs_0_), channel_id=1, source_target_pairs={{0,2},{4,6},{2,0},{6,4},{1,3},{5,7},{3,1},{7,5},{8,10},{12,14},{10... | collective-permute-start | bytes 196616 | tf_op jit(solution)/shard_map/ppermute | solution.py:53
  50.9 4.4 %collective-permute-start.12 = (f32[128,128]{1,0:T(8,128)S(1)}, f32[128,128]{1,0:T(8,128)S(1)}, u32[]{:S(2)}, u32[]{:S(2)}) collective-permute-start(f32[128,128]{1,0:T(8,128)S(1)} %get-tuple-element.29.refs_0_), channel_id=1, source_target_pairs={{0,4},{4,0},{2,6},{6,2},{1,5},{5,1},{3,7},{7,3},{8,12},{12,8},{10,... | collective-permute-start | bytes 196616 | tf_op jit(solution)/shard_map/ppermute | solution.py:53
  57.5 15.3 %collective-permute-start.15 = (f32[1152,128]{1,0:T(8,128)S(1)}, f32[1152,128]{1,0:T(8,128)S(1)}, u32[]{:S(2)}, u32[]{:S(2)}) collective-permute-start(f32[1152,128]{1,0:T(8,128)S(1)} %get-tuple-element.33), channel_id=1, source_target_pairs={{0,4},{4,5},{2,6},{6,7},{1,0},{5,1},{3,2},{7,3},{8,12},{12,13},{10... | collective-permute-start | bytes 1769480 | tf_op jit(solution)/shard_map/ppermute | solution.py:53
  59.0 13.7 %collective-permute-start.16 = (f32[1152,128]{1,0:T(8,128)S(1)}, f32[1152,128]{1,0:T(8,128)S(1)}, u32[]{:S(2)}, u32[]{:S(2)}) collective-permute-start(f32[1152,128]{1,0:T(8,128)S(1)} %get-tuple-element.34.own_ref), channel_id=1, source_target_pairs={{0,2},{4,1},{2,0},{6,3},{1,8},{5,9},{3,10},{7,11},{8,4},{12,5},{10... | collective-permute-start | bytes 1769480 | tf_op jit(solution)/shard_map/ppermute | solution.py:53
  73.6 1.3 %collective-permute-start.17 = (f32[128,128]{1,0:T(8,128)S(1)}, f32[128,128]{1,0:T(8,128)S(1)}, u32[]{:S(2)}, u32[]{:S(2)}) collective-permute-start(f32[128,128]{1,0:T(8,128)S(1)} %shard_map.48), channel_id=1, source_target_pairs={{0,1},{1,0},{2,3},{3,2},{4,5},{5,4},{6,7},{7,6},{8,9},{9,8},{10,11... | collective-permute-start | bytes 196616 | tf_op jit(solution)/shard_map/ppermute | solution.py:53
  74.9 4.3 %collective-permute-start.18 = (f32[128,128]{1,0:T(8,128)S(1)}, f32[128,128]{1,0:T(8,128)S(1)}, u32[]{:S(2)}, u32[]{:S(2)}) collective-permute-start(f32[128,128]{1,0:T(8,128)S(1)} %add.7.refs_0_), channel_id=1, source_target_pairs={{0,2},{1,3},{2,0},{3,1},{4,6},{5,7},{6,4},{7,5},{8,10},{9,11},{10,... | collective-permute-start | bytes 196616 | tf_op jit(solution)/shard_map/ppermute | solution.py:53

commit v5 on v4

--- a/solution.py
+++ b/solution.py
@@ -77,18 +77,19 @@
 
 def solve(first, across, second, offs):
     mask = eye_mask()
+    distance = (index((B, B), 1) - index((B, B), 0)) & (B - 1)
     angles = []
     turns = identity_halves()
+    a, d = diagonal(mask, first), diagonal(mask, second)
     held = 0
     for r in range(ROUNDS):
-        turn = (held - offs[r]) & (B - 1)
+        turn, ahead = (held - offs[r]) & (B - 1), (offs[r] - held) & (B - 1)
         held = offs[r]
+        c0 = pltpu.roll(diagonal(distance == ahead, across), turn, 1)
+        d = pltpu.roll(d, turn, 1)
         across = pltpu.roll(across, turn, 1)
         second = pltpu.roll(pltpu.roll(second, turn, 1), turn, 0)
         turns = [(top, pltpu.roll(low, turn, 1)) for top, low in turns]
-        a = diagonal(mask, first)
-        d = diagonal(mask, second)
-        c0 = diagonal(mask, across)
         h = 0.5 * (d - a)
         radius = jnp.sqrt(h * h + c0 * c0)
         sg = jnp.where(h >= 0, 1.0, -1.0)
@@ -105,6 +106,7 @@
         first = cc * first1 + sc * below1
         across = cc * across1 + sc * second1
         second = cc * second1 - sc * across1
+        a, d = c * (a * c + c0 * s) + s * (c0 * c + d * s), c * (d * c - c0 * s) - s * (c0 * c - a * s)
         turns = [(c * top + s * low, c * low - s * top) for top, low in turns]
     second = pltpu.roll(pltpu.roll(second, held, 1), held, 0)
     turns = [(top, pltpu.roll(low, held, 1)) for top, low in turns]
@@ -208,13 +210,14 @@
 
 
 def transposed_dot(left, right):
-    return lax.dot_general(
-        left,
-        right,
-        (((0,), (0,)), ((), ())),
-        precision=lax.Precision.HIGHEST,
-        preferred_element_type=jnp.float32,
-    )
+    lh, ll = split(left)
+    rh, rl = split(right)
+
+    def dot(a, b):
+        dims = (((0,), (0,)), ((), ()))
+        return lax.dot_general(a, b, dims, preferred_element_type=jnp.float32)
+
+    return (dot(ll, rh) + dot(lh, rl)) + dot(lh, rh)
 
 
 JOINED, RAW, EITHER = range(3)
@@ -237,13 +240,22 @@
         self.slot, self.part = layout(pair, row)
         self.odd = (self.slot & 1) == 1
         self.edge = jnp.logical_or(self.slot == 0, self.slot == self.pairs - 1)
+        self.gives_first = (
+            jnp.logical_and(jnp.logical_not(self.odd), self.slot != 0),
+            jnp.logical_or(self.odd, self.slot == 0),
+        )
         self.same = ((pair ^ row) & 1) == 0
         self.stays = jnp.logical_and(self.edge, self.same)
 
 
 def whole_gram_kernel(x_ref, out_ref):
-    gram = transposed_dot(x_ref[...], x_ref[...])
-    packed, diag = pack_two(gram[:B, :B], gram[B:, B:])
+    x = x_ref[...]
+    gram = transposed_dot(x, x)
+    squares = jnp.sum(x * x, axis=0, keepdims=True)
+    mask = eye_mask()
+    first = jnp.where(mask, jnp.broadcast_to(squares[:, :B], (B, B)), gram[:B, :B])
+    second = jnp.where(mask, jnp.broadcast_to(squares[:, B:], (B, B)), gram[B:, B:])
+    packed, diag = pack_two(first, second)
     out_ref[:B, :] = gram[:B, B:]
     out_ref[B : 2 * B, :] = packed
     out_ref[2 * B :, :] = diag
@@ -253,8 +265,8 @@
     return call(whole_gram_kernel, [(2 * B + 8, B)], (x,))[0]
 
 
-def base_of(way, rows):
-    return rows if way == JOINED else 0
+def base_of(way, rows, message):
+    return rows + (message.shape[0] if way == JOINED else 0)
 
 
 def older(odd, mu, mw):
@@ -267,67 +279,84 @@
     return solve(jnp.where(odd, gu, gw), across, jnp.where(odd, gw, gu), offs)
 
 
-def turn_kernel(step, goes, layout, count, offs_ref, *refs):
-    parts, refs = refs[:count], list(refs[count:])
+def solve_kernel(step, layout, count, offs_ref, *refs):
+    parts, refs = refs[:count], refs[count:]
     place = Place(layout)
     odd = place.odd
     offs = step_offsets(offs_ref, step)
     if step == 0:
+        rotation_ref, *messages = refs
         gram = tree_sum([p[...] for p in parts])
         first, second = unpack_two(gram[B : 2 * B], gram[2 * B : 2 * B + 1])
         angles, rotation, first, second = solve(first, gram[:B], second, offs)
         past = ()
     else:
-        mu, mw = refs.pop(0)[...], refs.pop(0)[...]
-        across = tree_sum([p[...] for p in parts])
-        angles, rotation, first, second = cross_solve(across, odd, mu, mw, offs)
+        mu_ref, mw_ref, rotation_ref, *messages = refs
+        mu, mw = mu_ref[...], mw_ref[...]
+        gram = tree_sum([p[...] for p in parts])
+        angles, rotation, first, second = cross_solve(gram, odd, mu, mw, offs)
         past = older(odd, mu, mw)
-    x_ref = refs.pop(0)
-    rows = x_ref.shape[0]
-    swap = jnp.logical_and(jnp.logical_not(odd), place.slot != 0)
-    blocks = []
-    for way, near in zip(goes, (True, False)):
-        message = refs.pop(0)
-        base = base_of(way, rows)
-        gives_first = swap if near else jnp.logical_not(swap)
-        message[base : base + PACKED, :] = pack(jnp.where(gives_first, first, second))
-        at = base + PACKED
-        write_record(message, at, angles)
-        at += RECORD
+    rotation_ref[...] = rotation
+    packed = pack(first), pack(second)
+    for message, gives_first in zip(messages, place.gives_first):
+        message[:PACKED, :] = jnp.where(gives_first, *packed)
+        write_record(message, PACKED, angles)
+        at = PACKED + RECORD
         for history in past:
             message[at : at + history.shape[0], :] = history
             at += history.shape[0]
-        if way != RAW:
-            blocks.append((message if way == JOINED else refs.pop(0), gives_first))
-    if len(blocks) == 1:
-        (block_ref, gives_first), = blocks
-        half = jnp.where(gives_first, rotation[:, :B], rotation[:, B:])
-        block_ref[:rows, :] = product(x_ref[...], half)
-        return
-    x = product(x_ref[...], rotation)
-    for block_ref, gives_first in blocks:
-
-        @pl.when(gives_first)
-        def _():
-            block_ref[:rows, :] = x[:, :B]
-
-        @pl.when(jnp.logical_not(gives_first))
-        def _():
-            block_ref[:rows, :] = x[:, B:]
-
-
-def turn(step, goes, layout, offsets, parts, messages, x):
-    rows = x.shape[0]
+
+
+def solved(step, layout, offsets, parts, messages=()):
     small = PACKED + RECORD
     if step:
         small += 2 * (messages[0].shape[0] - PACKED)
-    shapes = []
-    for way in goes:
-        shapes.append((base_of(way, rows) + small, B))
-        if way == EITHER:
-            shapes.append((rows, B))
-    kernel = functools.partial(turn_kernel, step, goes, layout, len(parts))
-    return call(kernel, shapes, (offsets, *parts, *messages, x))
+    kernel = functools.partial(solve_kernel, step, layout, len(parts))
+    shapes = [(2 * B, 2 * B), (small, B), (small, B)]
+    return call(kernel, shapes, (offsets, *parts, *messages))
+
+
+def turn_kernel(ways, layout, ordered, rotation_ref, near_ref, far_ref, *refs):
+    count = 1 if ordered else 2
+    xs, outs = refs[:count], list(refs[count:])
+    place = Place(layout)
+    rows = outs[0].shape[0] - base_excess(ways, near_ref)
+    x = jnp.concatenate([x_ref[:rows, :] for x_ref in xs], axis=1)
+    rotation = rotation_ref[...]
+    if not ordered:
+        swapped = jnp.concatenate([rotation[B:], rotation[:B]], axis=0)
+        rotation = jnp.where(place.odd, rotation, swapped)
+    if len(outs) == 1:
+        rotation = jnp.where(place.gives_first[0], rotation[:, :B], rotation[:, B:])
+    x = product(x, rotation)
+    messages = [m for m, way in zip((near_ref, far_ref), ways) if way != RAW]
+    sides = [g for g, way in zip(place.gives_first, ways) if way != RAW]
+    kept = [way for way in ways if way != RAW]
+    for out, message, gives_first, way in zip(outs, messages, sides, kept):
+        if way == JOINED:
+            out[rows:, :] = message[...]
+        if len(outs) == 1:
+            out[:rows, :] = x
+            continue
+
+        @pl.when(gives_first)
+        def _():
+            out[:rows, :] = x[:, :B]
+
+        @pl.when(jnp.logical_not(gives_first))
+        def _():
+            out[:rows, :] = x[:, B:]
+
+
+def base_excess(ways, message):
+    way = next(w for w in ways if w != RAW)
+    return message.shape[0] if way == JOINED else 0
+
+
+def turned(rows, ways, layout, rotation, near, far, *xs):
+    shapes = [(base_of(way, rows, near), B) for way in ways if way != RAW]
+    kernel = functools.partial(turn_kernel, ways, layout, len(xs) == 1)
+    return call(kernel, shapes, (rotation, near, far, *xs))
 
 
 def half_rotation(angles, offs, take_first):
@@ -335,15 +364,11 @@
     return jnp.concatenate([jnp.where(take_first, top, low) for top, low in halves], axis=0)
 
 
-def arrive_kernel(step, came, source, offs_ref, u_ref, w_ref, own_ref, *refs):
-    *refs, x_ref, gram_ref, mu_ref, mw_ref = refs
+def arrive_kernel(block_ref, u_ref, w_ref, own_ref, x_ref, gram_ref, mw_ref):
     rows = x_ref.shape[0]
     place = Place(crossed)
-    odd = place.odd
-    own = place.edge if source is crossed else place.stays
-    u_base, w_base = (base_of(way, rows) for way in came)
-    mu_ref[...] = u_ref[u_base:, :]
-    mw_ref[...] = jnp.where(own, own_ref[w_base:, :], w_ref[w_base:, :])
+    own = place.stays
+    mw_ref[...] = jnp.where(own, own_ref[rows:, :], w_ref[rows:, :])
 
     def put(first, block):
         @pl.when(first)
@@ -354,26 +379,48 @@
         def _():
             x_ref[:, B:] = block
 
-    if came[0] == JOINED:
-        put(odd, u_ref[:rows, :])
-    else:
-        put(odd, refs[0][...])
-    if came[1] == RAW:
-        takes_first = jnp.logical_or(jnp.logical_not(odd), place.slot == place.pairs - 1)
-        offs = step_offsets(offs_ref, step)
-        angles = read_record(mw_ref[PACKED : PACKED + RECORD, :])
-        put(jnp.logical_not(odd), product(refs[0][...], half_rotation(angles, offs, takes_first)))
-    else:
-
-        @pl.when(own)
-        def _():
-            put(jnp.logical_not(odd), own_ref[:rows, :])
-
-        @pl.when(jnp.logical_not(own))
-        def _():
-            put(jnp.logical_not(odd), w_ref[:rows, :])
+    put(place.odd, block_ref[...])
+    even = jnp.logical_not(place.odd)
+
+    @pl.when(own)
+    def _():
+        put(even, own_ref[:rows, :])
+
+    @pl.when(jnp.logical_not(own))
+    def _():
+        put(even, w_ref[:rows, :])
 
     gram_ref[...] = transposed_dot(x_ref[:, :B], x_ref[:, B:])
+
+
+def arrive(block, u, w, own):
+    rows = block.shape[0]
+    shapes = [(rows, 2 * B), (B, B), u.shape]
+    return call(arrive_kernel, shapes, (block, u, w, own))
+
+
+def arrive_raw_kernel(step, offs_ref, u_ref, w_ref, own_ref, raw_ref, *refs):
+    block_ref, gram_ref, mu_ref, mw_ref = refs
+    rows = raw_ref.shape[0]
+    place = Place(crossed)
+    own = place.edge
+    mu_ref[...] = u_ref[rows:, :]
+    mw_ref[...] = jnp.where(own, own_ref[...], w_ref[...])
+    at = slice(PACKED, PACKED + RECORD)
+    angles = read_record(jnp.where(own, own_ref[at, :], w_ref[at, :]))
+    takes_first = jnp.logical_or(jnp.logical_not(place.odd), place.slot == place.pairs - 1)
+    half = half_rotation(angles, step_offsets(offs_ref, step), takes_first)
+    block = product(raw_ref[...], half)
+    block_ref[...] = block
+    gram = transposed_dot(u_ref[:rows, :], block)
+    gram_ref[...] = jnp.where(place.odd, gram, gram.T)
+
+
+def arrive_raw(step, offsets, u, w, own, raw):
+    rows = raw.shape[0]
+    kernel = functools.partial(arrive_raw_kernel, step)
+    shapes = [(rows, B), (B, B), w.shape, w.shape]
+    return call(kernel, shapes, (offsets, u, w, own, raw))
 
 
 def ready_kernel(step, offs_ref, u_ref, block_ref, raw_ref, out_ref):
@@ -394,13 +441,6 @@
 def ready(step, offsets, u, block, raw):
     kernel = functools.partial(ready_kernel, step)
     return call(kernel, [block.shape], (offsets, u, block, raw))[0]
-
-
-def arrive(step, rows, came, source, offsets, messages, raw=()):
-    kernel = functools.partial(arrive_kernel, step, came, source)
-    small = messages[0].shape[0] - base_of(came[0], rows)
-    shapes = [(rows, 2 * B), (B, B), (small, B), (small, B)]
-    return call(kernel, shapes, (offsets, *messages, *raw))
 
 
 def last_gram_kernel(rows, u_ref, w_ref, own_ref, out_ref):
@@ -523,24 +563,25 @@
 
     raw = send(whitened, given, crossed, inner)
     terms = in_stages(whole_gram(whitened), given)
-    ways = (EITHER, JOINED)
-    near, block, far = turn(0, ways, given, offsets, terms, (), whitened)
+    rotation, near, far = solved(0, given, offsets, terms)
+    u = send(near, given, crossed, inner)
+    block, far = turned(rows, (EITHER, JOINED), given, rotation, near, far, whitened)
     w = send(far, given, crossed, outer)
-    u = send(near, given, crossed, inner)
     block = send(block, given, given, other_part(1))
     block = ready(0, offsets, u, block, raw)
-    x, cross, mu, mw = arrive(0, rows, ways, given, offsets, (u, w, far), (block,))
+    x, cross, mw = arrive(block, u, w, far)
 
     raw = send(x, crossed, crossed, outer, swap=False)
     terms = at_once(cross, crossed)
-    ways = (JOINED, RAW)
-    near, far = turn(1, ways, crossed, offsets, terms, (mu, mw), x)
+    rotation, near, far = solved(1, crossed, offsets, terms, (u, mw))
     w = send(far, crossed, crossed, outer)
+    (near,) = turned(rows, (JOINED, RAW), crossed, rotation, near, far, x)
     u = send(near, crossed, crossed, inner)
-    x, cross, mu, mw = arrive(1, rows, ways, crossed, offsets, (u, w, far), (raw,))
+    block, cross, mu, mw = arrive_raw(1, offsets, u, w, far, raw)
 
     terms = at_once(cross, crossed)
-    near, far = turn(2, (JOINED, JOINED), crossed, offsets, terms, (mu, mw), x)
+    rotation, near, far = solved(2, crossed, offsets, terms, (mu, mw))
+    near, far = turned(rows, (JOINED, JOINED), crossed, rotation, near, far, u, block)
     w = send(far, crossed, given, outer)
     u = send(near, crossed, given, inner)
     terms = in_stages(last_gram(rows, (u, w, far)), given)

time: 83.1 us -> 81.6 us (0.982)
  Pallas kernels: 18 us -> 16.3 us
    pallas_call x11 -> x14, Pallas kernels: 18 us -> 16.3 us  [call(): pl.pallas_call(kernel, out_shape=tuple((jax.ShapeDtypeStruct(shape, jnp.f...]
where the time goes in v5:
time: 81.6 us; the launch traced here: 81 us
  waiting for transfers between devices  36.1 us (44%)
  starting transfers between devices  26.5 us (32%)
  Pallas kernels  16.3 us (20%)
  local copies, waits for them, and re-layouts  1.23 us (2%)
    ppermute x19, waiting for transfers between devices, send(): return lax.ppermute(x, AXES, route(source, target, change, swap))  36.1 us
    ppermute x19, starting transfers between devices, send(): return lax.ppermute(x, AXES, route(source, target, change, swap))  26.5 us
    pallas_call x14, Pallas kernels, call(): pl.pallas_call(kernel, out_shape=tuple((jax.ShapeDtypeStruct(shape, jnp.f...  16.3 us
  transfers between devices with their start and end apart: 19, of which 13 were waited for; matrix products, arithmetic and copies ran while one was open for 0% of the time, Pallas kernels for 10%

profile of v5, /device:TPU:0, one launch (start us, length us, event | category | flops | bytes accessed | tf_op | source)
XLA Modules:
  0.0 81.0 jit_solution(17608202680230014404)
XLA Ops:
  0.6 0.5 collective-permute-start.4
  1.1 1.2 %copy-done = f32[1024,256]{1,0:T(8,128)S(1)} copy-done((f32[1024,256]{1,0:T(8,128)S(1)}, f32[1024,256]{1,0:T(8,128)}, u32[]{:S(2)}) %copy-start) | copy-done | bytes 1048600
  2.3 0.7 shard_map.41
  3.0 0.0 copy-start.2
  3.0 2.2 %collective-permute-start = (f32[264,128]{1,0:T(8,128)S(1)}, f32[264,128]{1,0:T(8,128)S(1)}, u32[]{:S(2)}, u32[]{:S(2)}) collective-permute-start(f32[264,128]{1,0:T(8,128)S(1)} %shard_map.41), channel_id=1, source_target_pairs={{0,1},{1,0},{2,3},{3,2},{4,5},{5,4},{6,7},{7,6},{8,9},{9,8},{10,11... | collective-permute-start | bytes 405512 | tf_op jit(solution)/shard_map/ppermute | solution.py:53
  5.2 1.0 %collective-permute-done = f32[264,128]{1,0:T(8,128)S(1)} collective-permute-done((f32[264,128]{1,0:T(8,128)S(1)}, f32[264,128]{1,0:T(8,128)S(1)}, u32[]{:S(2)}, u32[]{:S(2)}) %collective-permute-start) | collective-permute-done | bytes 135200 | tf_op jit(solution)/shard_map/ppermute | solution.py:53
  6.2 1.6 %collective-permute-start.1 = (f32[264,128]{1,0:T(8,128)S(1)}, f32[264,128]{1,0:T(8,128)S(1)}, u32[]{:S(2)}, u32[]{:S(2)}) collective-permute-start(f32[264,128]{1,0:T(8,128)S(1)} %add.6.refs_0_), channel_id=1, source_target_pairs={{0,2},{1,3},{2,0},{3,1},{4,6},{5,7},{6,4},{7,5},{8,10},{9,11},{10,... | collective-permute-start | bytes 405512 | tf_op jit(solution)/shard_map/ppermute | solution.py:53
  7.8 4.3 %collective-permute-done.1.refs_1_ = f32[264,128]{1,0:T(8,128)S(1)} collective-permute-done((f32[264,128]{1,0:T(8,128)S(1)}, f32[264,128]{1,0:T(8,128)S(1)}, u32[]{:S(2)}, u32[]{:S(2)}) %collective-permute-start.1) | collective-permute-done | bytes 135200 | tf_op jit(solution)/shard_map/ppermute | solution.py:53
  12.1 1.4 %shard_map.42 = (f32[256,256]{1,0:T(8,128)S(1)}, f32[80,128]{1,0:T(8,128)S(1)}, f32[80,128]{1,0:T(8,128)S(1)}) custom-call(s32[4,4]{1,0:T(4,128)S(1)} %copy-done.2, f32[264,128]{1,0:T(8,128)S(1)} %add.6.refs_0_, f32[264,128]{1,0:T(8,128)S(1)} %collective-permute-done.1.refs_1_), custom_call_target="tpu_custom_call" | custom-call | tf_op jit(solution)/shard_map/pallas_call | solution.py:227
  13.5 0.7 shard_map.43
  14.2 1.5 %collective-permute-start.5 = (f32[1104,128]{1,0:T(8,128)S(1)}, f32[1104,128]{1,0:T(8,128)S(1)}, u32[]{:S(2)}, u32[]{:S(2)}) collective-permute-start(f32[1104,128]{1,0:T(8,128)S(1)} %get-tuple-element.29.own_ref), channel_id=1, source_target_pairs={{0,2},{1,4},{2,0},{3,6},{4,8},{5,12},{6,10},{7,14},{8,1},{9,5},{10... | collective-permute-start | bytes 1695752 | tf_op jit(solution)/shard_map/ppermute | solution.py:53
  15.7 0.0 collective-permute-start.3
  15.7 0.5 collective-permute-start.2
  16.2 3.5 %collective-permute-done.2.u_ref.refs_4_ = f32[80,128]{1,0:T(8,128)S(1)} collective-permute-done((f32[80,128]{1,0:T(8,128)S(1)}, f32[80,128]{1,0:T(8,128)S(1)}, u32[]{:S(2)}, u32[]{:S(2)}) %collective-permute-start.2) | collective-permute-done | bytes 40992 | tf_op jit(solution)/shard_map/ppermute | solution.py:53
  19.7 1.0 %shard_map.44.block_ref = f32[1024,128]{1,0:T(8,128)S(1)} custom-call(s32[4,4]{1,0:T(4,128)S(1)} %copy-done.2, f32[80,128]{1,0:T(8,128)S(1)} %collective-permute-done.2.u_ref.refs_4_, f32[1024,128]{1,0:T(8,128)S(1)} %collective-permute-done.3.block_ref, f32[1024,256]{1,0:T(8,128)S(1)} %collective-permute-done.4.raw_ref), custom_call_target="tpu_custom_call" | custom-call | tf_op jit(solution)/shard_map/pallas_call | solution.py:227
  20.7 3.1 %collective-permute-done.5.w_ref = f32[1104,128]{1,0:T(8,128)S(1)} collective-permute-done((f32[1104,128]{1,0:T(8,128)S(1)}, f32[1104,128]{1,0:T(8,128)S(1)}, u32[]{:S(2)}, u32[]{:S(2)}) %collective-permute-start.5) | collective-permute-done | bytes 565280 | tf_op jit(solution)/shard_map/ppermute | solution.py:53
  23.8 0.5 shard_map.45
  24.4 0.7 collective-permute-start.11
  25.1 7.4 %collective-permute-start.8 = (f32[128,128]{1,0:T(8,128)S(1)}, f32[128,128]{1,0:T(8,128)S(1)}, u32[]{:S(2)}, u32[]{:S(2)}) collective-permute-start(f32[128,128]{1,0:T(8,128)S(1)} %get-tuple-element.30.refs_0_), channel_id=1, source_target_pairs={{0,6},{4,2},{2,4},{6,0},{1,7},{5,3},{3,5},{7,1},{8,14},{12,10},{10... | collective-permute-start | bytes 196616 | tf_op jit(solution)/shard_map/ppermute | solution.py:53
  32.5 0.5 collective-permute-start.7
  33.0 0.1 collective-permute-start.6
  33.2 1.6 %collective-permute-done.8.refs_3_ = f32[128,128]{1,0:T(8,128)S(1)} collective-permute-done((f32[128,128]{1,0:T(8,128)S(1)}, f32[128,128]{1,0:T(8,128)S(1)}, u32[]{:S(2)}, u32[]{:S(2)}) %collective-permute-start.8) | collective-permute-done | bytes 65568 | tf_op jit(solution)/shard_map/ppermute | solution.py:53
  34.8 2.4 %collective-permute-done.7.refs_2_ = f32[128,128]{1,0:T(8,128)S(1)} collective-permute-done((f32[128,128]{1,0:T(8,128)S(1)}, f32[128,128]{1,0:T(8,128)S(1)}, u32[]{:S(2)}, u32[]{:S(2)}) %collective-permute-start.7) | collective-permute-done | bytes 65568 | tf_op jit(solution)/shard_map/ppermute | solution.py:53
  37.1 0.2 collective-permute-done.6.refs_1_
  37.3 1.5 %shard_map.46 = (f32[256,256]{1,0:T(8,128)S(1)}, f32[96,128]{1,0:T(8,128)S(1)}, f32[96,128]{1,0:T(8,128)S(1)}) custom-call(s32[4,4]{1,0:T(4,128)S(1)} %copy-done.2, f32[128,128]{1,0:T(8,128)S(1)} %get-tuple-element.30.refs_0_, f32[128,128]{1,0:T(8,128)S(1)} %collective-permute-done.6.refs_1_, f32[128,128]{1,0:T(8,128)S(1)} %collective-permute-done.7.refs_2_, ...), custom_call_target="tpu_custom_call" | custom-call | tf_op jit(solution)/shard_map/pallas_call | solution.py:227
  38.8 0.6 shard_map.47
  39.4 1.5 %collective-permute-start.9 = (f32[1120,128]{1,0:T(8,128)S(1)}, f32[1120,128]{1,0:T(8,128)S(1)}, u32[]{:S(2)}, u32[]{:S(2)}) collective-permute-start(f32[1120,128]{1,0:T(8,128)S(1)} %shard_map.47), channel_id=1, source_target_pairs={{0,1},{4,5},{2,3},{6,7},{1,0},{5,4},{3,2},{7,6},{8,9},{12,13},{10,... | collective-permute-start | bytes 1720328 | tf_op jit(solution)/shard_map/ppermute | solution.py:53
  40.9 1.5 %collective-permute-start.10 = (f32[96,128]{1,0:T(8,128)S(1)}, f32[96,128]{1,0:T(8,128)S(1)}, u32[]{:S(2)}, u32[]{:S(2)}) collective-permute-start(f32[96,128]{1,0:T(8,128)S(1)} %get-tuple-element.34.far_ref.own_ref), channel_id=1, source_target_pairs={{0,2},{4,6},{2,0},{6,4},{1,8},{5,12},{3,10},{7,14},{8,1},{12,5},{1... | collective-permute-start | bytes 147464 | tf_op jit(solution)/shard_map/ppermute | solution.py:53
  42.4 2.6 %collective-permute-done.10.w_ref = f32[96,128]{1,0:T(8,128)S(1)} collective-permute-done((f32[96,128]{1,0:T(8,128)S(1)}, f32[96,128]{1,0:T(8,128)S(1)}, u32[]{:S(2)}, u32[]{:S(2)}) %collective-permute-start.10) | collective-permute-done | bytes 49184 | tf_op jit(solution)/shard_map/ppermute | solution.py:53
  45.0 1.7 %shard_map.48 = (f32[1024,128]{1,0:T(8,128)S(1)}, f32[128,128]{1,0:T(8,128)S(1)}, f32[96,128]{1,0:T(8,128)S(1)}, f32[96,128]{1,0:T(8,128)S(1)}) custom-call(s32[4,4]{1,0:T(4,128)S(1)} %copy-done.2, f32[1120,128]{1,0:T(8,128)S(1)} %collective-permute-done.9.u_ref.refs_0_, f32[96,128]{1,0:T(8,128)S(1)} %collective-permute-done.10.w_ref, ...), custom_call_target="tpu_custom_call" | custom-call | tf_op jit(solution)/shard_map/pallas_call | solution.py:227
  46.7 2.3 %collective-permute-start.14 = (f32[128,128]{1,0:T(8,128)S(1)}, f32[128,128]{1,0:T(8,128)S(1)}, u32[]{:S(2)}, u32[]{:S(2)}) collective-permute-start(f32[128,128]{1,0:T(8,128)S(1)} %get-tuple-element.36.refs_0_), channel_id=1, source_target_pairs={{0,6},{4,2},{2,4},{6,0},{1,7},{5,3},{3,5},{7,1},{8,14},{12,10},{10... | collective-permute-start | bytes 196616 | tf_op jit(solution)/shard_map/ppermute | solution.py:53
  49.0 0.5 collective-permute-start.13
  49.5 0.7 collective-permute-start.12
  50.2 1.7 %collective-permute-done.14.refs_3_ = f32[128,128]{1,0:T(8,128)S(1)} collective-permute-done((f32[128,128]{1,0:T(8,128)S(1)}, f32[128,128]{1,0:T(8,128)S(1)}, u32[]{:S(2)}, u32[]{:S(2)}) %collective-permute-start.14) | collective-permute-done | bytes 65568 | tf_op jit(solution)/shard_map/ppermute | solution.py:53
  51.9 2.1 %collective-permute-done.13.refs_2_ = f32[128,128]{1,0:T(8,128)S(1)} collective-permute-done((f32[128,128]{1,0:T(8,128)S(1)}, f32[128,128]{1,0:T(8,128)S(1)}, u32[]{:S(2)}, u32[]{:S(2)}) %collective-permute-start.13) | collective-permute-done | bytes 65568 | tf_op jit(solution)/shard_map/ppermute | solution.py:53
  54.0 1.5 %shard_map.49 = (f32[256,256]{1,0:T(8,128)S(1)}, f32[128,128]{1,0:T(8,128)S(1)}, f32[128,128]{1,0:T(8,128)S(1)}) custom-call(s32[4,4]{1,0:T(4,128)S(1)} %copy-done.2, f32[128,128]{1,0:T(8,128)S(1)} %get-tuple-element.36.refs_0_, f32[128,128]{1,0:T(8,128)S(1)} %collective-permute-done.12.refs_1_, f32[128,128]{1,0:T(8,128)S(1)} %collective-permute-done.13.refs_2_, ...), custom_call_target="tpu_custom_call" | custom-call | tf_op jit(solution)/shard_map/pallas_call | solution.py:227
  55.4 0.7 shard_map.50
  56.1 1.7 %collective-permute-start.15 = (f32[1152,128]{1,0:T(8,128)S(1)}, f32[1152,128]{1,0:T(8,128)S(1)}, u32[]{:S(2)}, u32[]{:S(2)}) collective-permute-start(f32[1152,128]{1,0:T(8,128)S(1)} %get-tuple-element.43), channel_id=1, source_target_pairs={{0,4},{4,5},{2,6},{6,7},{1,0},{5,1},{3,2},{7,3},{8,12},{12,13},{10... | collective-permute-start | bytes 1769480 | tf_op jit(solution)/shard_map/ppermute | solution.py:53
  57.8 1.5 %collective-permute-start.16 = (f32[1152,128]{1,0:T(8,128)S(1)}, f32[1152,128]{1,0:T(8,128)S(1)}, u32[]{:S(2)}, u32[]{:S(2)}) collective-permute-start(f32[1152,128]{1,0:T(8,128)S(1)} %get-tuple-element.44.own_ref), channel_id=1, source_target_pairs={{0,2},{4,1},{2,0},{6,3},{1,8},{5,9},{3,10},{7,11},{8,4},{12,5},{10... | collective-permute-start | bytes 1769480 | tf_op jit(solution)/shard_map/ppermute | solution.py:53
  59.3 12.2 %collective-permute-done.15.u_ref = f32[1152,128]{1,0:T(8,128)S(1)} collective-permute-done((f32[1152,128]{1,0:T(8,128)S(1)}, f32[1152,128]{1,0:T(8,128)S(1)}, u32[]{:S(2)}, u32[]{:S(2)}) %collective-permute-start.15) | collective-permute-done | bytes 589856 | tf_op jit(solution)/shard_map/ppermute | solution.py:53
  71.5 0.6 shard_map.51
  72.1 0.2 collective-permute-start.17
  72.3 1.1 %collective-permute-done.17 = f32[128,128]{1,0:T(8,128)S(1)} collective-permute-done((f32[128,128]{1,0:T(8,128)S(1)}, f32[128,128]{1,0:T(8,128)S(1)}, u32[]{:S(2)}, u32[]{:S(2)}) %collective-permute-start.17) | collective-permute-done | bytes 65568 | tf_op jit(solution)/shard_map/ppermute | solution.py:53
  73.4 1.6 %collective-permute-start.18 = (f32[128,128]{1,0:T(8,128)S(1)}, f32[128,128]{1,0:T(8,128)S(1)}, u32[]{:S(2)}, u32[]{:S(2)}) collective-permute-start(f32[128,128]{1,0:T(8,128)S(1)} %add.7.refs_0_), channel_id=1, source_target_pairs={{0,2},{1,3},{2,0},{3,1},{4,6},{5,7},{6,4},{7,5},{8,10},{9,11},{10,... | collective-permute-start | bytes 196616 | tf_op jit(solution)/shard_map/ppermute | solution.py:53
  75.0 0.1 shard_map.52
  75.1 2.3 %shard_map.53.refs_5_ = f32[512,256]{1,0:T(8,128)S(1)} custom-call(s32[4,4]{1,0:T(4,128)S(1)} %copy-done.2, f32[128,128]{1,0:T(8,128)S(1)} %get-tuple-element.45.mu_ref.refs_2_, f32[128,128]{1,0:T(8,128)S(1)} %get-tuple-element.46.mw_ref.refs_3_), custom_call_target="tpu_custom_call" | custom-call | tf_op jit(solution)/shard_map/pallas_call | solution.py:227
  77.5 0.3 collective-permute-done.18.refs_1_
  77.8 3.2 %shard_map.54 = (f32[1024,256]{1,0:T(8,128)}, f32[512,256]{1,0:T(8,128)}) custom-call(s32[4,4]{1,0:T(4,128)S(1)} %copy-done.2, f32[128,128]{1,0:T(8,128)S(1)} %add.7.refs_0_, f32[128,128]{1,0:T(8,128)S(1)} %collective-permute-done.18.refs_1_, f32[128,128]{1,0:T(8,128)S(1)} %get-tuple-element.45.mu_ref.refs_2_, ...), custom_call_target="tpu_custom_call" | custom-call | tf_op jit(solution)/shard_map/pallas_call | solution.py:227
  (12 shorter events, 0.0 us)
Async XLA Ops:
  0.6 19.1 %collective-permute-start.4 = (f32[1024,256]{1,0:T(8,128)}, f32[1024,256]{1,0:T(8,128)S(1)}, u32[]{:S(2)}, u32[]{:S(2)}) collective-permute-start(f32[1024,256]{1,0:T(8,128)} %refs_0_.1), channel_id=1, source_target_pairs={{0,1},{1,5},{2,3},{3,7},{4,0},{5,4},{6,2},{7,6},{8,9},{9,13},{10,1... | collective-permute-start | bytes 3145736 | tf_op jit(solution)/shard_map/ppermute | solution.py:53
  1.1 1.2 %copy-start = (f32[1024,256]{1,0:T(8,128)S(1)}, f32[1024,256]{1,0:T(8,128)}, u32[]{:S(2)}) copy-start(f32[1024,256]{1,0:T(8,128)} %refs_0_.1) | copy-start | bytes 3145732
  2.3 11.2 %copy-start.1 = (f32[1024,256]{1,0:T(8,128)S(1)}, f32[1024,256]{1,0:T(8,128)}, u32[]{:S(2)}) copy-start(f32[1024,256]{1,0:T(8,128)} %refs_0_.1) | copy-start | bytes 3145732
  3.0 9.1 %copy-start.2 = (s32[4,4]{1,0:T(4,128)S(1)}, s32[4,4]{1,0:T(4,128)}, u32[]{:S(2)}) copy-start(s32[4,4]{1,0:T(4,128)} %offs_ref.13) | copy-start | bytes 196
  3.0 3.2 %collective-permute-start = (f32[264,128]{1,0:T(8,128)S(1)}, f32[264,128]{1,0:T(8,128)S(1)}, u32[]{:S(2)}, u32[]{:S(2)}) collective-permute-start(f32[264,128]{1,0:T(8,128)S(1)} %shard_map.41), channel_id=1, source_target_pairs={{0,1},{1,0},{2,3},{3,2},{4,5},{5,4},{6,7},{7,6},{8,9},{9,8},{10,11... | collective-permute-start | bytes 405512 | tf_op jit(solution)/shard_map/ppermute | solution.py:53
  6.2 5.9 %collective-permute-start.1 = (f32[264,128]{1,0:T(8,128)S(1)}, f32[264,128]{1,0:T(8,128)S(1)}, u32[]{:S(2)}, u32[]{:S(2)}) collective-permute-start(f32[264,128]{1,0:T(8,128)S(1)} %add.6.refs_0_), channel_id=1, source_target_pairs={{0,2},{1,3},{2,0},{3,1},{4,6},{5,7},{6,4},{7,5},{8,10},{9,11},{10,... | collective-permute-start | bytes 405512 | tf_op jit(solution)/shard_map/ppermute | solution.py:53
  14.2 9.7 %collective-permute-start.5 = (f32[1104,128]{1,0:T(8,128)S(1)}, f32[1104,128]{1,0:T(8,128)S(1)}, u32[]{:S(2)}, u32[]{:S(2)}) collective-permute-start(f32[1104,128]{1,0:T(8,128)S(1)} %get-tuple-element.29.own_ref), channel_id=1, source_target_pairs={{0,2},{1,4},{2,0},{3,6},{4,8},{5,12},{6,10},{7,14},{8,1},{9,5},{10... | collective-permute-start | bytes 1695752 | tf_op jit(solution)/shard_map/ppermute | solution.py:53
  15.7 4.0 %collective-permute-start.3 = (f32[1024,128]{1,0:T(8,128)S(1)}, f32[1024,128]{1,0:T(8,128)S(1)}, u32[]{:S(2)}, u32[]{:S(2)}) collective-permute-start(f32[1024,128]{1,0:T(8,128)S(1)} %get-tuple-element.28), channel_id=1, source_target_pairs={{0,1},{1,0},{2,3},{3,2},{4,5},{5,4},{6,7},{7,6},{8,9},{9,8},{10,11... | collective-permute-start | bytes 1572872 | tf_op jit(solution)/shard_map/ppermute | solution.py:53
  15.7 4.0 %collective-permute-start.2 = (f32[80,128]{1,0:T(8,128)S(1)}, f32[80,128]{1,0:T(8,128)S(1)}, u32[]{:S(2)}, u32[]{:S(2)}) collective-permute-start(f32[80,128]{1,0:T(8,128)S(1)} %get-tuple-element.25.near_ref), channel_id=1, source_target_pairs={{0,1},{1,5},{2,3},{3,7},{4,0},{5,4},{6,2},{7,6},{8,9},{9,13},{10,1... | collective-permute-start | bytes 122888 | tf_op jit(solution)/shard_map/ppermute | solution.py:53
  24.4 20.6 %collective-permute-start.11 = (f32[1024,256]{1,0:T(8,128)S(1)}, f32[1024,256]{1,0:T(8,128)S(1)}, u32[]{:S(2)}, u32[]{:S(2)}) collective-permute-start(f32[1024,256]{1,0:T(8,128)S(1)} %get-tuple-element.35.refs_0_), channel_id=1, source_target_pairs={{0,0},{4,4},{2,2},{6,6},{1,8},{5,12},{3,10},{7,14},{8,1},{12,5},{1... | collective-permute-start | bytes 3145736 | tf_op jit(solution)/shard_map/ppermute | solution.py:53
  25.1 9.6 %collective-permute-start.8 = (f32[128,128]{1,0:T(8,128)S(1)}, f32[128,128]{1,0:T(8,128)S(1)}, u32[]{:S(2)}, u32[]{:S(2)}) collective-permute-start(f32[128,128]{1,0:T(8,128)S(1)} %get-tuple-element.30.refs_0_), channel_id=1, source_target_pairs={{0,6},{4,2},{2,4},{6,0},{1,7},{5,3},{3,5},{7,1},{8,14},{12,10},{10... | collective-permute-start | bytes 196616 | tf_op jit(solution)/shard_map/ppermute | solution.py:53
  32.5 4.6 %collective-permute-start.7 = (f32[128,128]{1,0:T(8,128)S(1)}, f32[128,128]{1,0:T(8,128)S(1)}, u32[]{:S(2)}, u32[]{:S(2)}) collective-permute-start(f32[128,128]{1,0:T(8,128)S(1)} %get-tuple-element.30.refs_0_), channel_id=1, source_target_pairs={{0,2},{4,6},{2,0},{6,4},{1,3},{5,7},{3,1},{7,5},{8,10},{12,14},{10... | collective-permute-start | bytes 196616 | tf_op jit(solution)/shard_map/ppermute | solution.py:53
  33.0 4.3 %collective-permute-start.6 = (f32[128,128]{1,0:T(8,128)S(1)}, f32[128,128]{1,0:T(8,128)S(1)}, u32[]{:S(2)}, u32[]{:S(2)}) collective-permute-start(f32[128,128]{1,0:T(8,128)S(1)} %get-tuple-element.30.refs_0_), channel_id=1, source_target_pairs={{0,4},{4,0},{2,6},{6,2},{1,5},{5,1},{3,7},{7,3},{8,12},{12,8},{10,... | collective-permute-start | bytes 196616 | tf_op jit(solution)/shard_map/ppermute | solution.py:53
  39.4 5.6 %collective-permute-start.9 = (f32[1120,128]{1,0:T(8,128)S(1)}, f32[1120,128]{1,0:T(8,128)S(1)}, u32[]{:S(2)}, u32[]{:S(2)}) collective-permute-start(f32[1120,128]{1,0:T(8,128)S(1)} %shard_map.47), channel_id=1, source_target_pairs={{0,1},{4,5},{2,3},{6,7},{1,0},{5,4},{3,2},{7,6},{8,9},{12,13},{10,... | collective-permute-start | bytes 1720328 | tf_op jit(solution)/shard_map/ppermute | solution.py:53
  40.9 4.1 %collective-permute-start.10 = (f32[96,128]{1,0:T(8,128)S(1)}, f32[96,128]{1,0:T(8,128)S(1)}, u32[]{:S(2)}, u32[]{:S(2)}) collective-permute-start(f32[96,128]{1,0:T(8,128)S(1)} %get-tuple-element.34.far_ref.own_ref), channel_id=1, source_target_pairs={{0,2},{4,6},{2,0},{6,4},{1,8},{5,12},{3,10},{7,14},{8,1},{12,5},{1... | collective-permute-start | bytes 147464 | tf_op jit(solution)/shard_map/ppermute | solution.py:53
  46.7 5.2 %collective-permute-start.14 = (f32[128,128]{1,0:T(8,128)S(1)}, f32[128,128]{1,0:T(8,128)S(1)}, u32[]{:S(2)}, u32[]{:S(2)}) collective-permute-start(f32[128,128]{1,0:T(8,128)S(1)} %get-tuple-element.36.refs_0_), channel_id=1, source_target_pairs={{0,6},{4,2},{2,4},{6,0},{1,7},{5,3},{3,5},{7,1},{8,14},{12,10},{10... | collective-permute-start | bytes 196616 | tf_op jit(solution)/shard_map/ppermute | solution.py:53
  49.0 5.0 %collective-permute-start.13 = (f32[128,128]{1,0:T(8,128)S(1)}, f32[128,128]{1,0:T(8,128)S(1)}, u32[]{:S(2)}, u32[]{:S(2)}) collective-permute-start(f32[128,128]{1,0:T(8,128)S(1)} %get-tuple-element.36.refs_0_), channel_id=1, source_target_pairs={{0,2},{4,6},{2,0},{6,4},{1,3},{5,7},{3,1},{7,5},{8,10},{12,14},{10... | collective-permute-start | bytes 196616 | tf_op jit(solution)/shard_map/ppermute | solution.py:53
  49.5 4.4 %collective-permute-start.12 = (f32[128,128]{1,0:T(8,128)S(1)}, f32[128,128]{1,0:T(8,128)S(1)}, u32[]{:S(2)}, u32[]{:S(2)}) collective-permute-start(f32[128,128]{1,0:T(8,128)S(1)} %get-tuple-element.36.refs_0_), channel_id=1, source_target_pairs={{0,4},{4,0},{2,6},{6,2},{1,5},{5,1},{3,7},{7,3},{8,12},{12,8},{10,... | collective-permute-start | bytes 196616 | tf_op jit(solution)/shard_map/ppermute | solution.py:53
  56.1 15.4 %collective-permute-start.15 = (f32[1152,128]{1,0:T(8,128)S(1)}, f32[1152,128]{1,0:T(8,128)S(1)}, u32[]{:S(2)}, u32[]{:S(2)}) collective-permute-start(f32[1152,128]{1,0:T(8,128)S(1)} %get-tuple-element.43), channel_id=1, source_target_pairs={{0,4},{4,5},{2,6},{6,7},{1,0},{5,1},{3,2},{7,3},{8,12},{12,13},{10... | collective-permute-start | bytes 1769480 | tf_op jit(solution)/shard_map/ppermute | solution.py:53
  57.8 13.7 %collective-permute-start.16 = (f32[1152,128]{1,0:T(8,128)S(1)}, f32[1152,128]{1,0:T(8,128)S(1)}, u32[]{:S(2)}, u32[]{:S(2)}) collective-permute-start(f32[1152,128]{1,0:T(8,128)S(1)} %get-tuple-element.44.own_ref), channel_id=1, source_target_pairs={{0,2},{4,1},{2,0},{6,3},{1,8},{5,9},{3,10},{7,11},{8,4},{12,5},{10... | collective-permute-start | bytes 1769480 | tf_op jit(solution)/shard_map/ppermute | solution.py:53
  72.1 1.3 %collective-permute-start.17 = (f32[128,128]{1,0:T(8,128)S(1)}, f32[128,128]{1,0:T(8,128)S(1)}, u32[]{:S(2)}, u32[]{:S(2)}) collective-permute-start(f32[128,128]{1,0:T(8,128)S(1)} %shard_map.51), channel_id=1, source_target_pairs={{0,1},{1,0},{2,3},{3,2},{4,5},{5,4},{6,7},{7,6},{8,9},{9,8},{10,11... | collective-permute-start | bytes 196616 | tf_op jit(solution)/shard_map/ppermute | solution.py:53
  73.4 4.3 %collective-permute-start.18 = (f32[128,128]{1,0:T(8,128)S(1)}, f32[128,128]{1,0:T(8,128)S(1)}, u32[]{:S(2)}, u32[]{:S(2)}) collective-permute-start(f32[128,128]{1,0:T(8,128)S(1)} %add.7.refs_0_), channel_id=1, source_target_pairs={{0,2},{1,3},{2,0},{3,1},{4,6},{5,7},{6,4},{7,5},{8,10},{9,11},{10,... | collective-permute-start | bytes 196616 | tf_op jit(solution)/shard_map/ppermute | solution.py:53

commit v6 on v5

--- a/solution.py
+++ b/solution.py
@@ -11,6 +11,7 @@
 ROUNDS = 4
 STEPS = 4
 RECORD = 2 * ROUNDS
+PIECES = 4
 HALF = B // 2
 PACKED = HALF + 8
 AXES = ("pair", "row")
@@ -94,7 +95,7 @@
         radius = jnp.sqrt(h * h + c0 * c0)
         sg = jnp.where(h >= 0, 1.0, -1.0)
         t = -sg * c0 / (jnp.abs(h) + radius + 1e-06 * (a + d))
-        c = 1.0 / jnp.sqrt(1.0 + t * t)
+        c = lax.rsqrt(1.0 + t * t)
         s = t * c
         angles.append((c, s))
         cc, sc = as_column(mask, c), as_column(mask, s)
@@ -106,8 +107,11 @@
         first = cc * first1 + sc * below1
         across = cc * across1 + sc * second1
         second = cc * second1 - sc * across1
-        a, d = c * (a * c + c0 * s) + s * (c0 * c + d * s), c * (d * c - c0 * s) - s * (c0 * c - a * s)
+        moved = s * (s * (d - a) + 2.0 * (c * c0))
+        a, d = a + moved, d - moved
         turns = [(c * top + s * low, c * low - s * top) for top, low in turns]
+    first = jnp.where(mask, jnp.broadcast_to(a, (B, B)), first)
+    second = jnp.where(mask, jnp.broadcast_to(d, (B, B)), second)
     second = pltpu.roll(pltpu.roll(second, held, 1), held, 0)
     turns = [(top, pltpu.roll(low, held, 1)) for top, low in turns]
     rotation = jnp.concatenate([jnp.concatenate(t, axis=1) for t in turns], axis=0)
@@ -399,9 +403,16 @@
     return call(arrive_kernel, shapes, (block, u, w, own))
 
 
-def arrive_raw_kernel(step, offs_ref, u_ref, w_ref, own_ref, raw_ref, *refs):
-    block_ref, gram_ref, mu_ref, mw_ref = refs
-    rows = raw_ref.shape[0]
+def ahead_kernel(u_ref, raw_ref, out_ref):
+    out_ref[...] = transposed_dot(u_ref[: raw_ref.shape[0], :], raw_ref[...])
+
+
+def ahead(u, raw):
+    return call(ahead_kernel, [(B, 2 * B)], (u, raw))[0]
+
+
+def arrive_raw_kernel(step, rows, offs_ref, u_ref, w_ref, own_ref, ahead_ref, *refs):
+    half_ref, gram_ref, mu_ref, mw_ref = refs
     place = Place(crossed)
     own = place.edge
     mu_ref[...] = u_ref[rows:, :]
@@ -410,17 +421,23 @@
     angles = read_record(jnp.where(own, own_ref[at, :], w_ref[at, :]))
     takes_first = jnp.logical_or(jnp.logical_not(place.odd), place.slot == place.pairs - 1)
     half = half_rotation(angles, step_offsets(offs_ref, step), takes_first)
-    block = product(raw_ref[...], half)
-    block_ref[...] = block
-    gram = transposed_dot(u_ref[:rows, :], block)
+    half_ref[...] = half
+    gram = product(ahead_ref[...], half)
     gram_ref[...] = jnp.where(place.odd, gram, gram.T)
 
 
-def arrive_raw(step, offsets, u, w, own, raw):
-    rows = raw.shape[0]
-    kernel = functools.partial(arrive_raw_kernel, step)
-    shapes = [(rows, B), (B, B), w.shape, w.shape]
-    return call(kernel, shapes, (offsets, u, w, own, raw))
+def arrive_raw(step, rows, offsets, u, w, own, products):
+    kernel = functools.partial(arrive_raw_kernel, step, rows)
+    shapes = [(2 * B, B), (B, B), w.shape, w.shape]
+    return call(kernel, shapes, (offsets, u, w, own, products))
+
+
+def outer_block_kernel(raw_ref, half_ref, out_ref):
+    out_ref[...] = product(raw_ref[...], half_ref[...])
+
+
+def outer_block(raw, half):
+    return call(outer_block_kernel, [(raw.shape[0], B)], (raw, half))[0]
 
 
 def ready_kernel(step, offs_ref, u_ref, block_ref, raw_ref, out_ref):
@@ -527,19 +544,39 @@
 
 
 def last_kernel(count, offs_ref, *refs):
-    parts, (mu_ref, mw_ref, x_ref, v_ref, x_out, v_out) = refs[:count], refs[count:]
+    parts, refs = refs[:count], refs[count:]
+    mu_ref, mw_ref, x_ref, v_ref, x_out, v_out, x_held, v_held, sems = refs
     odd = Place(given).odd
     gram = tree_sum([p[...] for p in parts])
     across = jnp.where(odd, gram, gram.T)
     offs = step_offsets(offs_ref, STEPS - 1)
     _, rotation, _, _ = cross_solve(across, odd, mu_ref[...], mw_ref[...], offs)
-    x_out[...] = product(x_ref[...], rotation)
-    v_out[...] = product(v_ref[...], rotation)
+    copies = []
+
+    def put(source, held, out, at):
+        held[at, :] = product(source[at, :], rotation)
+        copies.append(pltpu.make_async_copy(held.at[at], out.at[at], sems.at[len(copies)]))
+        copies[-1].start()
+
+    size = x_ref.shape[0] // PIECES
+    for i in range(PIECES):
+        put(x_ref, x_held, x_out, pl.ds(i * size, size))
+    put(v_ref, v_held, v_out, pl.ds(0, v_ref.shape[0]))
+    for copy in copies:
+        copy.wait()
 
 
 def last_step(offsets, parts, messages, x, v):
-    kernel = functools.partial(last_kernel, len(parts))
-    return call(kernel, [x.shape, v.shape], (offsets, *parts, *messages, x, v))
+    outside = pl.BlockSpec(memory_space=pl.ANY)
+    return pl.pallas_call(
+        functools.partial(last_kernel, len(parts)),
+        out_shape=tuple(jax.ShapeDtypeStruct(a.shape, jnp.float32) for a in (x, v)),
+        in_specs=[VMEM] * (len(parts) + 5),
+        out_specs=(outside, outside),
+        scratch_shapes=[pltpu.VMEM(a.shape, jnp.float32) for a in (x, v)]
+        + [pltpu.SemaphoreType.DMA((PIECES + 1,))],
+        compiler_params=PARAMS,
+    )(offsets, *parts, *messages, x, v)
 
 
 def in_stages(partial, layout):
@@ -577,7 +614,8 @@
     w = send(far, crossed, crossed, outer)
     (near,) = turned(rows, (JOINED, RAW), crossed, rotation, near, far, x)
     u = send(near, crossed, crossed, inner)
-    block, cross, mu, mw = arrive_raw(1, offsets, u, w, far, raw)
+    half, cross, mu, mw = arrive_raw(1, rows, offsets, u, w, far, ahead(u, raw))
+    block = outer_block(raw, half)
 
     terms = at_once(cross, crossed)
     rotation, near, far = solved(2, crossed, offsets, terms, (mu, mw))

time: 81.6 us -> 80.3 us (0.984)
  waiting for transfers between devices: 36.1 us -> 35 us
    pallas_call x14 -> x15, Pallas kernels: 16.3 us -> 13 us  [call(): pl.pallas_call(kernel, out_shape=tuple((jax.ShapeDtypeStruct(shape, jnp.f...]
    pallas_call x0 -> x1, Pallas kernels: none -> 2.85 us  [last_step(): pl.pallas_call(functools.partial(last_kernel, len(parts)), out_shape=tupl...]
    ppermute x19, waiting for transfers between devices: 36.1 us -> 35 us  [send(): return lax.ppermute(x, AXES, route(source, target, change, swap))]
  transfers between devices with their start and end apart: 19 -> 19, of which waited for: 13 -> 14; matrix products, arithmetic and copies ran while one was open for 0% -> 0% of each run, Pallas kernels for 10% -> 11%
where the time goes in v6:
time: 80.3 us; the launch traced here: 79.7 us
  waiting for transfers between devices  35 us (44%)
  starting transfers between devices  26.7 us (33%)
  Pallas kernels  15.9 us (20%)
  local copies, waits for them, and re-layouts  1.23 us (2%)
  between operations  0.94 us (1%)
    ppermute x19, waiting for transfers between devices, send(): return lax.ppermute(x, AXES, route(source, target, change, swap))  35 us
    ppermute x19, starting transfers between devices, send(): return lax.ppermute(x, AXES, route(source, target, change, swap))  26.7 us
    pallas_call x15, Pallas kernels, call(): pl.pallas_call(kernel, out_shape=tuple((jax.ShapeDtypeStruct(shape, jnp.f...  13 us
    pallas_call x1, Pallas kernels, last_step(): pl.pallas_call(functools.partial(last_kernel, len(parts)), out_shape=tupl...  2.85 us
  transfers between devices with their start and end apart: 19, of which 14 were waited for; matrix products, arithmetic and copies ran while one was open for 0% of the time, Pallas kernels for 11%

profile of v6, /device:TPU:0, one launch (start us, length us, event | category | flops | bytes accessed | tf_op | source)
XLA Modules:
  0.0 79.7 jit_solution(308368311504070872)
XLA Ops:
  0.6 0.5 collective-permute-start.4
  1.1 1.2 %copy-done = f32[1024,256]{1,0:T(8,128)S(1)} copy-done((f32[1024,256]{1,0:T(8,128)S(1)}, f32[1024,256]{1,0:T(8,128)}, u32[]{:S(2)}) %copy-start) | copy-done | bytes 1048600
  2.3 0.7 shard_map.41
  3.0 2.2 %collective-permute-start = (f32[264,128]{1,0:T(8,128)S(1)}, f32[264,128]{1,0:T(8,128)S(1)}, u32[]{:S(2)}, u32[]{:S(2)}) collective-permute-start(f32[264,128]{1,0:T(8,128)S(1)} %shard_map.41), channel_id=1, source_target_pairs={{0,1},{1,0},{2,3},{3,2},{4,5},{5,4},{6,7},{7,6},{8,9},{9,8},{10,11... | collective-permute-start | bytes 405512 | tf_op jit(solution)/shard_map/ppermute | solution.py:54
  5.2 1.0 %collective-permute-done = f32[264,128]{1,0:T(8,128)S(1)} collective-permute-done((f32[264,128]{1,0:T(8,128)S(1)}, f32[264,128]{1,0:T(8,128)S(1)}, u32[]{:S(2)}, u32[]{:S(2)}) %collective-permute-start) | collective-permute-done | bytes 135200 | tf_op jit(solution)/shard_map/ppermute | solution.py:54
  6.2 1.6 %collective-permute-start.1 = (f32[264,128]{1,0:T(8,128)S(1)}, f32[264,128]{1,0:T(8,128)S(1)}, u32[]{:S(2)}, u32[]{:S(2)}) collective-permute-start(f32[264,128]{1,0:T(8,128)S(1)} %add.6.refs_0_), channel_id=1, source_target_pairs={{0,2},{1,3},{2,0},{3,1},{4,6},{5,7},{6,4},{7,5},{8,10},{9,11},{10,... | collective-permute-start | bytes 405512 | tf_op jit(solution)/shard_map/ppermute | solution.py:54
  7.8 4.3 %collective-permute-done.1.refs_1_ = f32[264,128]{1,0:T(8,128)S(1)} collective-permute-done((f32[264,128]{1,0:T(8,128)S(1)}, f32[264,128]{1,0:T(8,128)S(1)}, u32[]{:S(2)}, u32[]{:S(2)}) %collective-permute-start.1) | collective-permute-done | bytes 135200 | tf_op jit(solution)/shard_map/ppermute | solution.py:54
  12.1 1.3 %shard_map.42 = (f32[256,256]{1,0:T(8,128)S(1)}, f32[80,128]{1,0:T(8,128)S(1)}, f32[80,128]{1,0:T(8,128)S(1)}) custom-call(s32[4,4]{1,0:T(4,128)S(1)} %copy-done.2, f32[264,128]{1,0:T(8,128)S(1)} %add.6.refs_0_, f32[264,128]{1,0:T(8,128)S(1)} %collective-permute-done.1.refs_1_), custom_call_target="tpu_custom_call" | custom-call | tf_op jit(solution)/shard_map/pallas_call | solution.py:231
  13.5 0.7 shard_map.43
  14.1 1.5 %collective-permute-start.5 = (f32[1104,128]{1,0:T(8,128)S(1)}, f32[1104,128]{1,0:T(8,128)S(1)}, u32[]{:S(2)}, u32[]{:S(2)}) collective-permute-start(f32[1104,128]{1,0:T(8,128)S(1)} %get-tuple-element.29.own_ref), channel_id=1, source_target_pairs={{0,2},{1,4},{2,0},{3,6},{4,8},{5,12},{6,10},{7,14},{8,1},{9,5},{10... | collective-permute-start | bytes 1695752 | tf_op jit(solution)/shard_map/ppermute | solution.py:54
  15.7 0.5 collective-permute-start.2
  16.2 3.5 %collective-permute-done.2.u_ref.refs_4_ = f32[80,128]{1,0:T(8,128)S(1)} collective-permute-done((f32[80,128]{1,0:T(8,128)S(1)}, f32[80,128]{1,0:T(8,128)S(1)}, u32[]{:S(2)}, u32[]{:S(2)}) %collective-permute-start.2) | collective-permute-done | bytes 40992 | tf_op jit(solution)/shard_map/ppermute | solution.py:54
  19.7 1.0 %shard_map.44.block_ref = f32[1024,128]{1,0:T(8,128)S(1)} custom-call(s32[4,4]{1,0:T(4,128)S(1)} %copy-done.2, f32[80,128]{1,0:T(8,128)S(1)} %collective-permute-done.2.u_ref.refs_4_, f32[1024,128]{1,0:T(8,128)S(1)} %collective-permute-done.3.block_ref, f32[1024,256]{1,0:T(8,128)S(1)} %collective-permute-done.4.raw_ref), custom_call_target="tpu_custom_call" | custom-call | tf_op jit(solution)/shard_map/pallas_call | solution.py:231
  20.7 3.1 %collective-permute-done.5.w_ref = f32[1104,128]{1,0:T(8,128)S(1)} collective-permute-done((f32[1104,128]{1,0:T(8,128)S(1)}, f32[1104,128]{1,0:T(8,128)S(1)}, u32[]{:S(2)}, u32[]{:S(2)}) %collective-permute-start.5) | collective-permute-done | bytes 565280 | tf_op jit(solution)/shard_map/ppermute | solution.py:54
  23.8 0.5 shard_map.45
  24.4 0.7 collective-permute-start.11
  25.1 7.4 %collective-permute-start.8 = (f32[128,128]{1,0:T(8,128)S(1)}, f32[128,128]{1,0:T(8,128)S(1)}, u32[]{:S(2)}, u32[]{:S(2)}) collective-permute-start(f32[128,128]{1,0:T(8,128)S(1)} %get-tuple-element.30.refs_0_), channel_id=1, source_target_pairs={{0,6},{4,2},{2,4},{6,0},{1,7},{5,3},{3,5},{7,1},{8,14},{12,10},{10... | collective-permute-start | bytes 196616 | tf_op jit(solution)/shard_map/ppermute | solution.py:54
  32.5 0.5 collective-permute-start.7
  33.1 1.6 %collective-permute-done.8.refs_3_ = f32[128,128]{1,0:T(8,128)S(1)} collective-permute-done((f32[128,128]{1,0:T(8,128)S(1)}, f32[128,128]{1,0:T(8,128)S(1)}, u32[]{:S(2)}, u32[]{:S(2)}) %collective-permute-start.8) | collective-permute-done | bytes 65568 | tf_op jit(solution)/shard_map/ppermute | solution.py:54
  34.7 2.4 %collective-permute-done.7.refs_2_ = f32[128,128]{1,0:T(8,128)S(1)} collective-permute-done((f32[128,128]{1,0:T(8,128)S(1)}, f32[128,128]{1,0:T(8,128)S(1)}, u32[]{:S(2)}, u32[]{:S(2)}) %collective-permute-start.7) | collective-permute-done | bytes 65568 | tf_op jit(solution)/shard_map/ppermute | solution.py:54
  37.1 0.2 collective-permute-done.6.refs_1_
  37.3 1.4 %shard_map.46 = (f32[256,256]{1,0:T(8,128)S(1)}, f32[96,128]{1,0:T(8,128)S(1)}, f32[96,128]{1,0:T(8,128)S(1)}) custom-call(s32[4,4]{1,0:T(4,128)S(1)} %copy-done.2, f32[128,128]{1,0:T(8,128)S(1)} %get-tuple-element.30.refs_0_, f32[128,128]{1,0:T(8,128)S(1)} %collective-permute-done.6.refs_1_, f32[128,128]{1,0:T(8,128)S(1)} %collective-permute-done.7.refs_2_, ...), custom_call_target="tpu_custom_call" | custom-call | tf_op jit(solution)/shard_map/pallas_call | solution.py:231
  38.7 0.6 shard_map.47
  39.3 1.5 %collective-permute-start.9 = (f32[1120,128]{1,0:T(8,128)S(1)}, f32[1120,128]{1,0:T(8,128)S(1)}, u32[]{:S(2)}, u32[]{:S(2)}) collective-permute-start(f32[1120,128]{1,0:T(8,128)S(1)} %shard_map.47), channel_id=1, source_target_pairs={{0,1},{4,5},{2,3},{6,7},{1,0},{5,4},{3,2},{7,6},{8,9},{12,13},{10,... | collective-permute-start | bytes 1720328 | tf_op jit(solution)/shard_map/ppermute | solution.py:54
  40.9 1.5 %collective-permute-start.10 = (f32[96,128]{1,0:T(8,128)S(1)}, f32[96,128]{1,0:T(8,128)S(1)}, u32[]{:S(2)}, u32[]{:S(2)}) collective-permute-start(f32[96,128]{1,0:T(8,128)S(1)} %get-tuple-element.34.far_ref.own_ref), channel_id=1, source_target_pairs={{0,2},{4,6},{2,0},{6,4},{1,8},{5,12},{3,10},{7,14},{8,1},{12,5},{1... | collective-permute-start | bytes 147464 | tf_op jit(solution)/shard_map/ppermute | solution.py:54
  42.4 0.1 collective-permute-done.9.u_ref.refs_0_
  42.5 0.4 shard_map.48.ahead_ref
  42.9 2.1 %collective-permute-done.10.w_ref = f32[96,128]{1,0:T(8,128)S(1)} collective-permute-done((f32[96,128]{1,0:T(8,128)S(1)}, f32[96,128]{1,0:T(8,128)S(1)}, u32[]{:S(2)}, u32[]{:S(2)}) %collective-permute-start.10) | collective-permute-done | bytes 49184 | tf_op jit(solution)/shard_map/ppermute | solution.py:54
  45.0 0.7 shard_map.49
  45.6 2.3 %collective-permute-start.14 = (f32[128,128]{1,0:T(8,128)S(1)}, f32[128,128]{1,0:T(8,128)S(1)}, u32[]{:S(2)}, u32[]{:S(2)}) collective-permute-start(f32[128,128]{1,0:T(8,128)S(1)} %get-tuple-element.36.refs_0_), channel_id=1, source_target_pairs={{0,6},{4,2},{2,4},{6,0},{1,7},{5,3},{3,5},{7,1},{8,14},{12,10},{10... | collective-permute-start | bytes 196616 | tf_op jit(solution)/shard_map/ppermute | solution.py:54
  48.0 0.5 collective-permute-start.13
  48.5 0.7 collective-permute-start.12
  49.2 0.6 shard_map.51.refs_1_
  49.8 1.1 %collective-permute-done.14.refs_3_ = f32[128,128]{1,0:T(8,128)S(1)} collective-permute-done((f32[128,128]{1,0:T(8,128)S(1)}, f32[128,128]{1,0:T(8,128)S(1)}, u32[]{:S(2)}, u32[]{:S(2)}) %collective-permute-start.14) | collective-permute-done | bytes 65568 | tf_op jit(solution)/shard_map/ppermute | solution.py:54
  50.9 2.0 %collective-permute-done.13.refs_2_ = f32[128,128]{1,0:T(8,128)S(1)} collective-permute-done((f32[128,128]{1,0:T(8,128)S(1)}, f32[128,128]{1,0:T(8,128)S(1)}, u32[]{:S(2)}, u32[]{:S(2)}) %collective-permute-start.13) | collective-permute-done | bytes 65568 | tf_op jit(solution)/shard_map/ppermute | solution.py:54
  52.9 1.4 %shard_map.50 = (f32[256,256]{1,0:T(8,128)S(1)}, f32[128,128]{1,0:T(8,128)S(1)}, f32[128,128]{1,0:T(8,128)S(1)}) custom-call(s32[4,4]{1,0:T(4,128)S(1)} %copy-done.2, f32[128,128]{1,0:T(8,128)S(1)} %get-tuple-element.36.refs_0_, f32[128,128]{1,0:T(8,128)S(1)} %collective-permute-done.12.refs_1_, f32[128,128]{1,0:T(8,128)S(1)} %collective-permute-done.13.refs_2_, ...), custom_call_target="tpu_custom_call" | custom-call | tf_op jit(solution)/shard_map/pallas_call | solution.py:231
  54.4 0.7 shard_map.52
  55.1 1.7 %collective-permute-start.15 = (f32[1152,128]{1,0:T(8,128)S(1)}, f32[1152,128]{1,0:T(8,128)S(1)}, u32[]{:S(2)}, u32[]{:S(2)}) collective-permute-start(f32[1152,128]{1,0:T(8,128)S(1)} %get-tuple-element.43), channel_id=1, source_target_pairs={{0,4},{4,5},{2,6},{6,7},{1,0},{5,1},{3,2},{7,3},{8,12},{12,13},{10... | collective-permute-start | bytes 1769480 | tf_op jit(solution)/shard_map/ppermute | solution.py:54
  56.7 1.5 %collective-permute-start.16 = (f32[1152,128]{1,0:T(8,128)S(1)}, f32[1152,128]{1,0:T(8,128)S(1)}, u32[]{:S(2)}, u32[]{:S(2)}) collective-permute-start(f32[1152,128]{1,0:T(8,128)S(1)} %get-tuple-element.44.own_ref), channel_id=1, source_target_pairs={{0,2},{4,1},{2,0},{6,3},{1,8},{5,9},{3,10},{7,11},{8,4},{12,5},{10... | collective-permute-start | bytes 1769480 | tf_op jit(solution)/shard_map/ppermute | solution.py:54
  58.3 12.2 %collective-permute-done.15.u_ref = f32[1152,128]{1,0:T(8,128)S(1)} collective-permute-done((f32[1152,128]{1,0:T(8,128)S(1)}, f32[1152,128]{1,0:T(8,128)S(1)}, u32[]{:S(2)}, u32[]{:S(2)}) %collective-permute-start.15) | collective-permute-done | bytes 589856 | tf_op jit(solution)/shard_map/ppermute | solution.py:54
  70.4 0.6 shard_map.53
  71.0 0.2 collective-permute-start.17
  71.3 1.1 %collective-permute-done.17 = f32[128,128]{1,0:T(8,128)S(1)} collective-permute-done((f32[128,128]{1,0:T(8,128)S(1)}, f32[128,128]{1,0:T(8,128)S(1)}, u32[]{:S(2)}, u32[]{:S(2)}) %collective-permute-start.17) | collective-permute-done | bytes 65568 | tf_op jit(solution)/shard_map/ppermute | solution.py:54
  72.4 1.6 %collective-permute-start.18 = (f32[128,128]{1,0:T(8,128)S(1)}, f32[128,128]{1,0:T(8,128)S(1)}, u32[]{:S(2)}, u32[]{:S(2)}) collective-permute-start(f32[128,128]{1,0:T(8,128)S(1)} %add.7.refs_0_), channel_id=1, source_target_pairs={{0,2},{1,3},{2,0},{3,1},{4,6},{5,7},{6,4},{7,5},{8,10},{9,11},{10,... | collective-permute-start | bytes 196616 | tf_op jit(solution)/shard_map/ppermute | solution.py:54
  74.0 0.1 shard_map.54
  74.1 2.3 %shard_map.55.refs_5_ = f32[512,256]{1,0:T(8,128)S(1)} custom-call(s32[4,4]{1,0:T(4,128)S(1)} %copy-done.2, f32[128,128]{1,0:T(8,128)S(1)} %get-tuple-element.45.mu_ref.refs_2_, f32[128,128]{1,0:T(8,128)S(1)} %get-tuple-element.46.mw_ref.refs_3_), custom_call_target="tpu_custom_call" | custom-call | tf_op jit(solution)/shard_map/pallas_call | solution.py:231
  76.4 0.3 collective-permute-done.18.refs_1_
  76.7 2.9 %shard_map.56 = (f32[1024,256]{1,0:T(8,128)}, f32[512,256]{1,0:T(8,128)}) custom-call(s32[4,4]{1,0:T(4,128)S(1)} %copy-done.2, f32[128,128]{1,0:T(8,128)S(1)} %add.7.refs_0_, f32[128,128]{1,0:T(8,128)S(1)} %collective-permute-done.18.refs_1_, f32[128,128]{1,0:T(8,128)S(1)} %get-tuple-element.45.mu_ref.refs_2_, ...), custom_call_target="tpu_custom_call" | custom-call | tf_op jit(solution)/shard_map/pallas_call | solution.py:571
  (14 shorter events, 0.2 us)
Async XLA Ops:
  0.6 19.1 %collective-permute-start.4 = (f32[1024,256]{1,0:T(8,128)}, f32[1024,256]{1,0:T(8,128)S(1)}, u32[]{:S(2)}, u32[]{:S(2)}) collective-permute-start(f32[1024,256]{1,0:T(8,128)} %refs_0_.1), channel_id=1, source_target_pairs={{0,1},{1,5},{2,3},{3,7},{4,0},{5,4},{6,2},{7,6},{8,9},{9,13},{10,1... | collective-permute-start | bytes 3145736 | tf_op jit(solution)/shard_map/ppermute | solution.py:54
  1.1 1.2 %copy-start = (f32[1024,256]{1,0:T(8,128)S(1)}, f32[1024,256]{1,0:T(8,128)}, u32[]{:S(2)}) copy-start(f32[1024,256]{1,0:T(8,128)} %refs_0_.1) | copy-start | bytes 3145732
  2.3 11.1 %copy-start.1 = (f32[1024,256]{1,0:T(8,128)S(1)}, f32[1024,256]{1,0:T(8,128)}, u32[]{:S(2)}) copy-start(f32[1024,256]{1,0:T(8,128)} %refs_0_.1) | copy-start | bytes 3145732
  3.0 9.1 %copy-start.2 = (s32[4,4]{1,0:T(4,128)S(1)}, s32[4,4]{1,0:T(4,128)}, u32[]{:S(2)}) copy-start(s32[4,4]{1,0:T(4,128)} %offs_ref.13) | copy-start | bytes 196
  3.0 3.2 %collective-permute-start = (f32[264,128]{1,0:T(8,128)S(1)}, f32[264,128]{1,0:T(8,128)S(1)}, u32[]{:S(2)}, u32[]{:S(2)}) collective-permute-start(f32[264,128]{1,0:T(8,128)S(1)} %shard_map.41), channel_id=1, source_target_pairs={{0,1},{1,0},{2,3},{3,2},{4,5},{5,4},{6,7},{7,6},{8,9},{9,8},{10,11... | collective-permute-start | bytes 405512 | tf_op jit(solution)/shard_map/ppermute | solution.py:54
  6.2 5.9 %collective-permute-start.1 = (f32[264,128]{1,0:T(8,128)S(1)}, f32[264,128]{1,0:T(8,128)S(1)}, u32[]{:S(2)}, u32[]{:S(2)}) collective-permute-start(f32[264,128]{1,0:T(8,128)S(1)} %add.6.refs_0_), channel_id=1, source_target_pairs={{0,2},{1,3},{2,0},{3,1},{4,6},{5,7},{6,4},{7,5},{8,10},{9,11},{10,... | collective-permute-start | bytes 405512 | tf_op jit(solution)/shard_map/ppermute | solution.py:54
  14.1 9.7 %collective-permute-start.5 = (f32[1104,128]{1,0:T(8,128)S(1)}, f32[1104,128]{1,0:T(8,128)S(1)}, u32[]{:S(2)}, u32[]{:S(2)}) collective-permute-start(f32[1104,128]{1,0:T(8,128)S(1)} %get-tuple-element.29.own_ref), channel_id=1, source_target_pairs={{0,2},{1,4},{2,0},{3,6},{4,8},{5,12},{6,10},{7,14},{8,1},{9,5},{10... | collective-permute-start | bytes 1695752 | tf_op jit(solution)/shard_map/ppermute | solution.py:54
  15.7 4.0 %collective-permute-start.3 = (f32[1024,128]{1,0:T(8,128)S(1)}, f32[1024,128]{1,0:T(8,128)S(1)}, u32[]{:S(2)}, u32[]{:S(2)}) collective-permute-start(f32[1024,128]{1,0:T(8,128)S(1)} %get-tuple-element.28), channel_id=1, source_target_pairs={{0,1},{1,0},{2,3},{3,2},{4,5},{5,4},{6,7},{7,6},{8,9},{9,8},{10,11... | collective-permute-start | bytes 1572872 | tf_op jit(solution)/shard_map/ppermute | solution.py:54
  15.7 4.0 %collective-permute-start.2 = (f32[80,128]{1,0:T(8,128)S(1)}, f32[80,128]{1,0:T(8,128)S(1)}, u32[]{:S(2)}, u32[]{:S(2)}) collective-permute-start(f32[80,128]{1,0:T(8,128)S(1)} %get-tuple-element.25.near_ref), channel_id=1, source_target_pairs={{0,1},{1,5},{2,3},{3,7},{4,0},{5,4},{6,2},{7,6},{8,9},{9,13},{10,1... | collective-permute-start | bytes 122888 | tf_op jit(solution)/shard_map/ppermute | solution.py:54
  24.4 18.1 %collective-permute-start.11 = (f32[1024,256]{1,0:T(8,128)S(1)}, f32[1024,256]{1,0:T(8,128)S(1)}, u32[]{:S(2)}, u32[]{:S(2)}) collective-permute-start(f32[1024,256]{1,0:T(8,128)S(1)} %get-tuple-element.35.refs_0_), channel_id=1, source_target_pairs={{0,0},{4,4},{2,2},{6,6},{1,8},{5,12},{3,10},{7,14},{8,1},{12,5},{1... | collective-permute-start | bytes 3145736 | tf_op jit(solution)/shard_map/ppermute | solution.py:54
  25.1 9.6 %collective-permute-start.8 = (f32[128,128]{1,0:T(8,128)S(1)}, f32[128,128]{1,0:T(8,128)S(1)}, u32[]{:S(2)}, u32[]{:S(2)}) collective-permute-start(f32[128,128]{1,0:T(8,128)S(1)} %get-tuple-element.30.refs_0_), channel_id=1, source_target_pairs={{0,6},{4,2},{2,4},{6,0},{1,7},{5,3},{3,5},{7,1},{8,14},{12,10},{10... | collective-permute-start | bytes 196616 | tf_op jit(solution)/shard_map/ppermute | solution.py:54
  32.5 4.6 %collective-permute-start.7 = (f32[128,128]{1,0:T(8,128)S(1)}, f32[128,128]{1,0:T(8,128)S(1)}, u32[]{:S(2)}, u32[]{:S(2)}) collective-permute-start(f32[128,128]{1,0:T(8,128)S(1)} %get-tuple-element.30.refs_0_), channel_id=1, source_target_pairs={{0,2},{4,6},{2,0},{6,4},{1,3},{5,7},{3,1},{7,5},{8,10},{12,14},{10... | collective-permute-start | bytes 196616 | tf_op jit(solution)/shard_map/ppermute | solution.py:54
  33.0 4.3 %collective-permute-start.6 = (f32[128,128]{1,0:T(8,128)S(1)}, f32[128,128]{1,0:T(8,128)S(1)}, u32[]{:S(2)}, u32[]{:S(2)}) collective-permute-start(f32[128,128]{1,0:T(8,128)S(1)} %get-tuple-element.30.refs_0_), channel_id=1, source_target_pairs={{0,4},{4,0},{2,6},{6,2},{1,5},{5,1},{3,7},{7,3},{8,12},{12,8},{10,... | collective-permute-start | bytes 196616 | tf_op jit(solution)/shard_map/ppermute | solution.py:54
  39.3 3.1 %collective-permute-start.9 = (f32[1120,128]{1,0:T(8,128)S(1)}, f32[1120,128]{1,0:T(8,128)S(1)}, u32[]{:S(2)}, u32[]{:S(2)}) collective-permute-start(f32[1120,128]{1,0:T(8,128)S(1)} %shard_map.47), channel_id=1, source_target_pairs={{0,1},{4,5},{2,3},{6,7},{1,0},{5,4},{3,2},{7,6},{8,9},{12,13},{10,... | collective-permute-start | bytes 1720328 | tf_op jit(solution)/shard_map/ppermute | solution.py:54
  40.9 4.1 %collective-permute-start.10 = (f32[96,128]{1,0:T(8,128)S(1)}, f32[96,128]{1,0:T(8,128)S(1)}, u32[]{:S(2)}, u32[]{:S(2)}) collective-permute-start(f32[96,128]{1,0:T(8,128)S(1)} %get-tuple-element.34.far_ref.own_ref), channel_id=1, source_target_pairs={{0,2},{4,6},{2,0},{6,4},{1,8},{5,12},{3,10},{7,14},{8,1},{12,5},{1... | collective-permute-start | bytes 147464 | tf_op jit(solution)/shard_map/ppermute | solution.py:54
  45.6 5.2 %collective-permute-start.14 = (f32[128,128]{1,0:T(8,128)S(1)}, f32[128,128]{1,0:T(8,128)S(1)}, u32[]{:S(2)}, u32[]{:S(2)}) collective-permute-start(f32[128,128]{1,0:T(8,128)S(1)} %get-tuple-element.36.refs_0_), channel_id=1, source_target_pairs={{0,6},{4,2},{2,4},{6,0},{1,7},{5,3},{3,5},{7,1},{8,14},{12,10},{10... | collective-permute-start | bytes 196616 | tf_op jit(solution)/shard_map/ppermute | solution.py:54
  48.0 5.0 %collective-permute-start.13 = (f32[128,128]{1,0:T(8,128)S(1)}, f32[128,128]{1,0:T(8,128)S(1)}, u32[]{:S(2)}, u32[]{:S(2)}) collective-permute-start(f32[128,128]{1,0:T(8,128)S(1)} %get-tuple-element.36.refs_0_), channel_id=1, source_target_pairs={{0,2},{4,6},{2,0},{6,4},{1,3},{5,7},{3,1},{7,5},{8,10},{12,14},{10... | collective-permute-start | bytes 196616 | tf_op jit(solution)/shard_map/ppermute | solution.py:54
  48.5 4.4 %collective-permute-start.12 = (f32[128,128]{1,0:T(8,128)S(1)}, f32[128,128]{1,0:T(8,128)S(1)}, u32[]{:S(2)}, u32[]{:S(2)}) collective-permute-start(f32[128,128]{1,0:T(8,128)S(1)} %get-tuple-element.36.refs_0_), channel_id=1, source_target_pairs={{0,4},{4,0},{2,6},{6,2},{1,5},{5,1},{3,7},{7,3},{8,12},{12,8},{10,... | collective-permute-start | bytes 196616 | tf_op jit(solution)/shard_map/ppermute | solution.py:54
  55.1 15.4 %collective-permute-start.15 = (f32[1152,128]{1,0:T(8,128)S(1)}, f32[1152,128]{1,0:T(8,128)S(1)}, u32[]{:S(2)}, u32[]{:S(2)}) collective-permute-start(f32[1152,128]{1,0:T(8,128)S(1)} %get-tuple-element.43), channel_id=1, source_target_pairs={{0,4},{4,5},{2,6},{6,7},{1,0},{5,1},{3,2},{7,3},{8,12},{12,13},{10... | collective-permute-start | bytes 1769480 | tf_op jit(solution)/shard_map/ppermute | solution.py:54
  56.7 13.7 %collective-permute-start.16 = (f32[1152,128]{1,0:T(8,128)S(1)}, f32[1152,128]{1,0:T(8,128)S(1)}, u32[]{:S(2)}, u32[]{:S(2)}) collective-permute-start(f32[1152,128]{1,0:T(8,128)S(1)} %get-tuple-element.44.own_ref), channel_id=1, source_target_pairs={{0,2},{4,1},{2,0},{6,3},{1,8},{5,9},{3,10},{7,11},{8,4},{12,5},{10... | collective-permute-start | bytes 1769480 | tf_op jit(solution)/shard_map/ppermute | solution.py:54
  71.0 1.3 %collective-permute-start.17 = (f32[128,128]{1,0:T(8,128)S(1)}, f32[128,128]{1,0:T(8,128)S(1)}, u32[]{:S(2)}, u32[]{:S(2)}) collective-permute-start(f32[128,128]{1,0:T(8,128)S(1)} %shard_map.53), channel_id=1, source_target_pairs={{0,1},{1,0},{2,3},{3,2},{4,5},{5,4},{6,7},{7,6},{8,9},{9,8},{10,11... | collective-permute-start | bytes 196616 | tf_op jit(solution)/shard_map/ppermute | solution.py:54
  72.4 4.3 %collective-permute-start.18 = (f32[128,128]{1,0:T(8,128)S(1)}, f32[128,128]{1,0:T(8,128)S(1)}, u32[]{:S(2)}, u32[]{:S(2)}) collective-permute-start(f32[128,128]{1,0:T(8,128)S(1)} %add.7.refs_0_), channel_id=1, source_target_pairs={{0,2},{1,3},{2,0},{3,1},{4,6},{5,7},{6,4},{7,5},{8,10},{9,11},{10,... | collective-permute-start | bytes 196616 | tf_op jit(solution)/shard_map/ppermute | solution.py:54

commit v7 on v6

--- a/solution.py
+++ b/solution.py
@@ -331,7 +331,8 @@
         swapped = jnp.concatenate([rotation[B:], rotation[:B]], axis=0)
         rotation = jnp.where(place.odd, rotation, swapped)
     if len(outs) == 1:
-        rotation = jnp.where(place.gives_first[0], rotation[:, :B], rotation[:, B:])
+        side = place.gives_first[0 if ways[1] == RAW else 1]
+        rotation = jnp.where(side, rotation[:, :B], rotation[:, B:])
     x = product(x, rotation)
     messages = [m for m, way in zip((near_ref, far_ref), ways) if way != RAW]
     sides = [g for g, way in zip(place.gives_first, ways) if way != RAW]
@@ -368,7 +369,7 @@
     return jnp.concatenate([jnp.where(take_first, top, low) for top, low in halves], axis=0)
 
 
-def arrive_kernel(block_ref, u_ref, w_ref, own_ref, x_ref, gram_ref, mw_ref):
+def arrive_kernel(block_ref, w_ref, own_ref, x_ref, mw_ref):
     rows = x_ref.shape[0]
     place = Place(crossed)
     own = place.stays
@@ -394,13 +395,19 @@
     def _():
         put(even, w_ref[:rows, :])
 
-    gram_ref[...] = transposed_dot(x_ref[:, :B], x_ref[:, B:])
-
-
-def arrive(block, u, w, own):
+
+def arrive(block, w, own):
     rows = block.shape[0]
-    shapes = [(rows, 2 * B), (B, B), u.shape]
-    return call(arrive_kernel, shapes, (block, u, w, own))
+    shapes = [(rows, 2 * B), (w.shape[0] - rows, B)]
+    return call(arrive_kernel, shapes, (block, w, own))
+
+
+def pair_gram_kernel(x_ref, out_ref):
+    out_ref[...] = transposed_dot(x_ref[:, :B], x_ref[:, B:])
+
+
+def pair_gram(x):
+    return call(pair_gram_kernel, [(B, B)], (x,))[0]
 
 
 def ahead_kernel(u_ref, raw_ref, out_ref):
@@ -602,14 +609,15 @@
     terms = in_stages(whole_gram(whitened), given)
     rotation, near, far = solved(0, given, offsets, terms)
     u = send(near, given, crossed, inner)
-    block, far = turned(rows, (EITHER, JOINED), given, rotation, near, far, whitened)
+    (block,) = turned(rows, (EITHER, RAW), given, rotation, near, far, whitened)
+    (far,) = turned(rows, (RAW, JOINED), given, rotation, near, far, whitened)
     w = send(far, given, crossed, outer)
     block = send(block, given, given, other_part(1))
     block = ready(0, offsets, u, block, raw)
-    x, cross, mw = arrive(block, u, w, far)
+    x, mw = arrive(block, w, far)
 
     raw = send(x, crossed, crossed, outer, swap=False)
-    terms = at_once(cross, crossed)
+    terms = at_once(pair_gram(x), crossed)
     rotation, near, far = solved(1, crossed, offsets, terms, (u, mw))
     w = send(far, crossed, crossed, outer)
     (near,) = turned(rows, (JOINED, RAW), crossed, rotation, near, far, x)
@@ -619,7 +627,9 @@
 
     terms = at_once(cross, crossed)
     rotation, near, far = solved(2, crossed, offsets, terms, (mu, mw))
-    near, far = turned(rows, (JOINED, JOINED), crossed, rotation, near, far, u, block)
+    (joined,) = turned(rows, (RAW, JOINED), crossed, rotation, near, far, u, block)
+    (near,) = turned(rows, (JOINED, RAW), crossed, rotation, near, far, u, block)
+    far = joined
     w = send(far, crossed, given, outer)
     u = send(near, crossed, given, inner)
     terms = in_stages(last_gram(rows, (u, w, far)), given)

time: 80.3 us -> 79.8 us (level)
  waiting for transfers between devices: 35 us -> 33.8 us
  Pallas kernels: 15.9 us -> 16.9 us
    ppermute x19, waiting for transfers between devices: 35 us -> 33.8 us  [send(): return lax.ppermute(x, AXES, route(source, target, change, swap))]
    pallas_call x15 -> x18, Pallas kernels: 13 us -> 14.1 us  [call(): pl.pallas_call(kernel, out_shape=tuple((jax.ShapeDtypeStruct(shape, jnp.f...]
  transfers between devices with their start and end apart: 19 -> 19, of which waited for: 14 -> 15; matrix products, arithmetic and copies ran while one was open for 0% -> 0% of each run, Pallas kernels for 11% -> 13%
where the time goes in v7:
time: 79.8 us; the launch traced here: 79.6 us
  waiting for transfers between devices  33.8 us (42%)
  starting transfers between devices  26.6 us (33%)
  Pallas kernels  16.9 us (21%)
  local copies, waits for them, and re-layouts  1.23 us (2%)
  between operations  0.96 us (1%)
    ppermute x19, waiting for transfers between devices, send(): return lax.ppermute(x, AXES, route(source, target, change, swap))  33.8 us
    ppermute x19, starting transfers between devices, send(): return lax.ppermute(x, AXES, route(source, target, change, swap))  26.6 us
    pallas_call x18, Pallas kernels, call(): pl.pallas_call(kernel, out_shape=tuple((jax.ShapeDtypeStruct(shape, jnp.f...  14.1 us
    pallas_call x1, Pallas kernels, last_step(): pl.pallas_call(functools.partial(last_kernel, len(parts)), out_shape=tupl...  2.86 us
  transfers between devices with their start and end apart: 19, of which 15 were waited for; matrix products, arithmetic and copies ran while one was open for 0% of the time, Pallas kernels for 13%

profile of v7, /device:TPU:0, one launch (start us, length us, event | category | flops | bytes accessed | tf_op | source)
XLA Modules:
  0.0 79.6 jit_solution(11979374995114853431)
XLA Ops:
  0.6 0.5 collective-permute-start.4
  1.1 1.2 %copy-done = f32[1024,256]{1,0:T(8,128)S(1)} copy-done((f32[1024,256]{1,0:T(8,128)S(1)}, f32[1024,256]{1,0:T(8,128)}, u32[]{:S(2)}) %copy-start) | copy-done | bytes 1048600
  2.3 0.7 shard_map.41
  3.0 2.2 %collective-permute-start = (f32[264,128]{1,0:T(8,128)S(1)}, f32[264,128]{1,0:T(8,128)S(1)}, u32[]{:S(2)}, u32[]{:S(2)}) collective-permute-start(f32[264,128]{1,0:T(8,128)S(1)} %shard_map.41), channel_id=1, source_target_pairs={{0,1},{1,0},{2,3},{3,2},{4,5},{5,4},{6,7},{7,6},{8,9},{9,8},{10,11... | collective-permute-start | bytes 405512 | tf_op jit(solution)/shard_map/ppermute | solution.py:54
  5.2 1.0 %collective-permute-done = f32[264,128]{1,0:T(8,128)S(1)} collective-permute-done((f32[264,128]{1,0:T(8,128)S(1)}, f32[264,128]{1,0:T(8,128)S(1)}, u32[]{:S(2)}, u32[]{:S(2)}) %collective-permute-start) | collective-permute-done | bytes 135200 | tf_op jit(solution)/shard_map/ppermute | solution.py:54
  6.2 1.6 %collective-permute-start.1 = (f32[264,128]{1,0:T(8,128)S(1)}, f32[264,128]{1,0:T(8,128)S(1)}, u32[]{:S(2)}, u32[]{:S(2)}) collective-permute-start(f32[264,128]{1,0:T(8,128)S(1)} %add.6.refs_0_), channel_id=1, source_target_pairs={{0,2},{1,3},{2,0},{3,1},{4,6},{5,7},{6,4},{7,5},{8,10},{9,11},{10,... | collective-permute-start | bytes 405512 | tf_op jit(solution)/shard_map/ppermute | solution.py:54
  7.8 4.3 %collective-permute-done.1.refs_1_ = f32[264,128]{1,0:T(8,128)S(1)} collective-permute-done((f32[264,128]{1,0:T(8,128)S(1)}, f32[264,128]{1,0:T(8,128)S(1)}, u32[]{:S(2)}, u32[]{:S(2)}) %collective-permute-start.1) | collective-permute-done | bytes 135200 | tf_op jit(solution)/shard_map/ppermute | solution.py:54
  12.1 1.3 %shard_map.42 = (f32[256,256]{1,0:T(8,128)S(1)}, f32[80,128]{1,0:T(8,128)S(1)}, f32[80,128]{1,0:T(8,128)S(1)}) custom-call(s32[4,4]{1,0:T(4,128)S(1)} %copy-done.2, f32[264,128]{1,0:T(8,128)S(1)} %add.6.refs_0_, f32[264,128]{1,0:T(8,128)S(1)} %collective-permute-done.1.refs_1_), custom_call_target="tpu_custom_call" | custom-call | tf_op jit(solution)/shard_map/pallas_call | solution.py:231
  13.5 0.6 shard_map.45.own_ref
  14.1 1.6 %collective-permute-start.5 = (f32[1104,128]{1,0:T(8,128)S(1)}, f32[1104,128]{1,0:T(8,128)S(1)}, u32[]{:S(2)}, u32[]{:S(2)}) collective-permute-start(f32[1104,128]{1,0:T(8,128)S(1)} %shard_map.45.own_ref), channel_id=1, source_target_pairs={{0,2},{1,4},{2,0},{3,6},{4,8},{5,12},{6,10},{7,14},{8,1},{9,5},{10... | collective-permute-start | bytes 1695752 | tf_op jit(solution)/shard_map/ppermute | solution.py:54
  15.6 0.6 shard_map.43
  16.3 0.5 collective-permute-start.2
  16.8 3.5 %collective-permute-done.2.u_ref.refs_4_ = f32[80,128]{1,0:T(8,128)S(1)} collective-permute-done((f32[80,128]{1,0:T(8,128)S(1)}, f32[80,128]{1,0:T(8,128)S(1)}, u32[]{:S(2)}, u32[]{:S(2)}) %collective-permute-start.2) | collective-permute-done | bytes 40992 | tf_op jit(solution)/shard_map/ppermute | solution.py:54
  20.3 1.0 %shard_map.44.block_ref = f32[1024,128]{1,0:T(8,128)S(1)} custom-call(s32[4,4]{1,0:T(4,128)S(1)} %copy-done.2, f32[80,128]{1,0:T(8,128)S(1)} %collective-permute-done.2.u_ref.refs_4_, f32[1024,128]{1,0:T(8,128)S(1)} %collective-permute-done.3.block_ref, f32[1024,256]{1,0:T(8,128)S(1)} %collective-permute-done.4.raw_ref), custom_call_target="tpu_custom_call" | custom-call | tf_op jit(solution)/shard_map/pallas_call | solution.py:231
  21.3 2.4 %collective-permute-done.5.w_ref = f32[1104,128]{1,0:T(8,128)S(1)} collective-permute-done((f32[1104,128]{1,0:T(8,128)S(1)}, f32[1104,128]{1,0:T(8,128)S(1)}, u32[]{:S(2)}, u32[]{:S(2)}) %collective-permute-start.5) | collective-permute-done | bytes 565280 | tf_op jit(solution)/shard_map/ppermute | solution.py:54
  23.7 0.1 shard_map.46
  23.9 0.7 collective-permute-start.11
  24.6 0.4 shard_map.47.refs_0_
  25.0 7.4 %collective-permute-start.8 = (f32[128,128]{1,0:T(8,128)S(1)}, f32[128,128]{1,0:T(8,128)S(1)}, u32[]{:S(2)}, u32[]{:S(2)}) collective-permute-start(f32[128,128]{1,0:T(8,128)S(1)} %shard_map.47.refs_0_), channel_id=1, source_target_pairs={{0,6},{4,2},{2,4},{6,0},{1,7},{5,3},{3,5},{7,1},{8,14},{12,10},{10... | collective-permute-start | bytes 196616 | tf_op jit(solution)/shard_map/ppermute | solution.py:54
  32.4 0.5 collective-permute-start.7
  33.1 1.6 %collective-permute-done.8.refs_3_ = f32[128,128]{1,0:T(8,128)S(1)} collective-permute-done((f32[128,128]{1,0:T(8,128)S(1)}, f32[128,128]{1,0:T(8,128)S(1)}, u32[]{:S(2)}, u32[]{:S(2)}) %collective-permute-start.8) | collective-permute-done | bytes 65568 | tf_op jit(solution)/shard_map/ppermute | solution.py:54
  34.7 2.5 %collective-permute-done.7.refs_2_ = f32[128,128]{1,0:T(8,128)S(1)} collective-permute-done((f32[128,128]{1,0:T(8,128)S(1)}, f32[128,128]{1,0:T(8,128)S(1)}, u32[]{:S(2)}, u32[]{:S(2)}) %collective-permute-start.7) | collective-permute-done | bytes 65568 | tf_op jit(solution)/shard_map/ppermute | solution.py:54
  37.2 1.4 %shard_map.48 = (f32[256,256]{1,0:T(8,128)S(1)}, f32[96,128]{1,0:T(8,128)S(1)}, f32[96,128]{1,0:T(8,128)S(1)}) custom-call(s32[4,4]{1,0:T(4,128)S(1)} %copy-done.2, f32[128,128]{1,0:T(8,128)S(1)} %shard_map.47.refs_0_, f32[128,128]{1,0:T(8,128)S(1)} %collective-permute-done.6.refs_1_, f32[128,128]{1,0:T(8,128)S(1)} %collective-permute-done.7.refs_2_, ...), custom_call_target="tpu_custom_call" | custom-call | tf_op jit(solution)/shard_map/pallas_call | solution.py:231
  38.7 0.6 shard_map.49
  39.3 1.5 %collective-permute-start.9 = (f32[1120,128]{1,0:T(8,128)S(1)}, f32[1120,128]{1,0:T(8,128)S(1)}, u32[]{:S(2)}, u32[]{:S(2)}) collective-permute-start(f32[1120,128]{1,0:T(8,128)S(1)} %shard_map.49), channel_id=1, source_target_pairs={{0,1},{4,5},{2,3},{6,7},{1,0},{5,4},{3,2},{7,6},{8,9},{12,13},{10,... | collective-permute-start | bytes 1720328 | tf_op jit(solution)/shard_map/ppermute | solution.py:54
  40.8 1.5 %collective-permute-start.10 = (f32[96,128]{1,0:T(8,128)S(1)}, f32[96,128]{1,0:T(8,128)S(1)}, u32[]{:S(2)}, u32[]{:S(2)}) collective-permute-start(f32[96,128]{1,0:T(8,128)S(1)} %get-tuple-element.27.far_ref.own_ref), channel_id=1, source_target_pairs={{0,2},{4,6},{2,0},{6,4},{1,8},{5,12},{3,10},{7,14},{8,1},{12,5},{1... | collective-permute-start | bytes 147464 | tf_op jit(solution)/shard_map/ppermute | solution.py:54
  42.4 0.4 shard_map.50.ahead_ref
  42.9 2.1 %collective-permute-done.10.w_ref = f32[96,128]{1,0:T(8,128)S(1)} collective-permute-done((f32[96,128]{1,0:T(8,128)S(1)}, f32[96,128]{1,0:T(8,128)S(1)}, u32[]{:S(2)}, u32[]{:S(2)}) %collective-permute-start.10) | collective-permute-done | bytes 49184 | tf_op jit(solution)/shard_map/ppermute | solution.py:54
  44.9 0.7 shard_map.51
  45.6 2.3 %collective-permute-start.14 = (f32[128,128]{1,0:T(8,128)S(1)}, f32[128,128]{1,0:T(8,128)S(1)}, u32[]{:S(2)}, u32[]{:S(2)}) collective-permute-start(f32[128,128]{1,0:T(8,128)S(1)} %get-tuple-element.28.refs_0_), channel_id=1, source_target_pairs={{0,6},{4,2},{2,4},{6,0},{1,7},{5,3},{3,5},{7,1},{8,14},{12,10},{10... | collective-permute-start | bytes 196616 | tf_op jit(solution)/shard_map/ppermute | solution.py:54
  47.9 0.5 collective-permute-start.13
  48.5 0.7 collective-permute-start.12
  49.2 0.6 shard_map.53.refs_1_
  49.8 1.2 %collective-permute-done.14.refs_3_ = f32[128,128]{1,0:T(8,128)S(1)} collective-permute-done((f32[128,128]{1,0:T(8,128)S(1)}, f32[128,128]{1,0:T(8,128)S(1)}, u32[]{:S(2)}, u32[]{:S(2)}) %collective-permute-start.14) | collective-permute-done | bytes 65568 | tf_op jit(solution)/shard_map/ppermute | solution.py:54
  51.0 1.6 %collective-permute-done.13.refs_2_ = f32[128,128]{1,0:T(8,128)S(1)} collective-permute-done((f32[128,128]{1,0:T(8,128)S(1)}, f32[128,128]{1,0:T(8,128)S(1)}, u32[]{:S(2)}, u32[]{:S(2)}) %collective-permute-start.13) | collective-permute-done | bytes 65568 | tf_op jit(solution)/shard_map/ppermute | solution.py:54
  52.6 0.5 collective-permute-done.12.refs_1_
  53.1 1.4 %shard_map.52 = (f32[256,256]{1,0:T(8,128)S(1)}, f32[128,128]{1,0:T(8,128)S(1)}, f32[128,128]{1,0:T(8,128)S(1)}) custom-call(s32[4,4]{1,0:T(4,128)S(1)} %copy-done.2, f32[128,128]{1,0:T(8,128)S(1)} %get-tuple-element.28.refs_0_, f32[128,128]{1,0:T(8,128)S(1)} %collective-permute-done.12.refs_1_, f32[128,128]{1,0:T(8,128)S(1)} %collective-permute-done.13.refs_2_, ...), custom_call_target="tpu_custom_call" | custom-call | tf_op jit(solution)/shard_map/pallas_call | solution.py:231
  54.6 0.6 shard_map.54
  55.2 1.4 %collective-permute-start.15 = (f32[1152,128]{1,0:T(8,128)S(1)}, f32[1152,128]{1,0:T(8,128)S(1)}, u32[]{:S(2)}, u32[]{:S(2)}) collective-permute-start(f32[1152,128]{1,0:T(8,128)S(1)} %shard_map.54), channel_id=1, source_target_pairs={{0,4},{4,5},{2,6},{6,7},{1,0},{5,1},{3,2},{7,3},{8,12},{12,13},{10... | collective-permute-start | bytes 1769480 | tf_op jit(solution)/shard_map/ppermute | solution.py:54
  56.6 0.6 shard_map.55.own_ref
  57.2 1.7 %collective-permute-start.16 = (f32[1152,128]{1,0:T(8,128)S(1)}, f32[1152,128]{1,0:T(8,128)S(1)}, u32[]{:S(2)}, u32[]{:S(2)}) collective-permute-start(f32[1152,128]{1,0:T(8,128)S(1)} %shard_map.55.own_ref), channel_id=1, source_target_pairs={{0,2},{4,1},{2,0},{6,3},{1,8},{5,9},{3,10},{7,11},{8,4},{12,5},{10... | collective-permute-start | bytes 1769480 | tf_op jit(solution)/shard_map/ppermute | solution.py:54
  58.9 11.5 %collective-permute-done.15.u_ref = f32[1152,128]{1,0:T(8,128)S(1)} collective-permute-done((f32[1152,128]{1,0:T(8,128)S(1)}, f32[1152,128]{1,0:T(8,128)S(1)}, u32[]{:S(2)}, u32[]{:S(2)}) %collective-permute-start.15) | collective-permute-done | bytes 589856 | tf_op jit(solution)/shard_map/ppermute | solution.py:54
  70.3 0.6 shard_map.56
  71.0 1.2 %collective-permute-done.17 = f32[128,128]{1,0:T(8,128)S(1)} collective-permute-done((f32[128,128]{1,0:T(8,128)S(1)}, f32[128,128]{1,0:T(8,128)S(1)}, u32[]{:S(2)}, u32[]{:S(2)}) %collective-permute-start.17) | collective-permute-done | bytes 65568 | tf_op jit(solution)/shard_map/ppermute | solution.py:54
  72.2 1.7 %collective-permute-start.18 = (f32[128,128]{1,0:T(8,128)S(1)}, f32[128,128]{1,0:T(8,128)S(1)}, u32[]{:S(2)}, u32[]{:S(2)}) collective-permute-start(f32[128,128]{1,0:T(8,128)S(1)} %add.7.refs_0_), channel_id=1, source_target_pairs={{0,2},{1,3},{2,0},{3,1},{4,6},{5,7},{6,4},{7,5},{8,10},{9,11},{10,... | collective-permute-start | bytes 196616 | tf_op jit(solution)/shard_map/ppermute | solution.py:54
  74.1 2.3 %shard_map.58.refs_5_ = f32[512,256]{1,0:T(8,128)S(1)} custom-call(s32[4,4]{1,0:T(4,128)S(1)} %copy-done.2, f32[128,128]{1,0:T(8,128)S(1)} %get-tuple-element.35.mu_ref.refs_2_, f32[128,128]{1,0:T(8,128)S(1)} %get-tuple-element.36.mw_ref.refs_3_), custom_call_target="tpu_custom_call" | custom-call | tf_op jit(solution)/shard_map/pallas_call | solution.py:231
  76.4 0.2 collective-permute-done.18.refs_1_
  76.6 2.9 %shard_map.59 = (f32[1024,256]{1,0:T(8,128)}, f32[512,256]{1,0:T(8,128)}) custom-call(s32[4,4]{1,0:T(4,128)S(1)} %copy-done.2, f32[128,128]{1,0:T(8,128)S(1)} %add.7.refs_0_, f32[128,128]{1,0:T(8,128)S(1)} %collective-permute-done.18.refs_1_, f32[128,128]{1,0:T(8,128)S(1)} %get-tuple-element.35.mu_ref.refs_2_, ...), custom_call_target="tpu_custom_call" | custom-call | tf_op jit(solution)/shard_map/pallas_call | solution.py:578
  (17 shorter events, 0.7 us)
Async XLA Ops:
  0.6 19.7 %collective-permute-start.4 = (f32[1024,256]{1,0:T(8,128)}, f32[1024,256]{1,0:T(8,128)S(1)}, u32[]{:S(2)}, u32[]{:S(2)}) collective-permute-start(f32[1024,256]{1,0:T(8,128)} %refs_0_.3), channel_id=1, source_target_pairs={{0,1},{1,5},{2,3},{3,7},{4,0},{5,4},{6,2},{7,6},{8,9},{9,13},{10,1... | collective-permute-start | bytes 3145736 | tf_op jit(solution)/shard_map/ppermute | solution.py:54
  1.1 1.2 %copy-start = (f32[1024,256]{1,0:T(8,128)S(1)}, f32[1024,256]{1,0:T(8,128)}, u32[]{:S(2)}) copy-start(f32[1024,256]{1,0:T(8,128)} %refs_0_.3) | copy-start | bytes 3145732
  2.3 11.1 %copy-start.1 = (f32[1024,256]{1,0:T(8,128)S(1)}, f32[1024,256]{1,0:T(8,128)}, u32[]{:S(2)}) copy-start(f32[1024,256]{1,0:T(8,128)} %refs_0_.3) | copy-start | bytes 3145732
  3.0 9.1 %copy-start.2 = (s32[4,4]{1,0:T(4,128)S(1)}, s32[4,4]{1,0:T(4,128)}, u32[]{:S(2)}) copy-start(s32[4,4]{1,0:T(4,128)} %offs_ref.13) | copy-start | bytes 196
  3.0 3.2 %collective-permute-start = (f32[264,128]{1,0:T(8,128)S(1)}, f32[264,128]{1,0:T(8,128)S(1)}, u32[]{:S(2)}, u32[]{:S(2)}) collective-permute-start(f32[264,128]{1,0:T(8,128)S(1)} %shard_map.41), channel_id=1, source_target_pairs={{0,1},{1,0},{2,3},{3,2},{4,5},{5,4},{6,7},{7,6},{8,9},{9,8},{10,11... | collective-permute-start | bytes 405512 | tf_op jit(solution)/shard_map/ppermute | solution.py:54
  6.2 5.9 %collective-permute-start.1 = (f32[264,128]{1,0:T(8,128)S(1)}, f32[264,128]{1,0:T(8,128)S(1)}, u32[]{:S(2)}, u32[]{:S(2)}) collective-permute-start(f32[264,128]{1,0:T(8,128)S(1)} %add.6.refs_0_), channel_id=1, source_target_pairs={{0,2},{1,3},{2,0},{3,1},{4,6},{5,7},{6,4},{7,5},{8,10},{9,11},{10,... | collective-permute-start | bytes 405512 | tf_op jit(solution)/shard_map/ppermute | solution.py:54
  14.1 9.7 %collective-permute-start.5 = (f32[1104,128]{1,0:T(8,128)S(1)}, f32[1104,128]{1,0:T(8,128)S(1)}, u32[]{:S(2)}, u32[]{:S(2)}) collective-permute-start(f32[1104,128]{1,0:T(8,128)S(1)} %shard_map.45.own_ref), channel_id=1, source_target_pairs={{0,2},{1,4},{2,0},{3,6},{4,8},{5,12},{6,10},{7,14},{8,1},{9,5},{10... | collective-permute-start | bytes 1695752 | tf_op jit(solution)/shard_map/ppermute | solution.py:54
  16.2 4.1 %collective-permute-start.3 = (f32[1024,128]{1,0:T(8,128)S(1)}, f32[1024,128]{1,0:T(8,128)S(1)}, u32[]{:S(2)}, u32[]{:S(2)}) collective-permute-start(f32[1024,128]{1,0:T(8,128)S(1)} %shard_map.43), channel_id=1, source_target_pairs={{0,1},{1,0},{2,3},{3,2},{4,5},{5,4},{6,7},{7,6},{8,9},{9,8},{10,11... | collective-permute-start | bytes 1572872 | tf_op jit(solution)/shard_map/ppermute | solution.py:54
  16.3 4.0 %collective-permute-start.2 = (f32[80,128]{1,0:T(8,128)S(1)}, f32[80,128]{1,0:T(8,128)S(1)}, u32[]{:S(2)}, u32[]{:S(2)}) collective-permute-start(f32[80,128]{1,0:T(8,128)S(1)} %get-tuple-element.20.near_ref), channel_id=1, source_target_pairs={{0,1},{1,5},{2,3},{3,7},{4,0},{5,4},{6,2},{7,6},{8,9},{9,13},{10,1... | collective-permute-start | bytes 122888 | tf_op jit(solution)/shard_map/ppermute | solution.py:54
  23.9 18.6 %collective-permute-start.11 = (f32[1024,256]{1,0:T(8,128)S(1)}, f32[1024,256]{1,0:T(8,128)S(1)}, u32[]{:S(2)}, u32[]{:S(2)}) collective-permute-start(f32[1024,256]{1,0:T(8,128)S(1)} %get-tuple-element.23.x_ref.refs_0_), channel_id=1, source_target_pairs={{0,0},{4,4},{2,2},{6,6},{1,8},{5,12},{3,10},{7,14},{8,1},{12,5},{1... | collective-permute-start | bytes 3145736 | tf_op jit(solution)/shard_map/ppermute | solution.py:54
  25.0 9.6 %collective-permute-start.8 = (f32[128,128]{1,0:T(8,128)S(1)}, f32[128,128]{1,0:T(8,128)S(1)}, u32[]{:S(2)}, u32[]{:S(2)}) collective-permute-start(f32[128,128]{1,0:T(8,128)S(1)} %shard_map.47.refs_0_), channel_id=1, source_target_pairs={{0,6},{4,2},{2,4},{6,0},{1,7},{5,3},{3,5},{7,1},{8,14},{12,10},{10... | collective-permute-start | bytes 196616 | tf_op jit(solution)/shard_map/ppermute | solution.py:54
  32.4 4.7 %collective-permute-start.7 = (f32[128,128]{1,0:T(8,128)S(1)}, f32[128,128]{1,0:T(8,128)S(1)}, u32[]{:S(2)}, u32[]{:S(2)}) collective-permute-start(f32[128,128]{1,0:T(8,128)S(1)} %shard_map.47.refs_0_), channel_id=1, source_target_pairs={{0,2},{4,6},{2,0},{6,4},{1,3},{5,7},{3,1},{7,5},{8,10},{12,14},{10... | collective-permute-start | bytes 196616 | tf_op jit(solution)/shard_map/ppermute | solution.py:54
  33.0 4.3 %collective-permute-start.6 = (f32[128,128]{1,0:T(8,128)S(1)}, f32[128,128]{1,0:T(8,128)S(1)}, u32[]{:S(2)}, u32[]{:S(2)}) collective-permute-start(f32[128,128]{1,0:T(8,128)S(1)} %shard_map.47.refs_0_), channel_id=1, source_target_pairs={{0,4},{4,0},{2,6},{6,2},{1,5},{5,1},{3,7},{7,3},{8,12},{12,8},{10,... | collective-permute-start | bytes 196616 | tf_op jit(solution)/shard_map/ppermute | solution.py:54
  39.3 3.1 %collective-permute-start.9 = (f32[1120,128]{1,0:T(8,128)S(1)}, f32[1120,128]{1,0:T(8,128)S(1)}, u32[]{:S(2)}, u32[]{:S(2)}) collective-permute-start(f32[1120,128]{1,0:T(8,128)S(1)} %shard_map.49), channel_id=1, source_target_pairs={{0,1},{4,5},{2,3},{6,7},{1,0},{5,4},{3,2},{7,6},{8,9},{12,13},{10,... | collective-permute-start | bytes 1720328 | tf_op jit(solution)/shard_map/ppermute | solution.py:54
  40.8 4.1 %collective-permute-start.10 = (f32[96,128]{1,0:T(8,128)S(1)}, f32[96,128]{1,0:T(8,128)S(1)}, u32[]{:S(2)}, u32[]{:S(2)}) collective-permute-start(f32[96,128]{1,0:T(8,128)S(1)} %get-tuple-element.27.far_ref.own_ref), channel_id=1, source_target_pairs={{0,2},{4,6},{2,0},{6,4},{1,8},{5,12},{3,10},{7,14},{8,1},{12,5},{1... | collective-permute-start | bytes 147464 | tf_op jit(solution)/shard_map/ppermute | solution.py:54
  45.6 5.4 %collective-permute-start.14 = (f32[128,128]{1,0:T(8,128)S(1)}, f32[128,128]{1,0:T(8,128)S(1)}, u32[]{:S(2)}, u32[]{:S(2)}) collective-permute-start(f32[128,128]{1,0:T(8,128)S(1)} %get-tuple-element.28.refs_0_), channel_id=1, source_target_pairs={{0,6},{4,2},{2,4},{6,0},{1,7},{5,3},{3,5},{7,1},{8,14},{12,10},{10... | collective-permute-start | bytes 196616 | tf_op jit(solution)/shard_map/ppermute | solution.py:54
  47.9 4.7 %collective-permute-start.13 = (f32[128,128]{1,0:T(8,128)S(1)}, f32[128,128]{1,0:T(8,128)S(1)}, u32[]{:S(2)}, u32[]{:S(2)}) collective-permute-start(f32[128,128]{1,0:T(8,128)S(1)} %get-tuple-element.28.refs_0_), channel_id=1, source_target_pairs={{0,2},{4,6},{2,0},{6,4},{1,3},{5,7},{3,1},{7,5},{8,10},{12,14},{10... | collective-permute-start | bytes 196616 | tf_op jit(solution)/shard_map/ppermute | solution.py:54
  48.5 4.6 %collective-permute-start.12 = (f32[128,128]{1,0:T(8,128)S(1)}, f32[128,128]{1,0:T(8,128)S(1)}, u32[]{:S(2)}, u32[]{:S(2)}) collective-permute-start(f32[128,128]{1,0:T(8,128)S(1)} %get-tuple-element.28.refs_0_), channel_id=1, source_target_pairs={{0,4},{4,0},{2,6},{6,2},{1,5},{5,1},{3,7},{7,3},{8,12},{12,8},{10,... | collective-permute-start | bytes 196616 | tf_op jit(solution)/shard_map/ppermute | solution.py:54
  55.2 15.1 %collective-permute-start.15 = (f32[1152,128]{1,0:T(8,128)S(1)}, f32[1152,128]{1,0:T(8,128)S(1)}, u32[]{:S(2)}, u32[]{:S(2)}) collective-permute-start(f32[1152,128]{1,0:T(8,128)S(1)} %shard_map.54), channel_id=1, source_target_pairs={{0,4},{4,5},{2,6},{6,7},{1,0},{5,1},{3,2},{7,3},{8,12},{12,13},{10... | collective-permute-start | bytes 1769480 | tf_op jit(solution)/shard_map/ppermute | solution.py:54
  57.2 13.1 %collective-permute-start.16 = (f32[1152,128]{1,0:T(8,128)S(1)}, f32[1152,128]{1,0:T(8,128)S(1)}, u32[]{:S(2)}, u32[]{:S(2)}) collective-permute-start(f32[1152,128]{1,0:T(8,128)S(1)} %shard_map.55.own_ref), channel_id=1, source_target_pairs={{0,2},{4,1},{2,0},{6,3},{1,8},{5,9},{3,10},{7,11},{8,4},{12,5},{10... | collective-permute-start | bytes 1769480 | tf_op jit(solution)/shard_map/ppermute | solution.py:54
  70.9 1.3 %collective-permute-start.17 = (f32[128,128]{1,0:T(8,128)S(1)}, f32[128,128]{1,0:T(8,128)S(1)}, u32[]{:S(2)}, u32[]{:S(2)}) collective-permute-start(f32[128,128]{1,0:T(8,128)S(1)} %shard_map.56), channel_id=1, source_target_pairs={{0,1},{1,0},{2,3},{3,2},{4,5},{5,4},{6,7},{7,6},{8,9},{9,8},{10,11... | collective-permute-start | bytes 196616 | tf_op jit(solution)/shard_map/ppermute | solution.py:54
  72.2 4.3 %collective-permute-start.18 = (f32[128,128]{1,0:T(8,128)S(1)}, f32[128,128]{1,0:T(8,128)S(1)}, u32[]{:S(2)}, u32[]{:S(2)}) collective-permute-start(f32[128,128]{1,0:T(8,128)S(1)} %add.7.refs_0_), channel_id=1, source_target_pairs={{0,2},{1,3},{2,0},{3,1},{4,6},{5,7},{6,4},{7,5},{8,10},{9,11},{10,... | collective-permute-start | bytes 196616 | tf_op jit(solution)/shard_map/ppermute | solution.py:54

commit v8 on v7

--- a/solution.py
+++ b/solution.py
@@ -320,11 +320,10 @@
     return call(kernel, shapes, (offsets, *parts, *messages))
 
 
-def turn_kernel(ways, layout, ordered, rotation_ref, near_ref, far_ref, *refs):
+def turn_kernel(ways, layout, ordered, rows, left_out, rotation_ref, near_ref, far_ref, *refs):
     count = 1 if ordered else 2
     xs, outs = refs[:count], list(refs[count:])
     place = Place(layout)
-    rows = outs[0].shape[0] - base_excess(ways, near_ref)
     x = jnp.concatenate([x_ref[:rows, :] for x_ref in xs], axis=1)
     rotation = rotation_ref[...]
     if not ordered:
@@ -338,30 +337,29 @@
     sides = [g for g, way in zip(place.gives_first, ways) if way != RAW]
     kept = [way for way in ways if way != RAW]
     for out, message, gives_first, way in zip(outs, messages, sides, kept):
+        start = left_out if message is far_ref else 0
+        size = rows - start
         if way == JOINED:
-            out[rows:, :] = message[...]
+            out[size:, :] = message[...]
         if len(outs) == 1:
-            out[:rows, :] = x
+            out[:size, :] = x[start:]
             continue
 
         @pl.when(gives_first)
         def _():
-            out[:rows, :] = x[:, :B]
+            out[:size, :] = x[start:, :B]
 
         @pl.when(jnp.logical_not(gives_first))
         def _():
-            out[:rows, :] = x[:, B:]
-
-
-def base_excess(ways, message):
-    way = next(w for w in ways if w != RAW)
-    return message.shape[0] if way == JOINED else 0
-
-
-def turned(rows, ways, layout, rotation, near, far, *xs):
-    shapes = [(base_of(way, rows, near), B) for way in ways if way != RAW]
-    kernel = functools.partial(turn_kernel, ways, layout, len(xs) == 1)
-    return call(kernel, shapes, (rotation, near, far, *xs))
+            out[:size, :] = x[start:, B:]
+
+
+def turned(rows, ways, layout, rotation, near, far, *xs, left_out=0):
+    sizes = [base_of(way, rows, near) for way in ways if way != RAW]
+    if ways[1] != RAW:
+        sizes[-1] -= left_out
+    kernel = functools.partial(turn_kernel, ways, layout, len(xs) == 1, rows, left_out)
+    return call(kernel, [(size, B) for size in sizes], (rotation, near, far, *xs))
 
 
 def half_rotation(angles, offs, take_first):
@@ -402,6 +400,14 @@
     return call(arrive_kernel, shapes, (block, w, own))
 
 
+def top_rows_kernel(x_ref, out_ref):
+    out_ref[...] = x_ref[: out_ref.shape[0], :]
+
+
+def top_rows(x, size):
+    return call(top_rows_kernel, [(size, x.shape[1])], (x,))[0]
+
+
 def pair_gram_kernel(x_ref, out_ref):
     out_ref[...] = transposed_dot(x_ref[:, :B], x_ref[:, B:])
 
@@ -423,28 +429,33 @@
     place = Place(crossed)
     own = place.edge
     mu_ref[...] = u_ref[rows:, :]
-    mw_ref[...] = jnp.where(own, own_ref[...], w_ref[...])
-    at = slice(PACKED, PACKED + RECORD)
+    rest = w_ref.shape[0] - mw_ref.shape[0]
+    mw_ref[...] = jnp.where(own, own_ref[rest:, :], w_ref[rest:, :])
+    at = slice(rest + PACKED, rest + PACKED + RECORD)
     angles = read_record(jnp.where(own, own_ref[at, :], w_ref[at, :]))
     takes_first = jnp.logical_or(jnp.logical_not(place.odd), place.slot == place.pairs - 1)
     half = half_rotation(angles, step_offsets(offs_ref, step), takes_first)
     half_ref[...] = half
-    gram = product(ahead_ref[...], half)
+    tail = jnp.where(own, own_ref[:rest, :], w_ref[:rest, :])
+    gram = product(ahead_ref[...], half) + transposed_dot(u_ref[rows - rest : rows, :], tail)
     gram_ref[...] = jnp.where(place.odd, gram, gram.T)
 
 
 def arrive_raw(step, rows, offsets, u, w, own, products):
     kernel = functools.partial(arrive_raw_kernel, step, rows)
-    shapes = [(2 * B, B), (B, B), w.shape, w.shape]
-    return call(kernel, shapes, (offsets, u, w, own, products))
-
-
-def outer_block_kernel(raw_ref, half_ref, out_ref):
-    out_ref[...] = product(raw_ref[...], half_ref[...])
-
-
-def outer_block(raw, half):
-    return call(outer_block_kernel, [(raw.shape[0], B)], (raw, half))[0]
+    small = (u.shape[0] - rows, B)
+    return call(kernel, [(2 * B, B), (B, B), small, small], (offsets, u, w, own, products))
+
+
+def outer_block_kernel(raw_ref, half_ref, w_ref, own_ref, out_ref):
+    size = raw_ref.shape[0]
+    rest = out_ref.shape[0] - size
+    out_ref[:size, :] = product(raw_ref[...], half_ref[...])
+    out_ref[size:, :] = jnp.where(Place(crossed).edge, own_ref[:rest, :], w_ref[:rest, :])
+
+
+def outer_block(rows, raw, half, w, own):
+    return call(outer_block_kernel, [(rows, B)], (raw, half, w, own))[0]
 
 
 def ready_kernel(step, offs_ref, u_ref, block_ref, raw_ref, out_ref):
@@ -616,14 +627,16 @@
     block = ready(0, offsets, u, block, raw)
     x, mw = arrive(block, w, far)
 
-    raw = send(x, crossed, crossed, outer, swap=False)
+    size = rows // 128 * 112
+    raw = send(top_rows(x, size), crossed, crossed, outer, swap=False)
     terms = at_once(pair_gram(x), crossed)
     rotation, near, far = solved(1, crossed, offsets, terms, (u, mw))
+    ways = (JOINED, JOINED)
+    near, far = turned(rows, ways, crossed, rotation, near, far, x, left_out=size)
     w = send(far, crossed, crossed, outer)
-    (near,) = turned(rows, (JOINED, RAW), crossed, rotation, near, far, x)
     u = send(near, crossed, crossed, inner)
     half, cross, mu, mw = arrive_raw(1, rows, offsets, u, w, far, ahead(u, raw))
-    block = outer_block(raw, half)
+    block = outer_block(rows, raw, half, w, far)
 
     terms = at_once(cross, crossed)
     rotation, near, far = solved(2, crossed, offsets, terms, (mu, mw))

time: 79.8 us -> 79.9 us (level)
  waiting for transfers between devices: 33.8 us -> 34.6 us
    pallas_call x18 -> x19, Pallas kernels: 14.1 us -> 14.2 us  [call(): pl.pallas_call(kernel, out_shape=tuple((jax.ShapeDtypeStruct(shape, jnp.f...]
where the time goes in v8:
time: 79.9 us; the launch traced here: 79.7 us
  waiting for transfers between devices  34.6 us (43%)
  starting transfers between devices  25.9 us (32%)
  Pallas kernels  17 us (21%)
  local copies, waits for them, and re-layouts  1.23 us (2%)
  between operations  0.98 us (1%)
    ppermute x19, waiting for transfers between devices, send(): return lax.ppermute(x, AXES, route(source, target, change, swap))  34.6 us
    ppermute x19, starting transfers between devices, send(): return lax.ppermute(x, AXES, route(source, target, change, swap))  25.9 us
    pallas_call x19, Pallas kernels, call(): pl.pallas_call(kernel, out_shape=tuple((jax.ShapeDtypeStruct(shape, jnp.f...  14.2 us
    pallas_call x1, Pallas kernels, last_step(): pl.pallas_call(functools.partial(last_kernel, len(parts)), out_shape=tupl...  2.86 us
  transfers between devices with their start and end apart: 19, of which 15 were waited for; matrix products, arithmetic and copies ran while one was open for 0% of the time, Pallas kernels for 13%

profile of v8, /device:TPU:0, one launch (start us, length us, event | category | flops | bytes accessed | tf_op | source)
XLA Modules:
  0.0 79.7 jit_solution(1161415621485725705)
XLA Ops:
  0.6 0.5 collective-permute-start.4
  1.1 1.2 %copy-done = f32[1024,256]{1,0:T(8,128)S(1)} copy-done((f32[1024,256]{1,0:T(8,128)S(1)}, f32[1024,256]{1,0:T(8,128)}, u32[]{:S(2)}) %copy-start) | copy-done | bytes 1048600
  2.3 0.7 shard_map.41
  3.0 2.2 %collective-permute-start = (f32[264,128]{1,0:T(8,128)S(1)}, f32[264,128]{1,0:T(8,128)S(1)}, u32[]{:S(2)}, u32[]{:S(2)}) collective-permute-start(f32[264,128]{1,0:T(8,128)S(1)} %shard_map.41), channel_id=1, source_target_pairs={{0,1},{1,0},{2,3},{3,2},{4,5},{5,4},{6,7},{7,6},{8,9},{9,8},{10,11... | collective-permute-start | bytes 405512 | tf_op jit(solution)/shard_map/ppermute | solution.py:54
  5.2 1.0 %collective-permute-done = f32[264,128]{1,0:T(8,128)S(1)} collective-permute-done((f32[264,128]{1,0:T(8,128)S(1)}, f32[264,128]{1,0:T(8,128)S(1)}, u32[]{:S(2)}, u32[]{:S(2)}) %collective-permute-start) | collective-permute-done | bytes 135200 | tf_op jit(solution)/shard_map/ppermute | solution.py:54
  6.2 1.6 %collective-permute-start.1 = (f32[264,128]{1,0:T(8,128)S(1)}, f32[264,128]{1,0:T(8,128)S(1)}, u32[]{:S(2)}, u32[]{:S(2)}) collective-permute-start(f32[264,128]{1,0:T(8,128)S(1)} %add.6.refs_0_), channel_id=1, source_target_pairs={{0,2},{1,3},{2,0},{3,1},{4,6},{5,7},{6,4},{7,5},{8,10},{9,11},{10,... | collective-permute-start | bytes 405512 | tf_op jit(solution)/shard_map/ppermute | solution.py:54
  7.8 4.3 %collective-permute-done.1.refs_1_ = f32[264,128]{1,0:T(8,128)S(1)} collective-permute-done((f32[264,128]{1,0:T(8,128)S(1)}, f32[264,128]{1,0:T(8,128)S(1)}, u32[]{:S(2)}, u32[]{:S(2)}) %collective-permute-start.1) | collective-permute-done | bytes 135200 | tf_op jit(solution)/shard_map/ppermute | solution.py:54
  12.1 1.3 %shard_map.42 = (f32[256,256]{1,0:T(8,128)S(1)}, f32[80,128]{1,0:T(8,128)S(1)}, f32[80,128]{1,0:T(8,128)S(1)}) custom-call(s32[4,4]{1,0:T(4,128)S(1)} %copy-done.2, f32[264,128]{1,0:T(8,128)S(1)} %add.6.refs_0_, f32[264,128]{1,0:T(8,128)S(1)} %collective-permute-done.1.refs_1_), custom_call_target="tpu_custom_call" | custom-call | tf_op jit(solution)/shard_map/pallas_call | solution.py:231
  13.5 0.6 shard_map.45.own_ref
  14.1 1.6 %collective-permute-start.5 = (f32[1104,128]{1,0:T(8,128)S(1)}, f32[1104,128]{1,0:T(8,128)S(1)}, u32[]{:S(2)}, u32[]{:S(2)}) collective-permute-start(f32[1104,128]{1,0:T(8,128)S(1)} %shard_map.45.own_ref), channel_id=1, source_target_pairs={{0,2},{1,4},{2,0},{3,6},{4,8},{5,12},{6,10},{7,14},{8,1},{9,5},{10... | collective-permute-start | bytes 1695752 | tf_op jit(solution)/shard_map/ppermute | solution.py:54
  15.6 0.6 shard_map.43
  16.3 0.5 collective-permute-start.2
  16.8 3.5 %collective-permute-done.2.u_ref.refs_4_ = f32[80,128]{1,0:T(8,128)S(1)} collective-permute-done((f32[80,128]{1,0:T(8,128)S(1)}, f32[80,128]{1,0:T(8,128)S(1)}, u32[]{:S(2)}, u32[]{:S(2)}) %collective-permute-start.2) | collective-permute-done | bytes 40992 | tf_op jit(solution)/shard_map/ppermute | solution.py:54
  20.3 1.0 %shard_map.44.block_ref = f32[1024,128]{1,0:T(8,128)S(1)} custom-call(s32[4,4]{1,0:T(4,128)S(1)} %copy-done.2, f32[80,128]{1,0:T(8,128)S(1)} %collective-permute-done.2.u_ref.refs_4_, f32[1024,128]{1,0:T(8,128)S(1)} %collective-permute-done.3.block_ref, f32[1024,256]{1,0:T(8,128)S(1)} %collective-permute-done.4.raw_ref), custom_call_target="tpu_custom_call" | custom-call | tf_op jit(solution)/shard_map/pallas_call | solution.py:231
  21.3 2.4 %collective-permute-done.5.w_ref = f32[1104,128]{1,0:T(8,128)S(1)} collective-permute-done((f32[1104,128]{1,0:T(8,128)S(1)}, f32[1104,128]{1,0:T(8,128)S(1)}, u32[]{:S(2)}, u32[]{:S(2)}) %collective-permute-start.5) | collective-permute-done | bytes 565280 | tf_op jit(solution)/shard_map/ppermute | solution.py:54
  23.7 0.1 shard_map.46
  24.0 0.7 collective-permute-start.11
  24.7 0.4 shard_map.47.refs_0_
  25.1 7.4 %collective-permute-start.8 = (f32[128,128]{1,0:T(8,128)S(1)}, f32[128,128]{1,0:T(8,128)S(1)}, u32[]{:S(2)}, u32[]{:S(2)}) collective-permute-start(f32[128,128]{1,0:T(8,128)S(1)} %shard_map.47.refs_0_), channel_id=1, source_target_pairs={{0,6},{4,2},{2,4},{6,0},{1,7},{5,3},{3,5},{7,1},{8,14},{12,10},{10... | collective-permute-start | bytes 196616 | tf_op jit(solution)/shard_map/ppermute | solution.py:54
  32.5 0.5 collective-permute-start.7
  33.1 1.6 %collective-permute-done.8.refs_3_ = f32[128,128]{1,0:T(8,128)S(1)} collective-permute-done((f32[128,128]{1,0:T(8,128)S(1)}, f32[128,128]{1,0:T(8,128)S(1)}, u32[]{:S(2)}, u32[]{:S(2)}) %collective-permute-start.8) | collective-permute-done | bytes 65568 | tf_op jit(solution)/shard_map/ppermute | solution.py:54
  34.7 2.5 %collective-permute-done.7.refs_2_ = f32[128,128]{1,0:T(8,128)S(1)} collective-permute-done((f32[128,128]{1,0:T(8,128)S(1)}, f32[128,128]{1,0:T(8,128)S(1)}, u32[]{:S(2)}, u32[]{:S(2)}) %collective-permute-start.7) | collective-permute-done | bytes 65568 | tf_op jit(solution)/shard_map/ppermute | solution.py:54
  37.3 1.4 %shard_map.48 = (f32[256,256]{1,0:T(8,128)S(1)}, f32[96,128]{1,0:T(8,128)S(1)}, f32[96,128]{1,0:T(8,128)S(1)}) custom-call(s32[4,4]{1,0:T(4,128)S(1)} %copy-done.2, f32[128,128]{1,0:T(8,128)S(1)} %shard_map.47.refs_0_, f32[128,128]{1,0:T(8,128)S(1)} %collective-permute-done.6.refs_1_, f32[128,128]{1,0:T(8,128)S(1)} %collective-permute-done.7.refs_2_, ...), custom_call_target="tpu_custom_call" | custom-call | tf_op jit(solution)/shard_map/pallas_call | solution.py:231
  38.7 0.6 shard_map.49
  39.4 1.5 %collective-permute-start.9 = (f32[1120,128]{1,0:T(8,128)S(1)}, f32[1120,128]{1,0:T(8,128)S(1)}, u32[]{:S(2)}, u32[]{:S(2)}) collective-permute-start(f32[1120,128]{1,0:T(8,128)S(1)} %get-tuple-element.30), channel_id=1, source_target_pairs={{0,1},{4,5},{2,3},{6,7},{1,0},{5,4},{3,2},{7,6},{8,9},{12,13},{10,... | collective-permute-start | bytes 1720328 | tf_op jit(solution)/shard_map/ppermute | solution.py:54
  40.9 1.5 %collective-permute-start.10 = (f32[224,128]{1,0:T(8,128)S(1)}, f32[224,128]{1,0:T(8,128)S(1)}, u32[]{:S(2)}, u32[]{:S(2)}) collective-permute-start(f32[224,128]{1,0:T(8,128)S(1)} %get-tuple-element.31.own_ref), channel_id=1, source_target_pairs={{0,2},{4,6},{2,0},{6,4},{1,8},{5,12},{3,10},{7,14},{8,1},{12,5},{1... | collective-permute-start | bytes 344072 | tf_op jit(solution)/shard_map/ppermute | solution.py:54
  42.5 0.4 shard_map.51.ahead_ref
  42.9 2.8 %collective-permute-done.10.w_ref = f32[224,128]{1,0:T(8,128)S(1)} collective-permute-done((f32[224,128]{1,0:T(8,128)S(1)}, f32[224,128]{1,0:T(8,128)S(1)}, u32[]{:S(2)}, u32[]{:S(2)}) %collective-permute-start.10) | collective-permute-done | bytes 114720 | tf_op jit(solution)/shard_map/ppermute | solution.py:54
  45.7 0.7 shard_map.52
  46.5 2.3 %collective-permute-start.14 = (f32[128,128]{1,0:T(8,128)S(1)}, f32[128,128]{1,0:T(8,128)S(1)}, u32[]{:S(2)}, u32[]{:S(2)}) collective-permute-start(f32[128,128]{1,0:T(8,128)S(1)} %get-tuple-element.32.refs_0_), channel_id=1, source_target_pairs={{0,6},{4,2},{2,4},{6,0},{1,7},{5,3},{3,5},{7,1},{8,14},{12,10},{10... | collective-permute-start | bytes 196616 | tf_op jit(solution)/shard_map/ppermute | solution.py:54
  48.8 0.5 collective-permute-start.13
  49.3 0.7 collective-permute-start.12
  50.0 0.5 shard_map.54.refs_1_
  50.6 1.6 %collective-permute-done.14.refs_3_ = f32[128,128]{1,0:T(8,128)S(1)} collective-permute-done((f32[128,128]{1,0:T(8,128)S(1)}, f32[128,128]{1,0:T(8,128)S(1)}, u32[]{:S(2)}, u32[]{:S(2)}) %collective-permute-start.14) | collective-permute-done | bytes 65568 | tf_op jit(solution)/shard_map/ppermute | solution.py:54
  52.2 1.0 %collective-permute-done.13.refs_2_ = f32[128,128]{1,0:T(8,128)S(1)} collective-permute-done((f32[128,128]{1,0:T(8,128)S(1)}, f32[128,128]{1,0:T(8,128)S(1)}, u32[]{:S(2)}, u32[]{:S(2)}) %collective-permute-start.13) | collective-permute-done | bytes 65568 | tf_op jit(solution)/shard_map/ppermute | solution.py:54
  53.2 0.4 collective-permute-done.12.refs_1_
  53.6 1.4 %shard_map.53 = (f32[256,256]{1,0:T(8,128)S(1)}, f32[128,128]{1,0:T(8,128)S(1)}, f32[128,128]{1,0:T(8,128)S(1)}) custom-call(s32[4,4]{1,0:T(4,128)S(1)} %copy-done.2, f32[128,128]{1,0:T(8,128)S(1)} %get-tuple-element.32.refs_0_, f32[128,128]{1,0:T(8,128)S(1)} %collective-permute-done.12.refs_1_, f32[128,128]{1,0:T(8,128)S(1)} %collective-permute-done.13.refs_2_, ...), custom_call_target="tpu_custom_call" | custom-call | tf_op jit(solution)/shard_map/pallas_call | solution.py:231
  55.0 0.6 shard_map.55
  55.6 1.1 %collective-permute-start.15 = (f32[1152,128]{1,0:T(8,128)S(1)}, f32[1152,128]{1,0:T(8,128)S(1)}, u32[]{:S(2)}, u32[]{:S(2)}) collective-permute-start(f32[1152,128]{1,0:T(8,128)S(1)} %shard_map.55), channel_id=1, source_target_pairs={{0,4},{4,5},{2,6},{6,7},{1,0},{5,1},{3,2},{7,3},{8,12},{12,13},{10... | collective-permute-start | bytes 1769480 | tf_op jit(solution)/shard_map/ppermute | solution.py:54
  56.7 0.6 shard_map.56.own_ref
  57.3 1.5 %collective-permute-start.16 = (f32[1152,128]{1,0:T(8,128)S(1)}, f32[1152,128]{1,0:T(8,128)S(1)}, u32[]{:S(2)}, u32[]{:S(2)}) collective-permute-start(f32[1152,128]{1,0:T(8,128)S(1)} %shard_map.56.own_ref), channel_id=1, source_target_pairs={{0,2},{4,1},{2,0},{6,3},{1,8},{5,9},{3,10},{7,11},{8,4},{12,5},{10... | collective-permute-start | bytes 1769480 | tf_op jit(solution)/shard_map/ppermute | solution.py:54
  58.9 11.6 %collective-permute-done.15.u_ref = f32[1152,128]{1,0:T(8,128)S(1)} collective-permute-done((f32[1152,128]{1,0:T(8,128)S(1)}, f32[1152,128]{1,0:T(8,128)S(1)}, u32[]{:S(2)}, u32[]{:S(2)}) %collective-permute-start.15) | collective-permute-done | bytes 589856 | tf_op jit(solution)/shard_map/ppermute | solution.py:54
  70.5 0.6 shard_map.57
  71.1 1.2 %collective-permute-done.17 = f32[128,128]{1,0:T(8,128)S(1)} collective-permute-done((f32[128,128]{1,0:T(8,128)S(1)}, f32[128,128]{1,0:T(8,128)S(1)}, u32[]{:S(2)}, u32[]{:S(2)}) %collective-permute-start.17) | collective-permute-done | bytes 65568 | tf_op jit(solution)/shard_map/ppermute | solution.py:54
  72.4 1.5 %collective-permute-start.18 = (f32[128,128]{1,0:T(8,128)S(1)}, f32[128,128]{1,0:T(8,128)S(1)}, u32[]{:S(2)}, u32[]{:S(2)}) collective-permute-start(f32[128,128]{1,0:T(8,128)S(1)} %add.7.refs_0_), channel_id=1, source_target_pairs={{0,2},{1,3},{2,0},{3,1},{4,6},{5,7},{6,4},{7,5},{8,10},{9,11},{10,... | collective-permute-start | bytes 196616 | tf_op jit(solution)/shard_map/ppermute | solution.py:54
  74.1 2.3 %shard_map.59.refs_5_ = f32[512,256]{1,0:T(8,128)S(1)} custom-call(s32[4,4]{1,0:T(4,128)S(1)} %copy-done.2, f32[128,128]{1,0:T(8,128)S(1)} %get-tuple-element.39.mu_ref.refs_2_, f32[128,128]{1,0:T(8,128)S(1)} %get-tuple-element.40.mw_ref.refs_3_), custom_call_target="tpu_custom_call" | custom-call | tf_op jit(solution)/shard_map/pallas_call | solution.py:231
  76.4 0.3 collective-permute-done.18.refs_1_
  76.7 2.9 %shard_map.60 = (f32[1024,256]{1,0:T(8,128)}, f32[512,256]{1,0:T(8,128)}) custom-call(s32[4,4]{1,0:T(4,128)S(1)} %copy-done.2, f32[128,128]{1,0:T(8,128)S(1)} %add.7.refs_0_, f32[128,128]{1,0:T(8,128)S(1)} %collective-permute-done.18.refs_1_, f32[128,128]{1,0:T(8,128)S(1)} %get-tuple-element.39.mu_ref.refs_2_, ...), custom_call_target="tpu_custom_call" | custom-call | tf_op jit(solution)/shard_map/pallas_call | solution.py:589
  (18 shorter events, 0.7 us)
Async XLA Ops:
  0.6 19.7 %collective-permute-start.4 = (f32[1024,256]{1,0:T(8,128)}, f32[1024,256]{1,0:T(8,128)S(1)}, u32[]{:S(2)}, u32[]{:S(2)}) collective-permute-start(f32[1024,256]{1,0:T(8,128)} %refs_0_.3), channel_id=1, source_target_pairs={{0,1},{1,5},{2,3},{3,7},{4,0},{5,4},{6,2},{7,6},{8,9},{9,13},{10,1... | collective-permute-start | bytes 3145736 | tf_op jit(solution)/shard_map/ppermute | solution.py:54
  1.1 1.2 %copy-start = (f32[1024,256]{1,0:T(8,128)S(1)}, f32[1024,256]{1,0:T(8,128)}, u32[]{:S(2)}) copy-start(f32[1024,256]{1,0:T(8,128)} %refs_0_.3) | copy-start | bytes 3145732
  2.3 11.1 %copy-start.1 = (f32[1024,256]{1,0:T(8,128)S(1)}, f32[1024,256]{1,0:T(8,128)}, u32[]{:S(2)}) copy-start(f32[1024,256]{1,0:T(8,128)} %refs_0_.3) | copy-start | bytes 3145732
  3.0 9.1 %copy-start.2 = (s32[4,4]{1,0:T(4,128)S(1)}, s32[4,4]{1,0:T(4,128)}, u32[]{:S(2)}) copy-start(s32[4,4]{1,0:T(4,128)} %offs_ref.13) | copy-start | bytes 196
  3.0 3.2 %collective-permute-start = (f32[264,128]{1,0:T(8,128)S(1)}, f32[264,128]{1,0:T(8,128)S(1)}, u32[]{:S(2)}, u32[]{:S(2)}) collective-permute-start(f32[264,128]{1,0:T(8,128)S(1)} %shard_map.41), channel_id=1, source_target_pairs={{0,1},{1,0},{2,3},{3,2},{4,5},{5,4},{6,7},{7,6},{8,9},{9,8},{10,11... | collective-permute-start | bytes 405512 | tf_op jit(solution)/shard_map/ppermute | solution.py:54
  6.2 5.9 %collective-permute-start.1 = (f32[264,128]{1,0:T(8,128)S(1)}, f32[264,128]{1,0:T(8,128)S(1)}, u32[]{:S(2)}, u32[]{:S(2)}) collective-permute-start(f32[264,128]{1,0:T(8,128)S(1)} %add.6.refs_0_), channel_id=1, source_target_pairs={{0,2},{1,3},{2,0},{3,1},{4,6},{5,7},{6,4},{7,5},{8,10},{9,11},{10,... | collective-permute-start | bytes 405512 | tf_op jit(solution)/shard_map/ppermute | solution.py:54
  14.1 9.7 %collective-permute-start.5 = (f32[1104,128]{1,0:T(8,128)S(1)}, f32[1104,128]{1,0:T(8,128)S(1)}, u32[]{:S(2)}, u32[]{:S(2)}) collective-permute-start(f32[1104,128]{1,0:T(8,128)S(1)} %shard_map.45.own_ref), channel_id=1, source_target_pairs={{0,2},{1,4},{2,0},{3,6},{4,8},{5,12},{6,10},{7,14},{8,1},{9,5},{10... | collective-permute-start | bytes 1695752 | tf_op jit(solution)/shard_map/ppermute | solution.py:54
  16.2 4.1 %collective-permute-start.3 = (f32[1024,128]{1,0:T(8,128)S(1)}, f32[1024,128]{1,0:T(8,128)S(1)}, u32[]{:S(2)}, u32[]{:S(2)}) collective-permute-start(f32[1024,128]{1,0:T(8,128)S(1)} %shard_map.43), channel_id=1, source_target_pairs={{0,1},{1,0},{2,3},{3,2},{4,5},{5,4},{6,7},{7,6},{8,9},{9,8},{10,11... | collective-permute-start | bytes 1572872 | tf_op jit(solution)/shard_map/ppermute | solution.py:54
  16.3 4.0 %collective-permute-start.2 = (f32[80,128]{1,0:T(8,128)S(1)}, f32[80,128]{1,0:T(8,128)S(1)}, u32[]{:S(2)}, u32[]{:S(2)}) collective-permute-start(f32[80,128]{1,0:T(8,128)S(1)} %get-tuple-element.22.near_ref), channel_id=1, source_target_pairs={{0,1},{1,5},{2,3},{3,7},{4,0},{5,4},{6,2},{7,6},{8,9},{9,13},{10,1... | collective-permute-start | bytes 122888 | tf_op jit(solution)/shard_map/ppermute | solution.py:54
  24.0 18.6 %collective-permute-start.11 = (f32[896,256]{1,0:T(8,128)S(1)}, f32[896,256]{1,0:T(8,128)S(1)}, u32[]{:S(2)}, u32[]{:S(2)}) collective-permute-start(f32[896,256]{1,0:T(8,128)S(1)} %shard_map.50), channel_id=1, source_target_pairs={{0,0},{4,4},{2,2},{6,6},{1,8},{5,12},{3,10},{7,14},{8,1},{12,5},{1... | collective-permute-start | bytes 2752520 | tf_op jit(solution)/shard_map/ppermute | solution.py:54
  25.1 9.6 %collective-permute-start.8 = (f32[128,128]{1,0:T(8,128)S(1)}, f32[128,128]{1,0:T(8,128)S(1)}, u32[]{:S(2)}, u32[]{:S(2)}) collective-permute-start(f32[128,128]{1,0:T(8,128)S(1)} %shard_map.47.refs_0_), channel_id=1, source_target_pairs={{0,6},{4,2},{2,4},{6,0},{1,7},{5,3},{3,5},{7,1},{8,14},{12,10},{10... | collective-permute-start | bytes 196616 | tf_op jit(solution)/shard_map/ppermute | solution.py:54
  32.5 4.7 %collective-permute-start.7 = (f32[128,128]{1,0:T(8,128)S(1)}, f32[128,128]{1,0:T(8,128)S(1)}, u32[]{:S(2)}, u32[]{:S(2)}) collective-permute-start(f32[128,128]{1,0:T(8,128)S(1)} %shard_map.47.refs_0_), channel_id=1, source_target_pairs={{0,2},{4,6},{2,0},{6,4},{1,3},{5,7},{3,1},{7,5},{8,10},{12,14},{10... | collective-permute-start | bytes 196616 | tf_op jit(solution)/shard_map/ppermute | solution.py:54
  33.0 4.3 %collective-permute-start.6 = (f32[128,128]{1,0:T(8,128)S(1)}, f32[128,128]{1,0:T(8,128)S(1)}, u32[]{:S(2)}, u32[]{:S(2)}) collective-permute-start(f32[128,128]{1,0:T(8,128)S(1)} %shard_map.47.refs_0_), channel_id=1, source_target_pairs={{0,4},{4,0},{2,6},{6,2},{1,5},{5,1},{3,7},{7,3},{8,12},{12,8},{10,... | collective-permute-start | bytes 196616 | tf_op jit(solution)/shard_map/ppermute | solution.py:54
  39.4 3.1 %collective-permute-start.9 = (f32[1120,128]{1,0:T(8,128)S(1)}, f32[1120,128]{1,0:T(8,128)S(1)}, u32[]{:S(2)}, u32[]{:S(2)}) collective-permute-start(f32[1120,128]{1,0:T(8,128)S(1)} %get-tuple-element.30), channel_id=1, source_target_pairs={{0,1},{4,5},{2,3},{6,7},{1,0},{5,4},{3,2},{7,6},{8,9},{12,13},{10,... | collective-permute-start | bytes 1720328 | tf_op jit(solution)/shard_map/ppermute | solution.py:54
  40.9 4.8 %collective-permute-start.10 = (f32[224,128]{1,0:T(8,128)S(1)}, f32[224,128]{1,0:T(8,128)S(1)}, u32[]{:S(2)}, u32[]{:S(2)}) collective-permute-start(f32[224,128]{1,0:T(8,128)S(1)} %get-tuple-element.31.own_ref), channel_id=1, source_target_pairs={{0,2},{4,6},{2,0},{6,4},{1,8},{5,12},{3,10},{7,14},{8,1},{12,5},{1... | collective-permute-start | bytes 344072 | tf_op jit(solution)/shard_map/ppermute | solution.py:54
  46.5 5.7 %collective-permute-start.14 = (f32[128,128]{1,0:T(8,128)S(1)}, f32[128,128]{1,0:T(8,128)S(1)}, u32[]{:S(2)}, u32[]{:S(2)}) collective-permute-start(f32[128,128]{1,0:T(8,128)S(1)} %get-tuple-element.32.refs_0_), channel_id=1, source_target_pairs={{0,6},{4,2},{2,4},{6,0},{1,7},{5,3},{3,5},{7,1},{8,14},{12,10},{10... | collective-permute-start | bytes 196616 | tf_op jit(solution)/shard_map/ppermute | solution.py:54
  48.8 4.4 %collective-permute-start.13 = (f32[128,128]{1,0:T(8,128)S(1)}, f32[128,128]{1,0:T(8,128)S(1)}, u32[]{:S(2)}, u32[]{:S(2)}) collective-permute-start(f32[128,128]{1,0:T(8,128)S(1)} %get-tuple-element.32.refs_0_), channel_id=1, source_target_pairs={{0,2},{4,6},{2,0},{6,4},{1,3},{5,7},{3,1},{7,5},{8,10},{12,14},{10... | collective-permute-start | bytes 196616 | tf_op jit(solution)/shard_map/ppermute | solution.py:54
  49.3 4.3 %collective-permute-start.12 = (f32[128,128]{1,0:T(8,128)S(1)}, f32[128,128]{1,0:T(8,128)S(1)}, u32[]{:S(2)}, u32[]{:S(2)}) collective-permute-start(f32[128,128]{1,0:T(8,128)S(1)} %get-tuple-element.32.refs_0_), channel_id=1, source_target_pairs={{0,4},{4,0},{2,6},{6,2},{1,5},{5,1},{3,7},{7,3},{8,12},{12,8},{10,... | collective-permute-start | bytes 196616 | tf_op jit(solution)/shard_map/ppermute | solution.py:54
  55.6 14.8 %collective-permute-start.15 = (f32[1152,128]{1,0:T(8,128)S(1)}, f32[1152,128]{1,0:T(8,128)S(1)}, u32[]{:S(2)}, u32[]{:S(2)}) collective-permute-start(f32[1152,128]{1,0:T(8,128)S(1)} %shard_map.55), channel_id=1, source_target_pairs={{0,4},{4,5},{2,6},{6,7},{1,0},{5,1},{3,2},{7,3},{8,12},{12,13},{10... | collective-permute-start | bytes 1769480 | tf_op jit(solution)/shard_map/ppermute | solution.py:54
  57.3 13.1 %collective-permute-start.16 = (f32[1152,128]{1,0:T(8,128)S(1)}, f32[1152,128]{1,0:T(8,128)S(1)}, u32[]{:S(2)}, u32[]{:S(2)}) collective-permute-start(f32[1152,128]{1,0:T(8,128)S(1)} %shard_map.56.own_ref), channel_id=1, source_target_pairs={{0,2},{4,1},{2,0},{6,3},{1,8},{5,9},{3,10},{7,11},{8,4},{12,5},{10... | collective-permute-start | bytes 1769480 | tf_op jit(solution)/shard_map/ppermute | solution.py:54
  71.1 1.3 %collective-permute-start.17 = (f32[128,128]{1,0:T(8,128)S(1)}, f32[128,128]{1,0:T(8,128)S(1)}, u32[]{:S(2)}, u32[]{:S(2)}) collective-permute-start(f32[128,128]{1,0:T(8,128)S(1)} %shard_map.57), channel_id=1, source_target_pairs={{0,1},{1,0},{2,3},{3,2},{4,5},{5,4},{6,7},{7,6},{8,9},{9,8},{10,11... | collective-permute-start | bytes 196616 | tf_op jit(solution)/shard_map/ppermute | solution.py:54
  72.4 4.3 %collective-permute-start.18 = (f32[128,128]{1,0:T(8,128)S(1)}, f32[128,128]{1,0:T(8,128)S(1)}, u32[]{:S(2)}, u32[]{:S(2)}) collective-permute-start(f32[128,128]{1,0:T(8,128)S(1)} %add.7.refs_0_), channel_id=1, source_target_pairs={{0,2},{1,3},{2,0},{3,1},{4,6},{5,7},{6,4},{7,5},{8,10},{9,11},{10,... | collective-permute-start | bytes 196616 | tf_op jit(solution)/shard_map/ppermute | solution.py:54

commit v9 on v8

--- a/solution.py
+++ b/solution.py
@@ -11,7 +11,7 @@
 ROUNDS = 4
 STEPS = 4
 RECORD = 2 * ROUNDS
-PIECES = 4
+PIECES = 8
 HALF = B // 2
 PACKED = HALF + 8
 AXES = ("pair", "row")

time: 79.9 us -> 79.9 us (level)
  no operation moved by 1% of the time
where the time goes in v9:
time: 79.9 us; the launch traced here: 79.8 us
  waiting for transfers between devices  34.6 us (43%)
  starting transfers between devices  25.9 us (32%)
  Pallas kernels  17.1 us (21%)
  local copies, waits for them, and re-layouts  1.23 us (2%)
  between operations  0.98 us (1%)
    ppermute x19, waiting for transfers between devices, send(): return lax.ppermute(x, AXES, route(source, target, change, swap))  34.6 us
    ppermute x19, starting transfers between devices, send(): return lax.ppermute(x, AXES, route(source, target, change, swap))  25.9 us
    pallas_call x19, Pallas kernels, call(): pl.pallas_call(kernel, out_shape=tuple((jax.ShapeDtypeStruct(shape, jnp.f...  14.2 us
    pallas_call x1, Pallas kernels, last_step(): pl.pallas_call(functools.partial(last_kernel, len(parts)), out_shape=tupl...  2.9 us
  transfers between devices with their start and end apart: 19, of which 15 were waited for; matrix products, arithmetic and copies ran while one was open for 0% of the time, Pallas kernels for 13%

profile of v9, /device:TPU:0, one launch (start us, length us, event | category | flops | bytes accessed | tf_op | source)
XLA Modules:
  0.0 79.8 jit_solution(1905700276723090040)
XLA Ops:
  0.6 0.5 collective-permute-start.4
  1.1 1.2 %copy-done = f32[1024,256]{1,0:T(8,128)S(1)} copy-done((f32[1024,256]{1,0:T(8,128)S(1)}, f32[1024,256]{1,0:T(8,128)}, u32[]{:S(2)}) %copy-start) | copy-done | bytes 1048600
  2.3 0.7 shard_map.41
  3.0 2.2 %collective-permute-start = (f32[264,128]{1,0:T(8,128)S(1)}, f32[264,128]{1,0:T(8,128)S(1)}, u32[]{:S(2)}, u32[]{:S(2)}) collective-permute-start(f32[264,128]{1,0:T(8,128)S(1)} %shard_map.41), channel_id=1, source_target_pairs={{0,1},{1,0},{2,3},{3,2},{4,5},{5,4},{6,7},{7,6},{8,9},{9,8},{10,11... | collective-permute-start | bytes 405512 | tf_op jit(solution)/shard_map/ppermute | solution.py:54
  5.2 1.0 %collective-permute-done = f32[264,128]{1,0:T(8,128)S(1)} collective-permute-done((f32[264,128]{1,0:T(8,128)S(1)}, f32[264,128]{1,0:T(8,128)S(1)}, u32[]{:S(2)}, u32[]{:S(2)}) %collective-permute-start) | collective-permute-done | bytes 135200 | tf_op jit(solution)/shard_map/ppermute | solution.py:54
  6.2 1.6 %collective-permute-start.1 = (f32[264,128]{1,0:T(8,128)S(1)}, f32[264,128]{1,0:T(8,128)S(1)}, u32[]{:S(2)}, u32[]{:S(2)}) collective-permute-start(f32[264,128]{1,0:T(8,128)S(1)} %add.6.refs_0_), channel_id=1, source_target_pairs={{0,2},{1,3},{2,0},{3,1},{4,6},{5,7},{6,4},{7,5},{8,10},{9,11},{10,... | collective-permute-start | bytes 405512 | tf_op jit(solution)/shard_map/ppermute | solution.py:54
  7.8 4.3 %collective-permute-done.1.refs_1_ = f32[264,128]{1,0:T(8,128)S(1)} collective-permute-done((f32[264,128]{1,0:T(8,128)S(1)}, f32[264,128]{1,0:T(8,128)S(1)}, u32[]{:S(2)}, u32[]{:S(2)}) %collective-permute-start.1) | collective-permute-done | bytes 135200 | tf_op jit(solution)/shard_map/ppermute | solution.py:54
  12.1 1.3 %shard_map.42 = (f32[256,256]{1,0:T(8,128)S(1)}, f32[80,128]{1,0:T(8,128)S(1)}, f32[80,128]{1,0:T(8,128)S(1)}) custom-call(s32[4,4]{1,0:T(4,128)S(1)} %copy-done.2, f32[264,128]{1,0:T(8,128)S(1)} %add.6.refs_0_, f32[264,128]{1,0:T(8,128)S(1)} %collective-permute-done.1.refs_1_), custom_call_target="tpu_custom_call" | custom-call | tf_op jit(solution)/shard_map/pallas_call | solution.py:231
  13.5 0.6 shard_map.45.own_ref
  14.1 1.6 %collective-permute-start.5 = (f32[1104,128]{1,0:T(8,128)S(1)}, f32[1104,128]{1,0:T(8,128)S(1)}, u32[]{:S(2)}, u32[]{:S(2)}) collective-permute-start(f32[1104,128]{1,0:T(8,128)S(1)} %shard_map.45.own_ref), channel_id=1, source_target_pairs={{0,2},{1,4},{2,0},{3,6},{4,8},{5,12},{6,10},{7,14},{8,1},{9,5},{10... | collective-permute-start | bytes 1695752 | tf_op jit(solution)/shard_map/ppermute | solution.py:54
  15.6 0.6 shard_map.43
  16.3 0.5 collective-permute-start.2
  16.8 3.5 %collective-permute-done.2.u_ref.refs_4_ = f32[80,128]{1,0:T(8,128)S(1)} collective-permute-done((f32[80,128]{1,0:T(8,128)S(1)}, f32[80,128]{1,0:T(8,128)S(1)}, u32[]{:S(2)}, u32[]{:S(2)}) %collective-permute-start.2) | collective-permute-done | bytes 40992 | tf_op jit(solution)/shard_map/ppermute | solution.py:54
  20.3 1.0 %shard_map.44.block_ref = f32[1024,128]{1,0:T(8,128)S(1)} custom-call(s32[4,4]{1,0:T(4,128)S(1)} %copy-done.2, f32[80,128]{1,0:T(8,128)S(1)} %collective-permute-done.2.u_ref.refs_4_, f32[1024,128]{1,0:T(8,128)S(1)} %collective-permute-done.3.block_ref, f32[1024,256]{1,0:T(8,128)S(1)} %collective-permute-done.4.raw_ref), custom_call_target="tpu_custom_call" | custom-call | tf_op jit(solution)/shard_map/pallas_call | solution.py:231
  21.3 2.4 %collective-permute-done.5.w_ref = f32[1104,128]{1,0:T(8,128)S(1)} collective-permute-done((f32[1104,128]{1,0:T(8,128)S(1)}, f32[1104,128]{1,0:T(8,128)S(1)}, u32[]{:S(2)}, u32[]{:S(2)}) %collective-permute-start.5) | collective-permute-done | bytes 565280 | tf_op jit(solution)/shard_map/ppermute | solution.py:54
  23.7 0.1 shard_map.46
  24.0 0.7 collective-permute-start.11
  24.7 0.4 shard_map.47.refs_0_
  25.1 7.4 %collective-permute-start.8 = (f32[128,128]{1,0:T(8,128)S(1)}, f32[128,128]{1,0:T(8,128)S(1)}, u32[]{:S(2)}, u32[]{:S(2)}) collective-permute-start(f32[128,128]{1,0:T(8,128)S(1)} %shard_map.47.refs_0_), channel_id=1, source_target_pairs={{0,6},{4,2},{2,4},{6,0},{1,7},{5,3},{3,5},{7,1},{8,14},{12,10},{10... | collective-permute-start | bytes 196616 | tf_op jit(solution)/shard_map/ppermute | solution.py:54
  32.5 0.5 collective-permute-start.7
  33.1 1.6 %collective-permute-done.8.refs_3_ = f32[128,128]{1,0:T(8,128)S(1)} collective-permute-done((f32[128,128]{1,0:T(8,128)S(1)}, f32[128,128]{1,0:T(8,128)S(1)}, u32[]{:S(2)}, u32[]{:S(2)}) %collective-permute-start.8) | collective-permute-done | bytes 65568 | tf_op jit(solution)/shard_map/ppermute | solution.py:54
  34.7 2.5 %collective-permute-done.7.refs_2_ = f32[128,128]{1,0:T(8,128)S(1)} collective-permute-done((f32[128,128]{1,0:T(8,128)S(1)}, f32[128,128]{1,0:T(8,128)S(1)}, u32[]{:S(2)}, u32[]{:S(2)}) %collective-permute-start.7) | collective-permute-done | bytes 65568 | tf_op jit(solution)/shard_map/ppermute | solution.py:54
  37.3 1.4 %shard_map.48 = (f32[256,256]{1,0:T(8,128)S(1)}, f32[96,128]{1,0:T(8,128)S(1)}, f32[96,128]{1,0:T(8,128)S(1)}) custom-call(s32[4,4]{1,0:T(4,128)S(1)} %copy-done.2, f32[128,128]{1,0:T(8,128)S(1)} %shard_map.47.refs_0_, f32[128,128]{1,0:T(8,128)S(1)} %collective-permute-done.6.refs_1_, f32[128,128]{1,0:T(8,128)S(1)} %collective-permute-done.7.refs_2_, ...), custom_call_target="tpu_custom_call" | custom-call | tf_op jit(solution)/shard_map/pallas_call | solution.py:231
  38.7 0.6 shard_map.49
  39.4 1.5 %collective-permute-start.9 = (f32[1120,128]{1,0:T(8,128)S(1)}, f32[1120,128]{1,0:T(8,128)S(1)}, u32[]{:S(2)}, u32[]{:S(2)}) collective-permute-start(f32[1120,128]{1,0:T(8,128)S(1)} %get-tuple-element.30), channel_id=1, source_target_pairs={{0,1},{4,5},{2,3},{6,7},{1,0},{5,4},{3,2},{7,6},{8,9},{12,13},{10,... | collective-permute-start | bytes 1720328 | tf_op jit(solution)/shard_map/ppermute | solution.py:54
  40.9 1.5 %collective-permute-start.10 = (f32[224,128]{1,0:T(8,128)S(1)}, f32[224,128]{1,0:T(8,128)S(1)}, u32[]{:S(2)}, u32[]{:S(2)}) collective-permute-start(f32[224,128]{1,0:T(8,128)S(1)} %get-tuple-element.31.own_ref), channel_id=1, source_target_pairs={{0,2},{4,6},{2,0},{6,4},{1,8},{5,12},{3,10},{7,14},{8,1},{12,5},{1... | collective-permute-start | bytes 344072 | tf_op jit(solution)/shard_map/ppermute | solution.py:54
  42.5 0.4 shard_map.51.ahead_ref
  42.9 2.8 %collective-permute-done.10.w_ref = f32[224,128]{1,0:T(8,128)S(1)} collective-permute-done((f32[224,128]{1,0:T(8,128)S(1)}, f32[224,128]{1,0:T(8,128)S(1)}, u32[]{:S(2)}, u32[]{:S(2)}) %collective-permute-start.10) | collective-permute-done | bytes 114720 | tf_op jit(solution)/shard_map/ppermute | solution.py:54
  45.7 0.7 shard_map.52
  46.5 2.3 %collective-permute-start.14 = (f32[128,128]{1,0:T(8,128)S(1)}, f32[128,128]{1,0:T(8,128)S(1)}, u32[]{:S(2)}, u32[]{:S(2)}) collective-permute-start(f32[128,128]{1,0:T(8,128)S(1)} %get-tuple-element.32.refs_0_), channel_id=1, source_target_pairs={{0,6},{4,2},{2,4},{6,0},{1,7},{5,3},{3,5},{7,1},{8,14},{12,10},{10... | collective-permute-start | bytes 196616 | tf_op jit(solution)/shard_map/ppermute | solution.py:54
  48.8 0.5 collective-permute-start.13
  49.3 0.7 collective-permute-start.12
  50.0 0.5 shard_map.54.refs_1_
  50.6 1.6 %collective-permute-done.14.refs_3_ = f32[128,128]{1,0:T(8,128)S(1)} collective-permute-done((f32[128,128]{1,0:T(8,128)S(1)}, f32[128,128]{1,0:T(8,128)S(1)}, u32[]{:S(2)}, u32[]{:S(2)}) %collective-permute-start.14) | collective-permute-done | bytes 65568 | tf_op jit(solution)/shard_map/ppermute | solution.py:54
  52.2 1.0 %collective-permute-done.13.refs_2_ = f32[128,128]{1,0:T(8,128)S(1)} collective-permute-done((f32[128,128]{1,0:T(8,128)S(1)}, f32[128,128]{1,0:T(8,128)S(1)}, u32[]{:S(2)}, u32[]{:S(2)}) %collective-permute-start.13) | collective-permute-done | bytes 65568 | tf_op jit(solution)/shard_map/ppermute | solution.py:54
  53.2 0.4 collective-permute-done.12.refs_1_
  53.6 1.4 %shard_map.53 = (f32[256,256]{1,0:T(8,128)S(1)}, f32[128,128]{1,0:T(8,128)S(1)}, f32[128,128]{1,0:T(8,128)S(1)}) custom-call(s32[4,4]{1,0:T(4,128)S(1)} %copy-done.2, f32[128,128]{1,0:T(8,128)S(1)} %get-tuple-element.32.refs_0_, f32[128,128]{1,0:T(8,128)S(1)} %collective-permute-done.12.refs_1_, f32[128,128]{1,0:T(8,128)S(1)} %collective-permute-done.13.refs_2_, ...), custom_call_target="tpu_custom_call" | custom-call | tf_op jit(solution)/shard_map/pallas_call | solution.py:231
  55.0 0.6 shard_map.55
  55.6 1.1 %collective-permute-start.15 = (f32[1152,128]{1,0:T(8,128)S(1)}, f32[1152,128]{1,0:T(8,128)S(1)}, u32[]{:S(2)}, u32[]{:S(2)}) collective-permute-start(f32[1152,128]{1,0:T(8,128)S(1)} %shard_map.55), channel_id=1, source_target_pairs={{0,4},{4,5},{2,6},{6,7},{1,0},{5,1},{3,2},{7,3},{8,12},{12,13},{10... | collective-permute-start | bytes 1769480 | tf_op jit(solution)/shard_map/ppermute | solution.py:54
  56.7 0.6 shard_map.56.own_ref
  57.3 1.5 %collective-permute-start.16 = (f32[1152,128]{1,0:T(8,128)S(1)}, f32[1152,128]{1,0:T(8,128)S(1)}, u32[]{:S(2)}, u32[]{:S(2)}) collective-permute-start(f32[1152,128]{1,0:T(8,128)S(1)} %shard_map.56.own_ref), channel_id=1, source_target_pairs={{0,2},{4,1},{2,0},{6,3},{1,8},{5,9},{3,10},{7,11},{8,4},{12,5},{10... | collective-permute-start | bytes 1769480 | tf_op jit(solution)/shard_map/ppermute | solution.py:54
  58.9 11.6 %collective-permute-done.15.u_ref = f32[1152,128]{1,0:T(8,128)S(1)} collective-permute-done((f32[1152,128]{1,0:T(8,128)S(1)}, f32[1152,128]{1,0:T(8,128)S(1)}, u32[]{:S(2)}, u32[]{:S(2)}) %collective-permute-start.15) | collective-permute-done | bytes 589856 | tf_op jit(solution)/shard_map/ppermute | solution.py:54
  70.5 0.6 shard_map.57
  71.1 1.2 %collective-permute-done.17 = f32[128,128]{1,0:T(8,128)S(1)} collective-permute-done((f32[128,128]{1,0:T(8,128)S(1)}, f32[128,128]{1,0:T(8,128)S(1)}, u32[]{:S(2)}, u32[]{:S(2)}) %collective-permute-start.17) | collective-permute-done | bytes 65568 | tf_op jit(solution)/shard_map/ppermute | solution.py:54
  72.4 1.5 %collective-permute-start.18 = (f32[128,128]{1,0:T(8,128)S(1)}, f32[128,128]{1,0:T(8,128)S(1)}, u32[]{:S(2)}, u32[]{:S(2)}) collective-permute-start(f32[128,128]{1,0:T(8,128)S(1)} %add.7.refs_0_), channel_id=1, source_target_pairs={{0,2},{1,3},{2,0},{3,1},{4,6},{5,7},{6,4},{7,5},{8,10},{9,11},{10,... | collective-permute-start | bytes 196616 | tf_op jit(solution)/shard_map/ppermute | solution.py:54
  74.1 2.3 %shard_map.59.refs_5_ = f32[512,256]{1,0:T(8,128)S(1)} custom-call(s32[4,4]{1,0:T(4,128)S(1)} %copy-done.2, f32[128,128]{1,0:T(8,128)S(1)} %get-tuple-element.39.mu_ref.refs_2_, f32[128,128]{1,0:T(8,128)S(1)} %get-tuple-element.40.mw_ref.refs_3_), custom_call_target="tpu_custom_call" | custom-call | tf_op jit(solution)/shard_map/pallas_call | solution.py:231
  76.4 0.3 collective-permute-done.18.refs_1_
  76.7 2.9 %shard_map.60 = (f32[1024,256]{1,0:T(8,128)}, f32[512,256]{1,0:T(8,128)}) custom-call(s32[4,4]{1,0:T(4,128)S(1)} %copy-done.2, f32[128,128]{1,0:T(8,128)S(1)} %add.7.refs_0_, f32[128,128]{1,0:T(8,128)S(1)} %collective-permute-done.18.refs_1_, f32[128,128]{1,0:T(8,128)S(1)} %get-tuple-element.39.mu_ref.refs_2_, ...), custom_call_target="tpu_custom_call" | custom-call | tf_op jit(solution)/shard_map/pallas_call | solution.py:589
  (18 shorter events, 0.7 us)
Async XLA Ops:
  0.6 19.7 %collective-permute-start.4 = (f32[1024,256]{1,0:T(8,128)}, f32[1024,256]{1,0:T(8,128)S(1)}, u32[]{:S(2)}, u32[]{:S(2)}) collective-permute-start(f32[1024,256]{1,0:T(8,128)} %refs_0_.3), channel_id=1, source_target_pairs={{0,1},{1,5},{2,3},{3,7},{4,0},{5,4},{6,2},{7,6},{8,9},{9,13},{10,1... | collective-permute-start | bytes 3145736 | tf_op jit(solution)/shard_map/ppermute | solution.py:54
  1.1 1.2 %copy-start = (f32[1024,256]{1,0:T(8,128)S(1)}, f32[1024,256]{1,0:T(8,128)}, u32[]{:S(2)}) copy-start(f32[1024,256]{1,0:T(8,128)} %refs_0_.3) | copy-start | bytes 3145732
  2.3 11.1 %copy-start.1 = (f32[1024,256]{1,0:T(8,128)S(1)}, f32[1024,256]{1,0:T(8,128)}, u32[]{:S(2)}) copy-start(f32[1024,256]{1,0:T(8,128)} %refs_0_.3) | copy-start | bytes 3145732
  3.0 9.1 %copy-start.2 = (s32[4,4]{1,0:T(4,128)S(1)}, s32[4,4]{1,0:T(4,128)}, u32[]{:S(2)}) copy-start(s32[4,4]{1,0:T(4,128)} %offs_ref.13) | copy-start | bytes 196
  3.0 3.2 %collective-permute-start = (f32[264,128]{1,0:T(8,128)S(1)}, f32[264,128]{1,0:T(8,128)S(1)}, u32[]{:S(2)}, u32[]{:S(2)}) collective-permute-start(f32[264,128]{1,0:T(8,128)S(1)} %shard_map.41), channel_id=1, source_target_pairs={{0,1},{1,0},{2,3},{3,2},{4,5},{5,4},{6,7},{7,6},{8,9},{9,8},{10,11... | collective-permute-start | bytes 405512 | tf_op jit(solution)/shard_map/ppermute | solution.py:54
  6.2 5.9 %collective-permute-start.1 = (f32[264,128]{1,0:T(8,128)S(1)}, f32[264,128]{1,0:T(8,128)S(1)}, u32[]{:S(2)}, u32[]{:S(2)}) collective-permute-start(f32[264,128]{1,0:T(8,128)S(1)} %add.6.refs_0_), channel_id=1, source_target_pairs={{0,2},{1,3},{2,0},{3,1},{4,6},{5,7},{6,4},{7,5},{8,10},{9,11},{10,... | collective-permute-start | bytes 405512 | tf_op jit(solution)/shard_map/ppermute | solution.py:54
  14.1 9.7 %collective-permute-start.5 = (f32[1104,128]{1,0:T(8,128)S(1)}, f32[1104,128]{1,0:T(8,128)S(1)}, u32[]{:S(2)}, u32[]{:S(2)}) collective-permute-start(f32[1104,128]{1,0:T(8,128)S(1)} %shard_map.45.own_ref), channel_id=1, source_target_pairs={{0,2},{1,4},{2,0},{3,6},{4,8},{5,12},{6,10},{7,14},{8,1},{9,5},{10... | collective-permute-start | bytes 1695752 | tf_op jit(solution)/shard_map/ppermute | solution.py:54
  16.2 4.1 %collective-permute-start.3 = (f32[1024,128]{1,0:T(8,128)S(1)}, f32[1024,128]{1,0:T(8,128)S(1)}, u32[]{:S(2)}, u32[]{:S(2)}) collective-permute-start(f32[1024,128]{1,0:T(8,128)S(1)} %shard_map.43), channel_id=1, source_target_pairs={{0,1},{1,0},{2,3},{3,2},{4,5},{5,4},{6,7},{7,6},{8,9},{9,8},{10,11... | collective-permute-start | bytes 1572872 | tf_op jit(solution)/shard_map/ppermute | solution.py:54
  16.3 4.0 %collective-permute-start.2 = (f32[80,128]{1,0:T(8,128)S(1)}, f32[80,128]{1,0:T(8,128)S(1)}, u32[]{:S(2)}, u32[]{:S(2)}) collective-permute-start(f32[80,128]{1,0:T(8,128)S(1)} %get-tuple-element.22.near_ref), channel_id=1, source_target_pairs={{0,1},{1,5},{2,3},{3,7},{4,0},{5,4},{6,2},{7,6},{8,9},{9,13},{10,1... | collective-permute-start | bytes 122888 | tf_op jit(solution)/shard_map/ppermute | solution.py:54
  24.0 18.6 %collective-permute-start.11 = (f32[896,256]{1,0:T(8,128)S(1)}, f32[896,256]{1,0:T(8,128)S(1)}, u32[]{:S(2)}, u32[]{:S(2)}) collective-permute-start(f32[896,256]{1,0:T(8,128)S(1)} %shard_map.50), channel_id=1, source_target_pairs={{0,0},{4,4},{2,2},{6,6},{1,8},{5,12},{3,10},{7,14},{8,1},{12,5},{1... | collective-permute-start | bytes 2752520 | tf_op jit(solution)/shard_map/ppermute | solution.py:54
  25.1 9.6 %collective-permute-start.8 = (f32[128,128]{1,0:T(8,128)S(1)}, f32[128,128]{1,0:T(8,128)S(1)}, u32[]{:S(2)}, u32[]{:S(2)}) collective-permute-start(f32[128,128]{1,0:T(8,128)S(1)} %shard_map.47.refs_0_), channel_id=1, source_target_pairs={{0,6},{4,2},{2,4},{6,0},{1,7},{5,3},{3,5},{7,1},{8,14},{12,10},{10... | collective-permute-start | bytes 196616 | tf_op jit(solution)/shard_map/ppermute | solution.py:54
  32.5 4.7 %collective-permute-start.7 = (f32[128,128]{1,0:T(8,128)S(1)}, f32[128,128]{1,0:T(8,128)S(1)}, u32[]{:S(2)}, u32[]{:S(2)}) collective-permute-start(f32[128,128]{1,0:T(8,128)S(1)} %shard_map.47.refs_0_), channel_id=1, source_target_pairs={{0,2},{4,6},{2,0},{6,4},{1,3},{5,7},{3,1},{7,5},{8,10},{12,14},{10... | collective-permute-start | bytes 196616 | tf_op jit(solution)/shard_map/ppermute | solution.py:54
  33.0 4.3 %collective-permute-start.6 = (f32[128,128]{1,0:T(8,128)S(1)}, f32[128,128]{1,0:T(8,128)S(1)}, u32[]{:S(2)}, u32[]{:S(2)}) collective-permute-start(f32[128,128]{1,0:T(8,128)S(1)} %shard_map.47.refs_0_), channel_id=1, source_target_pairs={{0,4},{4,0},{2,6},{6,2},{1,5},{5,1},{3,7},{7,3},{8,12},{12,8},{10,... | collective-permute-start | bytes 196616 | tf_op jit(solution)/shard_map/ppermute | solution.py:54
  39.4 3.1 %collective-permute-start.9 = (f32[1120,128]{1,0:T(8,128)S(1)}, f32[1120,128]{1,0:T(8,128)S(1)}, u32[]{:S(2)}, u32[]{:S(2)}) collective-permute-start(f32[1120,128]{1,0:T(8,128)S(1)} %get-tuple-element.30), channel_id=1, source_target_pairs={{0,1},{4,5},{2,3},{6,7},{1,0},{5,4},{3,2},{7,6},{8,9},{12,13},{10,... | collective-permute-start | bytes 1720328 | tf_op jit(solution)/shard_map/ppermute | solution.py:54
  40.9 4.8 %collective-permute-start.10 = (f32[224,128]{1,0:T(8,128)S(1)}, f32[224,128]{1,0:T(8,128)S(1)}, u32[]{:S(2)}, u32[]{:S(2)}) collective-permute-start(f32[224,128]{1,0:T(8,128)S(1)} %get-tuple-element.31.own_ref), channel_id=1, source_target_pairs={{0,2},{4,6},{2,0},{6,4},{1,8},{5,12},{3,10},{7,14},{8,1},{12,5},{1... | collective-permute-start | bytes 344072 | tf_op jit(solution)/shard_map/ppermute | solution.py:54
  46.5 5.7 %collective-permute-start.14 = (f32[128,128]{1,0:T(8,128)S(1)}, f32[128,128]{1,0:T(8,128)S(1)}, u32[]{:S(2)}, u32[]{:S(2)}) collective-permute-start(f32[128,128]{1,0:T(8,128)S(1)} %get-tuple-element.32.refs_0_), channel_id=1, source_target_pairs={{0,6},{4,2},{2,4},{6,0},{1,7},{5,3},{3,5},{7,1},{8,14},{12,10},{10... | collective-permute-start | bytes 196616 | tf_op jit(solution)/shard_map/ppermute | solution.py:54
  48.8 4.4 %collective-permute-start.13 = (f32[128,128]{1,0:T(8,128)S(1)}, f32[128,128]{1,0:T(8,128)S(1)}, u32[]{:S(2)}, u32[]{:S(2)}) collective-permute-start(f32[128,128]{1,0:T(8,128)S(1)} %get-tuple-element.32.refs_0_), channel_id=1, source_target_pairs={{0,2},{4,6},{2,0},{6,4},{1,3},{5,7},{3,1},{7,5},{8,10},{12,14},{10... | collective-permute-start | bytes 196616 | tf_op jit(solution)/shard_map/ppermute | solution.py:54
  49.3 4.3 %collective-permute-start.12 = (f32[128,128]{1,0:T(8,128)S(1)}, f32[128,128]{1,0:T(8,128)S(1)}, u32[]{:S(2)}, u32[]{:S(2)}) collective-permute-start(f32[128,128]{1,0:T(8,128)S(1)} %get-tuple-element.32.refs_0_), channel_id=1, source_target_pairs={{0,4},{4,0},{2,6},{6,2},{1,5},{5,1},{3,7},{7,3},{8,12},{12,8},{10,... | collective-permute-start | bytes 196616 | tf_op jit(solution)/shard_map/ppermute | solution.py:54
  55.6 14.8 %collective-permute-start.15 = (f32[1152,128]{1,0:T(8,128)S(1)}, f32[1152,128]{1,0:T(8,128)S(1)}, u32[]{:S(2)}, u32[]{:S(2)}) collective-permute-start(f32[1152,128]{1,0:T(8,128)S(1)} %shard_map.55), channel_id=1, source_target_pairs={{0,4},{4,5},{2,6},{6,7},{1,0},{5,1},{3,2},{7,3},{8,12},{12,13},{10... | collective-permute-start | bytes 1769480 | tf_op jit(solution)/shard_map/ppermute | solution.py:54
  57.3 13.1 %collective-permute-start.16 = (f32[1152,128]{1,0:T(8,128)S(1)}, f32[1152,128]{1,0:T(8,128)S(1)}, u32[]{:S(2)}, u32[]{:S(2)}) collective-permute-start(f32[1152,128]{1,0:T(8,128)S(1)} %shard_map.56.own_ref), channel_id=1, source_target_pairs={{0,2},{4,1},{2,0},{6,3},{1,8},{5,9},{3,10},{7,11},{8,4},{12,5},{10... | collective-permute-start | bytes 1769480 | tf_op jit(solution)/shard_map/ppermute | solution.py:54
  71.1 1.3 %collective-permute-start.17 = (f32[128,128]{1,0:T(8,128)S(1)}, f32[128,128]{1,0:T(8,128)S(1)}, u32[]{:S(2)}, u32[]{:S(2)}) collective-permute-start(f32[128,128]{1,0:T(8,128)S(1)} %shard_map.57), channel_id=1, source_target_pairs={{0,1},{1,0},{2,3},{3,2},{4,5},{5,4},{6,7},{7,6},{8,9},{9,8},{10,11... | collective-permute-start | bytes 196616 | tf_op jit(solution)/shard_map/ppermute | solution.py:54
  72.4 4.3 %collective-permute-start.18 = (f32[128,128]{1,0:T(8,128)S(1)}, f32[128,128]{1,0:T(8,128)S(1)}, u32[]{:S(2)}, u32[]{:S(2)}) collective-permute-start(f32[128,128]{1,0:T(8,128)S(1)} %add.7.refs_0_), channel_id=1, source_target_pairs={{0,2},{1,3},{2,0},{3,1},{4,6},{5,7},{6,4},{7,5},{8,10},{9,11},{10,... | collective-permute-start | bytes 196616 | tf_op jit(solution)/shard_map/ppermute | solution.py:54
